TPU v7x, 256 devices: a whole 4x4x8 slice. The times are simulated.
256 devices in a mesh: pipe: 8 (over y_lo, x), expert: 32 (over y_hi, z, core).
Axes of the slice: x: 4, y: 4 (y_hi: 2, y_lo: 2; y = y_hi * 2 + y_lo), z: 8, core: 2. Of those that a mesh axis runs over, the one named last changes fastest.
Arguments:
- x_fwd: bfloat16 [8, 2048, 3584], P('pipe', 'expert'), may hold values from -6 to 6
- routes_fwd: int32 [8, 2048, 1], P('pipe', 'expert'), may hold values from 0 to 7; in each aligned block of 64 rows (0 to 63, 64 to 127, ..., all dimensions but the last counted through in order) at most 12 rows name the same one
- gates_fwd: float32 [8, 2048, 1], P('pipe', 'expert'), may hold values from 0.25 to 1.5
- x_bwd: bfloat16 [8, 2048, 3584], P('pipe', 'expert'), may hold values from -6 to 6
- grad_bwd: bfloat16 [8, 2048, 3584], P('pipe', 'expert'), may hold values from -6 to 6
- routes_bwd: int32 [8, 2048, 1], P('pipe', 'expert'), may hold values from 0 to 7; in each aligned block of 64 rows (0 to 63, 64 to 127, ..., all dimensions but the last counted through in order) at most 12 rows name the same one
- gates_bwd: float32 [8, 2048, 1], P('pipe', 'expert'), may hold values from 0.25 to 1.5
- gate_proj: bfloat16 [8, 3584, 8192], P('pipe', None, 'expert'), may hold values from -0.09375 to 0.09375
- up_proj: bfloat16 [8, 3584, 8192], P('pipe', None, 'expert'), may hold values from -0.09375 to 0.09375
- down_proj: bfloat16 [8, 8192, 3584], P('pipe', 'expert'), may hold values from -0.1875 to 0.1875
Outputs:
- fwd_next: bfloat16 [8, 2048, 3584], P('pipe', 'expert')
- bwd_next: bfloat16 [8, 2048, 3584], P('pipe', 'expert')
Inputs may be any that keep to these rules, and one draw needn't show every extreme that they name: `routes_fwd`: each token names 1 different experts. Among the 64 tokens of one device no expert is named more than 12 times, and in every draw some expert is named exactly 12 times by the tokens of one device. `routes_bwd`: as for routes_fwd.
All inputs are finite; a program needn't handle non-finite values.
Results may differ from a plain program's by a relative error of at most 0.007.
Values may be sent and summed in bfloat16 or wider, within the bound.
No kernel may reach another device: no remote copies, remote signals or barrier semaphores. Data moves between devices by JAX's collectives and lax.ppermute only.
A program may use at most 128 MiB of HBM per device.

v0:
```python
import jax
import jax.numpy as jnp
from jax import lax
from jax.sharding import PartitionSpec as P

HSPLIT = 4
TOPK = 1


def shifted(block, axis, distance):
    devices = range(lax.axis_size(axis))
    route = [(i - distance, i) for i in devices if i - distance in devices]
    return lax.ppermute(block, axis, route)


def slot_table(routes, experts, capacity):
    flat_ids = routes.reshape(-1)
    hit_table = (flat_ids[:, None] == jnp.arange(experts, dtype=jnp.int32)[None, :]).astype(
        jnp.int32
    )
    earlier = jnp.cumsum(hit_table, axis=0) - hit_table
    places = jnp.sum(earlier * hit_table, axis=1)
    return (flat_ids * capacity + places).reshape(routes.shape)


def dispatch_rows(tokens, slot_ids, experts, capacity):
    numbered = jnp.arange(experts * capacity, dtype=jnp.int32)
    picker = jnp.any(slot_ids[None, :, :] == numbered[:, None, None], axis=2).astype(jnp.bfloat16)
    filled = jnp.dot(picker, tokens, preferred_element_type=jnp.float32).astype(jnp.bfloat16)
    return jnp.repeat(filled.reshape(experts, capacity, tokens.shape[1]), HSPLIT, axis=0)


def combine_rows(base, returned, slot_ids, weights, experts, capacity):
    width = base.shape[1]
    summed = jnp.sum(returned.astype(jnp.float32).reshape(experts, HSPLIT, capacity, width), axis=1)
    summed = summed.reshape(experts * capacity, width)
    numbered = jnp.arange(experts * capacity, dtype=jnp.int32)
    mixing = jnp.sum(
        weights[:, :, None] * (slot_ids[:, :, None] == numbered[None, None, :]).astype(jnp.float32),
        axis=1,
    )
    total = base.astype(jnp.float32) + jnp.dot(mixing, summed, precision=lax.Precision.HIGHEST)
    return total.astype(jnp.bfloat16)


def forward_rows(received, gate_cols, up_cols, down_rows):
    in_shape = received.shape
    row_block = received.reshape(-1, in_shape[-1])
    pre_gate = jnp.dot(row_block, gate_cols, preferred_element_type=jnp.float32)
    pre_up = jnp.dot(row_block, up_cols, preferred_element_type=jnp.float32)
    hidden = (jax.nn.silu(pre_gate) * pre_up).astype(jnp.bfloat16)
    result = jnp.dot(hidden, down_rows, preferred_element_type=jnp.float32).astype(jnp.bfloat16)
    return result.reshape(in_shape)


def backward_rows(received_x, received_g, gate_cols, up_cols, down_rows):
    in_shape = received_x.shape
    rows_x = received_x.reshape(-1, in_shape[-1])
    rows_g = received_g.reshape(-1, in_shape[-1])
    contract = (((1,), (1,)), ((), ()))
    pre_gate = jnp.dot(rows_x, gate_cols, preferred_element_type=jnp.float32)
    pre_up = jnp.dot(rows_x, up_cols, preferred_element_type=jnp.float32)
    act_grad = lax.dot_general(rows_g, down_rows, contract, preferred_element_type=jnp.float32)
    sigmoid_gate = jax.nn.sigmoid(pre_gate)
    gate_grad = (act_grad * pre_up * sigmoid_gate * (1.0 + pre_gate * (1.0 - sigmoid_gate))).astype(
        jnp.bfloat16
    )
    up_grad = (act_grad * pre_gate * sigmoid_gate).astype(jnp.bfloat16)
    back_rows = lax.dot_general(gate_grad, gate_cols, contract, preferred_element_type=jnp.float32)
    back_rows = back_rows + lax.dot_general(
        up_grad, up_cols, contract, preferred_element_type=jnp.float32
    )
    return back_rows.astype(jnp.bfloat16).reshape(in_shape)


def body(
    x_fwd,
    routes_fwd,
    gates_fwd,
    x_bwd,
    grad_bwd,
    routes_bwd,
    gates_bwd,
    gate_proj,
    up_proj,
    down_proj,
):
    tokens_a = x_fwd[0]
    tokens_b = x_bwd[0]
    grads_b = grad_bwd[0]
    gate_cols = gate_proj[0]
    up_cols = up_proj[0]
    down_rows = down_proj[0]
    experts = lax.axis_size("expert") // HSPLIT
    tok_rows = tokens_a.shape[0]
    capacity = min(tok_rows, tok_rows * TOPK * 3 // (2 * experts))
    slots_a = slot_table(routes_fwd[0], experts, capacity)
    slots_b = slot_table(routes_bwd[0], experts, capacity)
    send_a = dispatch_rows(tokens_a, slots_a, experts, capacity)
    send_x = dispatch_rows(tokens_b, slots_b, experts, capacity)
    send_g = dispatch_rows(grads_b, slots_b, experts, capacity)
    back_a = lax.all_to_all(
        forward_rows(
            lax.all_to_all(send_a, "expert", split_axis=0, concat_axis=0, tiled=True),
            gate_cols,
            up_cols,
            down_rows,
        ),
        "expert",
        split_axis=0,
        concat_axis=0,
        tiled=True,
    )
    back_b = lax.all_to_all(
        backward_rows(
            lax.all_to_all(send_x, "expert", split_axis=0, concat_axis=0, tiled=True),
            lax.all_to_all(send_g, "expert", split_axis=0, concat_axis=0, tiled=True),
            gate_cols,
            up_cols,
            down_rows,
        ),
        "expert",
        split_axis=0,
        concat_axis=0,
        tiled=True,
    )
    out_fwd = combine_rows(tokens_a, back_a, slots_a, gates_fwd[0], experts, capacity)
    out_bwd = combine_rows(grads_b, back_b, slots_b, gates_bwd[0], experts, capacity)
    fwd_next = shifted(out_fwd, "pipe", 1)
    bwd_next = shifted(out_bwd, "pipe", -1)
    return (fwd_next[None], bwd_next[None])


def solution(mesh):
    in_specs = (
        P("pipe", "expert", None),
        P("pipe", "expert", None),
        P("pipe", "expert", None),
        P("pipe", "expert", None),
        P("pipe", "expert", None),
        P("pipe", "expert", None),
        P("pipe", "expert", None),
        P("pipe", None, "expert"),
        P("pipe", None, "expert"),
        P("pipe", "expert", None),
    )
    out_specs = (P("pipe", "expert", None), P("pipe", "expert", None))
    return jax.shard_map(body, mesh=mesh, in_specs=in_specs, out_specs=out_specs, check_vma=False)
```

profile of v0, /device:TPU:9, one launch (start us, length us, event | category | flops | bytes accessed | tf_op | source)
XLA Modules:
  0.0 500.5 jit_solution(3332331879535475281)
XLA Ops:
  4.7 2.3 broadcast_in_dim.10
  7.0 11.2 %all-to-all-start = ((bf16[32,12,3584]{2,1,0:T(8,128)(2,1)}), bf16[32,12,3584]{2,1,0:T(8,128)(2,1)}, u32[]{:S(2)}, u32[]{:S(2)}) async-start(bf16[32,12,3584]{2,1,0:T(8,128)(2,1)} %bitcast.93), calls=%async_computation | async-start | bytes 7340032 | tf_op jit(solution)/shard_map/all_to_all | solution.py:104
  19.2 84.0 %all-to-all-done = bf16[32,12,3584]{2,1,0:T(8,128)(2,1)} async-done(((bf16[32,12,3584]{2,1,0:T(8,128)(2,1)}), bf16[32,12,3584]{2,1,0:T(8,128)(2,1)}, u32[]{:S(2)}, u32[]{:S(2)}) %all-to-all-start) | async-done | bytes 2752544 | tf_op jit(solution)/shard_map/all_to_all | solution.py:104
  103.2 2.3 broadcast_in_dim.24
  105.5 7.2 %all-to-all-start.2 = ((bf16[32,12,3584]{2,1,0:T(8,128)(2,1)}), bf16[32,12,3584]{2,1,0:T(8,128)(2,1)}, u32[]{:S(2)}, u32[]{:S(2)}) async-start(bf16[32,12,3584]{2,1,0:T(8,128)(2,1)} %bitcast.95), calls=%async_computation.2 | async-start | bytes 7340032 | tf_op jit(solution)/shard_map/all_to_all | solution.py:117
  113.3 84.3 %all-to-all-done.2 = bf16[32,12,3584]{2,1,0:T(8,128)(2,1)} async-done(((bf16[32,12,3584]{2,1,0:T(8,128)(2,1)}), bf16[32,12,3584]{2,1,0:T(8,128)(2,1)}, u32[]{:S(2)}, u32[]{:S(2)}) %all-to-all-start.2) | async-done | bytes 2752544 | tf_op jit(solution)/shard_map/all_to_all | solution.py:117
  197.7 2.2 broadcast_in_dim.25
  199.9 7.1 %all-to-all-start.3 = ((bf16[32,12,3584]{2,1,0:T(8,128)(2,1)}), bf16[32,12,3584]{2,1,0:T(8,128)(2,1)}, u32[]{:S(2)}, u32[]{:S(2)}) async-start(bf16[32,12,3584]{2,1,0:T(8,128)(2,1)} %bitcast.94), calls=%async_computation.3 | async-start | bytes 7340032 | tf_op jit(solution)/shard_map/all_to_all | solution.py:116
  207.0 5.4 %reshape.354 = bf16[384,3584]{1,0:T(8,128)(2,1)} reshape(bf16[32,12,3584]{2,1,0:T(8,128)(2,1)} %all-to-all-done) | data formatting | bytes 5505024 | tf_op jit(solution)/shard_map/reshape | solution.py:48
  212.4 3.2 fusion.15
  215.6 6.9 %convolution_convert_fusion = bf16[384,3584]{1,0:T(8,128)(2,1)} fusion(bf16[1,256,3584]{2,1,0:T(8,128)(2,1)} %param.19, bf16[384,3584]{1,0:T(8,128)(2,1)} %reshape.354, bf16[1,3584,256]{2,1,0:T(8,128)(2,1)S(1)} %copy-done, f32[384,256]{1,0:T(8,128)S(1)} %fusion.15), kind=kOutput, calls=%fused_computation.4 | convolution fusion | flops 1411252224 | bytes 9568256 | tf_op jit(solution)/shard_map/dot_general | solution.py:52
  222.5 5.3 %reshape.355 = bf16[32,12,3584]{2,1,0:T(8,128)(2,1)} reshape(bf16[384,3584]{1,0:T(8,128)(2,1)} %convolution_convert_fusion) | data formatting | bytes 5505024 | tf_op jit(solution)/shard_map/reshape | solution.py:53
  227.8 64.2 %all-to-all-done.3 = bf16[32,12,3584]{2,1,0:T(8,128)(2,1)} async-done(((bf16[32,12,3584]{2,1,0:T(8,128)(2,1)}), bf16[32,12,3584]{2,1,0:T(8,128)(2,1)}, u32[]{:S(2)}, u32[]{:S(2)}) %all-to-all-start.3) | async-done | bytes 2752544 | tf_op jit(solution)/shard_map/all_to_all | solution.py:116
  292.0 7.1 %all-to-all-start.1 = ((bf16[32,12,3584]{2,1,0:T(8,128)(2,1)}), bf16[32,12,3584]{2,1,0:T(8,128)(2,1)}, u32[]{:S(2)}, u32[]{:S(2)}) async-start(bf16[32,12,3584]{2,1,0:T(8,128)(2,1)} %reshape.355), calls=%async_computation.1 | async-start | bytes 7340032 | tf_op jit(solution)/shard_map/all_to_all | solution.py:102
  299.1 5.3 %reshape.361 = bf16[384,3584]{1,0:T(8,128)(2,1)} reshape(bf16[32,12,3584]{2,1,0:T(8,128)(2,1)} %all-to-all-done.2) | data formatting | bytes 5505024 | tf_op jit(solution)/shard_map/reshape | solution.py:59
  304.4 5.4 %reshape.364 = bf16[384,3584]{1,0:T(8,128)(2,1)} reshape(bf16[32,12,3584]{2,1,0:T(8,128)(2,1)} %all-to-all-done.3) | data formatting | bytes 5505024 | tf_op jit(solution)/shard_map/reshape | solution.py:58
  309.8 3.4 fusion.3
  314.4 7.8 %fusion.11 = f32[384,3584]{1,0:T(8,128)} fusion(bf16[1,3584,256]{2,1,0:T(8,128)(2,1)} %param.17, f32[384,256]{1,0:T(8,128)S(1)} %fusion.3, bf16[384,3584]{1,0:T(8,128)(2,1)} %reshape.364, bf16[1,3584,256]{2,1,0:T(8,128)(2,1)S(1)} %copy-done, f32[384,256]{1,0:T(8,128)S(1)} %fusion.13), kind=kOutput, calls=%fused_computation.20 | convolution fusion | flops 1410269184 | bytes 12713984 | tf_op jit(solution)/shard_map/dot_general | solution.py:69
  322.2 5.0 %fusion = bf16[384,3584]{1,0:T(8,128)(2,1)} fusion(f32[384,3584]{1,0:T(8,128)} %fusion.11, bf16[1,3584,256]{2,1,0:T(8,128)(2,1)S(1)} %copy-done, f32[384,256]{1,0:T(8,128)S(1)} %fusion.3, f32[384,256]{1,0:T(8,128)S(1)} %fusion.13), kind=kOutput, calls=%fused_computation.3 | convolution fusion | flops 707985408 | bytes 10878976 | tf_op jit(solution)/shard_map/dot_general | solution.py:70
  327.2 5.3 %reshape.365 = bf16[32,12,3584]{2,1,0:T(8,128)(2,1)} reshape(bf16[384,3584]{1,0:T(8,128)(2,1)} %fusion) | data formatting | bytes 5505024 | tf_op jit(solution)/shard_map/reshape | solution.py:73
  332.6 51.5 %all-to-all-done.1 = bf16[32,12,3584]{2,1,0:T(8,128)(2,1)} async-done(((bf16[32,12,3584]{2,1,0:T(8,128)(2,1)}), bf16[32,12,3584]{2,1,0:T(8,128)(2,1)}, u32[]{:S(2)}, u32[]{:S(2)}) %all-to-all-start.1) | async-done | bytes 2752544 | tf_op jit(solution)/shard_map/all_to_all | solution.py:102
  384.1 7.1 %all-to-all-start.4 = ((bf16[32,12,3584]{2,1,0:T(8,128)(2,1)}), bf16[32,12,3584]{2,1,0:T(8,128)(2,1)}, u32[]{:S(2)}, u32[]{:S(2)}) async-start(bf16[32,12,3584]{2,1,0:T(8,128)(2,1)} %reshape.365), calls=%async_computation.4 | async-start | bytes 7340032 | tf_op jit(solution)/shard_map/all_to_all | solution.py:114
  391.6 4.1 convert_reduce_fusion.1
  395.8 1.5 reshape.358
  397.3 2.7 fusion.1
  400.0 3.1 collective-permute-start
  403.1 73.0 %all-to-all-done.4 = bf16[32,12,3584]{2,1,0:T(8,128)(2,1)} async-done(((bf16[32,12,3584]{2,1,0:T(8,128)(2,1)}), bf16[32,12,3584]{2,1,0:T(8,128)(2,1)}, u32[]{:S(2)}, u32[]{:S(2)}) %all-to-all-start.4) | async-done | bytes 2752544 | tf_op jit(solution)/shard_map/all_to_all | solution.py:114
  476.1 4.1 convert_reduce_fusion
  481.8 1.9 fusion.2
  483.8 5.2 %collective-permute-start.1 = (bf16[64,3584]{1,0:T(8,128)(2,1)S(1)}, bf16[64,3584]{1,0:T(8,128)(2,1)S(1)}, u32[]{:S(2)}, u32[]{:S(2)}) collective-permute-start(bf16[64,3584]{1,0:T(8,128)(2,1)S(1)} %fusion.2), channel_id=1, source_target_pairs={{32,0},{64,32},{96,64},{128,96},{160,128},{192,160},{224,192},{33,... | collective-permute-start | bytes 1376264 | tf_op jit(solution)/shard_map/ppermute | solution.py:13
  488.9 8.9 %collective-permute-done.1 = bf16[64,3584]{1,0:T(8,128)(2,1)S(1)} collective-permute-done((bf16[64,3584]{1,0:T(8,128)(2,1)S(1)}, bf16[64,3584]{1,0:T(8,128)(2,1)S(1)}, u32[]{:S(2)}, u32[]{:S(2)}) %collective-permute-start.1) | collective-permute-done | bytes 458784 | tf_op jit(solution)/shard_map/ppermute | solution.py:13
  497.9 1.8 copy.14
  (40 shorter events, 9.6 us)
Async XLA Ops:
  0.6 215.0 %copy-start = (bf16[1,3584,256]{2,1,0:T(8,128)(2,1)S(1)}, bf16[1,3584,256]{2,1,0:T(8,128)(2,1)}, u32[]{:S(2)}) copy-start(bf16[1,3584,256]{2,1,0:T(8,128)(2,1)} %param.18) | copy-start | bytes 5505028
  7.0 11.2 %copy-start.6 = (s32[1,64,1]{1,2,0:T(1,128)S(1)}, s32[1,64,1]{1,2,0:T(1,128)}, u32[]{:S(2)}) copy-start(s32[1,64,1]{1,2,0:T(1,128)} %param.15) | copy-start | bytes 772
  7.0 11.6 %copy-start.3 = (bf16[1,64,3584]{2,1,0:T(8,128)(2,1)S(1)}, bf16[1,64,3584]{2,1,0:T(8,128)(2,1)}, u32[]{:S(2)}) copy-start(bf16[1,64,3584]{2,1,0:T(8,128)(2,1)} %param.14) | copy-start | bytes 1376260
  7.0 96.2 %all-to-all-start = ((bf16[32,12,3584]{2,1,0:T(8,128)(2,1)}), bf16[32,12,3584]{2,1,0:T(8,128)(2,1)}, u32[]{:S(2)}, u32[]{:S(2)}) async-start(bf16[32,12,3584]{2,1,0:T(8,128)(2,1)} %bitcast.93), calls=%async_computation | async-start | bytes 7340032 | tf_op jit(solution)/shard_map/all_to_all | solution.py:104
  105.5 7.2 %copy-start.4 = (bf16[1,64,3584]{2,1,0:T(8,128)(2,1)S(1)}, bf16[1,64,3584]{2,1,0:T(8,128)(2,1)}, u32[]{:S(2)}) copy-start(bf16[1,64,3584]{2,1,0:T(8,128)(2,1)} %param.13) | copy-start | bytes 1376260
  105.5 92.2 %all-to-all-start.2 = ((bf16[32,12,3584]{2,1,0:T(8,128)(2,1)}), bf16[32,12,3584]{2,1,0:T(8,128)(2,1)}, u32[]{:S(2)}, u32[]{:S(2)}) async-start(bf16[32,12,3584]{2,1,0:T(8,128)(2,1)} %bitcast.95), calls=%async_computation.2 | async-start | bytes 7340032 | tf_op jit(solution)/shard_map/all_to_all | solution.py:117
  199.9 92.1 %all-to-all-start.3 = ((bf16[32,12,3584]{2,1,0:T(8,128)(2,1)}), bf16[32,12,3584]{2,1,0:T(8,128)(2,1)}, u32[]{:S(2)}, u32[]{:S(2)}) async-start(bf16[32,12,3584]{2,1,0:T(8,128)(2,1)} %bitcast.94), calls=%async_computation.3 | async-start | bytes 7340032 | tf_op jit(solution)/shard_map/all_to_all | solution.py:116
  292.0 92.1 %all-to-all-start.1 = ((bf16[32,12,3584]{2,1,0:T(8,128)(2,1)}), bf16[32,12,3584]{2,1,0:T(8,128)(2,1)}, u32[]{:S(2)}, u32[]{:S(2)}) async-start(bf16[32,12,3584]{2,1,0:T(8,128)(2,1)} %reshape.355), calls=%async_computation.1 | async-start | bytes 7340032 | tf_op jit(solution)/shard_map/all_to_all | solution.py:102
  309.8 3.4 copy-start.1
  309.8 3.7 copy-start.2
  332.6 58.6 %copy-start.5 = (s32[1,64,1]{1,2,0:T(1,128)S(1)}, s32[1,64,1]{1,2,0:T(1,128)}, u32[]{:S(2)}) copy-start(s32[1,64,1]{1,2,0:T(1,128)} %param.11) | copy-start | bytes 772
  332.6 58.6 %copy-start.7 = (f32[1,64,1]{1,2,0:T(1,128)S(1)}, f32[1,64,1]{1,2,0:T(1,128)}, u32[]{:S(2)}) copy-start(f32[1,64,1]{1,2,0:T(1,128)} %param.12) | copy-start | bytes 772
  332.6 58.8 %copy-start.8 = (f32[1,64,1]{1,2,0:T(1,128)S(1)}, f32[1,64,1]{1,2,0:T(1,128)}, u32[]{:S(2)}) copy-start(f32[1,64,1]{1,2,0:T(1,128)} %param.16) | copy-start | bytes 772
  384.1 92.1 %all-to-all-start.4 = ((bf16[32,12,3584]{2,1,0:T(8,128)(2,1)}), bf16[32,12,3584]{2,1,0:T(8,128)(2,1)}, u32[]{:S(2)}, u32[]{:S(2)}) async-start(bf16[32,12,3584]{2,1,0:T(8,128)(2,1)} %reshape.365), calls=%async_computation.4 | async-start | bytes 7340032 | tf_op jit(solution)/shard_map/all_to_all | solution.py:114
  400.0 88.9 %collective-permute-start = (bf16[64,3584]{1,0:T(8,128)(2,1)}, bf16[64,3584]{1,0:T(8,128)(2,1)}, u32[]{:S(2)}, u32[]{:S(2)}) collective-permute-start(bf16[64,3584]{1,0:T(8,128)(2,1)} %fusion.1), channel_id=1, source_target_pairs={{0,32},{32,64},{64,96},{96,128},{128,160},{160,192},{192,224},{1,3... | collective-permute-start | bytes 1376264 | tf_op jit(solution)/shard_map/ppermute | solution.py:13
  483.8 14.1 %collective-permute-start.1 = (bf16[64,3584]{1,0:T(8,128)(2,1)S(1)}, bf16[64,3584]{1,0:T(8,128)(2,1)S(1)}, u32[]{:S(2)}, u32[]{:S(2)}) collective-permute-start(bf16[64,3584]{1,0:T(8,128)(2,1)S(1)} %fusion.2), channel_id=1, source_target_pairs={{32,0},{64,32},{96,64},{128,96},{160,128},{192,160},{224,192},{33,... | collective-permute-start | bytes 1376264 | tf_op jit(solution)/shard_map/ppermute | solution.py:13
where the time goes:
time: 506 us; the launch traced here: 500 us
  waiting for transfers between devices  366 us (72%)
  starting transfers between devices  48 us (9%)
  local copies, waits for them, and re-layouts  40 us (8%)
  matrix products  34.2 us (7%)
  other arithmetic  11.5 us (2%)
    all_to_all x1, waiting for transfers between devices, body(): lax.all_to_all(send_g, 'expert', split_axis=0, concat_axis=0, tiled=True)  84.3 us
    all_to_all x1, waiting for transfers between devices, body(): lax.all_to_all(send_a, 'expert', split_axis=0, concat_axis=0, tiled=True)  84 us
    all_to_all x1, waiting for transfers between devices, body(): lax.all_to_all(backward_rows(lax.all_to_all(send_x, 'expert', split_axis=...  73 us
    all_to_all x1, waiting for transfers between devices, body(): lax.all_to_all(send_x, 'expert', split_axis=0, concat_axis=0, tiled=True)  64.2 us
    all_to_all x1, waiting for transfers between devices, body(): lax.all_to_all(forward_rows(lax.all_to_all(send_a, 'expert', split_axis=0...  51.5 us
    all_to_all x1, starting transfers between devices, body(): lax.all_to_all(send_a, 'expert', split_axis=0, concat_axis=0, tiled=True)  11.2 us
  transfers between devices with their start and end apart: 7, of which 6 were waited for; matrix products, arithmetic and copies ran while one was open for 14% of the time, Pallas kernels for 0%

commit v1 on v0

--- a/solution.py
+++ b/solution.py
@@ -15,11 +15,9 @@
 
 def slot_table(routes, experts, capacity):
     flat_ids = routes.reshape(-1)
-    hit_table = (flat_ids[:, None] == jnp.arange(experts, dtype=jnp.int32)[None, :]).astype(
-        jnp.int32
-    )
-    earlier = jnp.cumsum(hit_table, axis=0) - hit_table
-    places = jnp.sum(earlier * hit_table, axis=1)
+    order = jnp.arange(flat_ids.shape[0], dtype=jnp.int32)
+    before = (order[None, :] < order[:, None]) & (flat_ids[None, :] == flat_ids[:, None])
+    places = jnp.sum(before.astype(jnp.int32), axis=1)
     return (flat_ids * capacity + places).reshape(routes.shape)
 
 

time: 506 us -> 505 us (level)
  no operation moved by 1% of the time
where the time goes in v1:
time: 505 us; the launch traced here: 500 us
  waiting for transfers between devices  366 us (72%)
  starting transfers between devices  48.1 us (10%)
  local copies, waits for them, and re-layouts  39.9 us (8%)
  matrix products  34.2 us (7%)
  other arithmetic  10.5 us (2%)
    all_to_all x1, waiting for transfers between devices, body(): lax.all_to_all(send_g, 'expert', split_axis=0, concat_axis=0, tiled=True)  84.3 us
    all_to_all x1, waiting for transfers between devices, body(): lax.all_to_all(send_a, 'expert', split_axis=0, concat_axis=0, tiled=True)  84.1 us
    all_to_all x1, waiting for transfers between devices, body(): lax.all_to_all(backward_rows(lax.all_to_all(send_x, 'expert', split_axis=...  73 us
    all_to_all x1, waiting for transfers between devices, body(): lax.all_to_all(send_x, 'expert', split_axis=0, concat_axis=0, tiled=True)  64.2 us
    all_to_all x1, waiting for transfers between devices, body(): lax.all_to_all(forward_rows(lax.all_to_all(send_a, 'expert', split_axis=0...  51.5 us
    all_to_all x1, starting transfers between devices, body(): lax.all_to_all(send_a, 'expert', split_axis=0, concat_axis=0, tiled=True)  11.2 us
  transfers between devices with their start and end apart: 7, of which 6 were waited for; matrix products, arithmetic and copies ran while one was open for 14% of the time, Pallas kernels for 0%

profile of v1, /device:TPU:9, one launch (start us, length us, event | category | flops | bytes accessed | tf_op | source)
XLA Modules:
  0.0 499.6 jit_solution(4893664643288382137)
XLA Ops:
  3.9 2.3 broadcast_in_dim.10
  6.2 11.2 %all-to-all-start = ((bf16[32,12,3584]{2,1,0:T(8,128)(2,1)}), bf16[32,12,3584]{2,1,0:T(8,128)(2,1)}, u32[]{:S(2)}, u32[]{:S(2)}) async-start(bf16[32,12,3584]{2,1,0:T(8,128)(2,1)} %bitcast.94), calls=%async_computation | async-start | bytes 7340032 | tf_op jit(solution)/shard_map/all_to_all | solution.py:102
  18.2 84.1 %all-to-all-done = bf16[32,12,3584]{2,1,0:T(8,128)(2,1)} async-done(((bf16[32,12,3584]{2,1,0:T(8,128)(2,1)}), bf16[32,12,3584]{2,1,0:T(8,128)(2,1)}, u32[]{:S(2)}, u32[]{:S(2)}) %all-to-all-start) | async-done | bytes 2752544 | tf_op jit(solution)/shard_map/all_to_all | solution.py:102
  102.4 2.3 broadcast_in_dim.12
  104.6 7.2 %all-to-all-start.2 = ((bf16[32,12,3584]{2,1,0:T(8,128)(2,1)}), bf16[32,12,3584]{2,1,0:T(8,128)(2,1)}, u32[]{:S(2)}, u32[]{:S(2)}) async-start(bf16[32,12,3584]{2,1,0:T(8,128)(2,1)} %bitcast.95), calls=%async_computation.2 | async-start | bytes 7340032 | tf_op jit(solution)/shard_map/all_to_all | solution.py:115
  112.5 84.3 %all-to-all-done.2 = bf16[32,12,3584]{2,1,0:T(8,128)(2,1)} async-done(((bf16[32,12,3584]{2,1,0:T(8,128)(2,1)}), bf16[32,12,3584]{2,1,0:T(8,128)(2,1)}, u32[]{:S(2)}, u32[]{:S(2)}) %all-to-all-start.2) | async-done | bytes 2752544 | tf_op jit(solution)/shard_map/all_to_all | solution.py:115
  196.8 2.2 broadcast_in_dim.13
  199.1 7.1 %all-to-all-start.3 = ((bf16[32,12,3584]{2,1,0:T(8,128)(2,1)}), bf16[32,12,3584]{2,1,0:T(8,128)(2,1)}, u32[]{:S(2)}, u32[]{:S(2)}) async-start(bf16[32,12,3584]{2,1,0:T(8,128)(2,1)} %bitcast.93), calls=%async_computation.3 | async-start | bytes 7340032 | tf_op jit(solution)/shard_map/all_to_all | solution.py:114
  206.2 5.4 %reshape.356 = bf16[384,3584]{1,0:T(8,128)(2,1)} reshape(bf16[32,12,3584]{2,1,0:T(8,128)(2,1)} %all-to-all-done) | data formatting | bytes 5505024 | tf_op jit(solution)/shard_map/reshape | solution.py:46
  211.5 3.2 fusion.15
  214.7 6.9 %convolution_convert_fusion = bf16[384,3584]{1,0:T(8,128)(2,1)} fusion(bf16[1,256,3584]{2,1,0:T(8,128)(2,1)} %param.19, bf16[384,3584]{1,0:T(8,128)(2,1)} %reshape.356, bf16[1,3584,256]{2,1,0:T(8,128)(2,1)S(1)} %copy-done, f32[384,256]{1,0:T(8,128)S(1)} %fusion.15), kind=kOutput, calls=%fused_computation.4 | convolution fusion | flops 1411252224 | bytes 9568256 | tf_op jit(solution)/shard_map/dot_general | solution.py:50
  221.6 5.3 %reshape.357 = bf16[32,12,3584]{2,1,0:T(8,128)(2,1)} reshape(bf16[384,3584]{1,0:T(8,128)(2,1)} %convolution_convert_fusion) | data formatting | bytes 5505024 | tf_op jit(solution)/shard_map/reshape | solution.py:51
  226.9 64.2 %all-to-all-done.3 = bf16[32,12,3584]{2,1,0:T(8,128)(2,1)} async-done(((bf16[32,12,3584]{2,1,0:T(8,128)(2,1)}), bf16[32,12,3584]{2,1,0:T(8,128)(2,1)}, u32[]{:S(2)}, u32[]{:S(2)}) %all-to-all-start.3) | async-done | bytes 2752544 | tf_op jit(solution)/shard_map/all_to_all | solution.py:114
  291.1 7.1 %all-to-all-start.1 = ((bf16[32,12,3584]{2,1,0:T(8,128)(2,1)}), bf16[32,12,3584]{2,1,0:T(8,128)(2,1)}, u32[]{:S(2)}, u32[]{:S(2)}) async-start(bf16[32,12,3584]{2,1,0:T(8,128)(2,1)} %reshape.357), calls=%async_computation.1 | async-start | bytes 7340032 | tf_op jit(solution)/shard_map/all_to_all | solution.py:100
  298.3 5.3 %reshape.363 = bf16[384,3584]{1,0:T(8,128)(2,1)} reshape(bf16[32,12,3584]{2,1,0:T(8,128)(2,1)} %all-to-all-done.2) | data formatting | bytes 5505024 | tf_op jit(solution)/shard_map/reshape | solution.py:57
  303.6 5.4 %reshape.366 = bf16[384,3584]{1,0:T(8,128)(2,1)} reshape(bf16[32,12,3584]{2,1,0:T(8,128)(2,1)} %all-to-all-done.3) | data formatting | bytes 5505024 | tf_op jit(solution)/shard_map/reshape | solution.py:56
  309.0 3.4 fusion.3
  313.6 7.8 %fusion.11 = f32[384,3584]{1,0:T(8,128)} fusion(bf16[1,3584,256]{2,1,0:T(8,128)(2,1)} %param.17, f32[384,256]{1,0:T(8,128)S(1)} %fusion.3, bf16[384,3584]{1,0:T(8,128)(2,1)} %reshape.366, bf16[1,3584,256]{2,1,0:T(8,128)(2,1)S(1)} %copy-done, f32[384,256]{1,0:T(8,128)S(1)} %fusion.13), kind=kOutput, calls=%fused_computation.20 | convolution fusion | flops 1410269184 | bytes 12713984 | tf_op jit(solution)/shard_map/dot_general | solution.py:67
  321.4 5.0 %fusion = bf16[384,3584]{1,0:T(8,128)(2,1)} fusion(f32[384,3584]{1,0:T(8,128)} %fusion.11, bf16[1,3584,256]{2,1,0:T(8,128)(2,1)S(1)} %copy-done, f32[384,256]{1,0:T(8,128)S(1)} %fusion.3, f32[384,256]{1,0:T(8,128)S(1)} %fusion.13), kind=kOutput, calls=%fused_computation.3 | convolution fusion | flops 707985408 | bytes 10878976 | tf_op jit(solution)/shard_map/dot_general | solution.py:68
  326.4 5.3 %reshape.367 = bf16[32,12,3584]{2,1,0:T(8,128)(2,1)} reshape(bf16[384,3584]{1,0:T(8,128)(2,1)} %fusion) | data formatting | bytes 5505024 | tf_op jit(solution)/shard_map/reshape | solution.py:71
  331.7 51.5 %all-to-all-done.1 = bf16[32,12,3584]{2,1,0:T(8,128)(2,1)} async-done(((bf16[32,12,3584]{2,1,0:T(8,128)(2,1)}), bf16[32,12,3584]{2,1,0:T(8,128)(2,1)}, u32[]{:S(2)}, u32[]{:S(2)}) %all-to-all-start.1) | async-done | bytes 2752544 | tf_op jit(solution)/shard_map/all_to_all | solution.py:100
  383.2 7.1 %all-to-all-start.4 = ((bf16[32,12,3584]{2,1,0:T(8,128)(2,1)}), bf16[32,12,3584]{2,1,0:T(8,128)(2,1)}, u32[]{:S(2)}, u32[]{:S(2)}) async-start(bf16[32,12,3584]{2,1,0:T(8,128)(2,1)} %reshape.367), calls=%async_computation.4 | async-start | bytes 7340032 | tf_op jit(solution)/shard_map/all_to_all | solution.py:112
  390.8 4.1 convert_reduce_fusion.1
  396.5 2.7 fusion.1
  399.2 3.1 collective-permute-start
  402.3 73.0 %all-to-all-done.4 = bf16[32,12,3584]{2,1,0:T(8,128)(2,1)} async-done(((bf16[32,12,3584]{2,1,0:T(8,128)(2,1)}), bf16[32,12,3584]{2,1,0:T(8,128)(2,1)}, u32[]{:S(2)}, u32[]{:S(2)}) %all-to-all-start.4) | async-done | bytes 2752544 | tf_op jit(solution)/shard_map/all_to_all | solution.py:112
  475.3 4.1 convert_reduce_fusion
  479.4 1.5 reshape.370
  480.9 1.9 fusion.2
  482.9 5.2 %collective-permute-start.1 = (bf16[64,3584]{1,0:T(8,128)(2,1)S(1)}, bf16[64,3584]{1,0:T(8,128)(2,1)S(1)}, u32[]{:S(2)}, u32[]{:S(2)}) collective-permute-start(bf16[64,3584]{1,0:T(8,128)(2,1)S(1)} %fusion.2), channel_id=1, source_target_pairs={{32,0},{64,32},{96,64},{128,96},{160,128},{192,160},{224,192},{33,... | collective-permute-start | bytes 1376264 | tf_op jit(solution)/shard_map/ppermute | solution.py:13
  488.1 8.9 %collective-permute-done.1 = bf16[64,3584]{1,0:T(8,128)(2,1)S(1)} collective-permute-done((bf16[64,3584]{1,0:T(8,128)(2,1)S(1)}, bf16[64,3584]{1,0:T(8,128)(2,1)S(1)}, u32[]{:S(2)}, u32[]{:S(2)}) %collective-permute-start.1) | collective-permute-done | bytes 458784 | tf_op jit(solution)/shard_map/ppermute | solution.py:13
  497.0 1.8 copy.14
  (36 shorter events, 8.6 us)
Async XLA Ops:
  0.6 214.1 %copy-start = (bf16[1,3584,256]{2,1,0:T(8,128)(2,1)S(1)}, bf16[1,3584,256]{2,1,0:T(8,128)(2,1)}, u32[]{:S(2)}) copy-start(bf16[1,3584,256]{2,1,0:T(8,128)(2,1)} %param.18) | copy-start | bytes 5505028
  6.2 11.2 %copy-start.8 = (s32[1,64,1]{1,2,0:T(1,128)S(1)}, s32[1,64,1]{1,2,0:T(1,128)}, u32[]{:S(2)}) copy-start(s32[1,64,1]{1,2,0:T(1,128)} %param.15) | copy-start | bytes 772
  6.2 11.4 %copy-start.3 = (bf16[1,64,3584]{2,1,0:T(8,128)(2,1)S(1)}, bf16[1,64,3584]{2,1,0:T(8,128)(2,1)}, u32[]{:S(2)}) copy-start(bf16[1,64,3584]{2,1,0:T(8,128)(2,1)} %param.14) | copy-start | bytes 1376260
  6.2 96.2 %all-to-all-start = ((bf16[32,12,3584]{2,1,0:T(8,128)(2,1)}), bf16[32,12,3584]{2,1,0:T(8,128)(2,1)}, u32[]{:S(2)}, u32[]{:S(2)}) async-start(bf16[32,12,3584]{2,1,0:T(8,128)(2,1)} %bitcast.94), calls=%async_computation | async-start | bytes 7340032 | tf_op jit(solution)/shard_map/all_to_all | solution.py:102
  104.6 7.3 %copy-start.4 = (bf16[1,64,3584]{2,1,0:T(8,128)(2,1)S(1)}, bf16[1,64,3584]{2,1,0:T(8,128)(2,1)}, u32[]{:S(2)}) copy-start(bf16[1,64,3584]{2,1,0:T(8,128)(2,1)} %param.13) | copy-start | bytes 1376260
  104.6 92.2 %all-to-all-start.2 = ((bf16[32,12,3584]{2,1,0:T(8,128)(2,1)}), bf16[32,12,3584]{2,1,0:T(8,128)(2,1)}, u32[]{:S(2)}, u32[]{:S(2)}) async-start(bf16[32,12,3584]{2,1,0:T(8,128)(2,1)} %bitcast.95), calls=%async_computation.2 | async-start | bytes 7340032 | tf_op jit(solution)/shard_map/all_to_all | solution.py:115
  199.1 92.1 %all-to-all-start.3 = ((bf16[32,12,3584]{2,1,0:T(8,128)(2,1)}), bf16[32,12,3584]{2,1,0:T(8,128)(2,1)}, u32[]{:S(2)}, u32[]{:S(2)}) async-start(bf16[32,12,3584]{2,1,0:T(8,128)(2,1)} %bitcast.93), calls=%async_computation.3 | async-start | bytes 7340032 | tf_op jit(solution)/shard_map/all_to_all | solution.py:114
  291.1 92.1 %all-to-all-start.1 = ((bf16[32,12,3584]{2,1,0:T(8,128)(2,1)}), bf16[32,12,3584]{2,1,0:T(8,128)(2,1)}, u32[]{:S(2)}, u32[]{:S(2)}) async-start(bf16[32,12,3584]{2,1,0:T(8,128)(2,1)} %reshape.357), calls=%async_computation.1 | async-start | bytes 7340032 | tf_op jit(solution)/shard_map/all_to_all | solution.py:100
  309.0 3.4 copy-start.1
  309.0 3.7 copy-start.2
  331.7 58.6 %copy-start.7 = (s32[1,64,1]{1,2,0:T(1,128)S(1)}, s32[1,64,1]{1,2,0:T(1,128)}, u32[]{:S(2)}) copy-start(s32[1,64,1]{1,2,0:T(1,128)} %param.11) | copy-start | bytes 772
  331.7 58.6 %copy-start.5 = (f32[1,64,1]{1,2,0:T(1,128)S(1)}, f32[1,64,1]{1,2,0:T(1,128)}, u32[]{:S(2)}) copy-start(f32[1,64,1]{1,2,0:T(1,128)} %param.12) | copy-start | bytes 772
  331.7 58.8 %copy-start.6 = (f32[1,64,1]{1,2,0:T(1,128)S(1)}, f32[1,64,1]{1,2,0:T(1,128)}, u32[]{:S(2)}) copy-start(f32[1,64,1]{1,2,0:T(1,128)} %param.16) | copy-start | bytes 772
  383.2 92.1 %all-to-all-start.4 = ((bf16[32,12,3584]{2,1,0:T(8,128)(2,1)}), bf16[32,12,3584]{2,1,0:T(8,128)(2,1)}, u32[]{:S(2)}, u32[]{:S(2)}) async-start(bf16[32,12,3584]{2,1,0:T(8,128)(2,1)} %reshape.367), calls=%async_computation.4 | async-start | bytes 7340032 | tf_op jit(solution)/shard_map/all_to_all | solution.py:112
  399.2 88.9 %collective-permute-start = (bf16[64,3584]{1,0:T(8,128)(2,1)}, bf16[64,3584]{1,0:T(8,128)(2,1)}, u32[]{:S(2)}, u32[]{:S(2)}) collective-permute-start(bf16[64,3584]{1,0:T(8,128)(2,1)} %fusion.1), channel_id=1, source_target_pairs={{0,32},{32,64},{64,96},{96,128},{128,160},{160,192},{192,224},{1,3... | collective-permute-start | bytes 1376264 | tf_op jit(solution)/shard_map/ppermute | solution.py:13
  482.9 14.1 %collective-permute-start.1 = (bf16[64,3584]{1,0:T(8,128)(2,1)S(1)}, bf16[64,3584]{1,0:T(8,128)(2,1)S(1)}, u32[]{:S(2)}, u32[]{:S(2)}) collective-permute-start(bf16[64,3584]{1,0:T(8,128)(2,1)S(1)} %fusion.2), channel_id=1, source_target_pairs={{32,0},{64,32},{96,64},{128,96},{160,128},{192,160},{224,192},{33,... | collective-permute-start | bytes 1376264 | tf_op jit(solution)/shard_map/ppermute | solution.py:13

commit v2 on v1

v2 whole, which is shorter than its diff:
```python
import jax
import jax.numpy as jnp
from jax import lax
from jax.experimental import pallas as pl
from jax.experimental.pallas import tpu as pltpu
from jax.sharding import PartitionSpec as P

D = 3584
HALF = D // 2
HID = 256
TOK = 64
CAP = 12
MSG = 4 * CAP
ROWS = 8 * CAP
PAIRS = 4
STEPS = 4
BF = jnp.bfloat16
F32 = jnp.float32
NT = (((1,), (1,)), ((), ()))


def at(y, p, b, c):
    return ((y * PAIRS + p) * 2 + b) * 2 + c


def places_of():
    return [
        (y, p, b, c) for y in range(2) for p in range(PAIRS) for b in range(2) for c in range(2)
    ]


def near(step):
    pairs = []
    for y, p, b, c in places_of():
        if step == 0:
            dp, nb = 0, b
        elif step == 3:
            dp, nb = 2, 1 - b
        elif (step == 1) == (b == 0):
            dp, nb = 1, 0
        else:
            dp, nb = -1, 1
        pairs.append((at(y, p, b, c), at(c, (p + dp) % PAIRS, nb, y)))
    return pairs


def other_core(block):
    pairs = [(at(y, p, b, c), at(y, p, b, 1 - c)) for y, p, b, c in places_of()]
    return lax.ppermute(block, "expert", pairs)


def other_chip(block):
    pairs = [(at(y, p, b, c), at(y, p, 1 - b, c)) for y, p, b, c in places_of()]
    return lax.ppermute(block, "expert", pairs)


def to_section(block, distance, pairs):
    sections, members = lax.axis_size("pipe"), lax.axis_size("expert")
    route = [
        (s * members + i, (s + distance) * members + j)
        for s in range(sections)
        if 0 <= s + distance < sections
        for i, j in pairs
    ]
    return lax.ppermute(block, ("pipe", "expert"), route)


def vmem(n):
    return [pl.BlockSpec(memory_space=pltpu.VMEM)] * n


def call(kernel, outs, n_in, name, smem=0, flops=0, scratch=(), limit=40):
    return pl.pallas_call(
        kernel,
        out_shape=outs,
        in_specs=[pl.BlockSpec(memory_space=pltpu.SMEM)] * smem + vmem(n_in),
        out_specs=tuple(vmem(len(outs))),
        scratch_shapes=scratch,
        compiler_params=pltpu.CompilerParams(vmem_limit_bytes=limit * 2**20),
        cost_estimate=pl.CostEstimate(flops=flops, bytes_accessed=4_000_000, transcendentals=0),
        name=name,
    )


def row_numbers(me_ref, own_ref, other_ref, span):
    me = me_ref[0]
    core, chip, pair = me % 2, (me // 2) % 2, (me // 4) % PAIRS
    column = jnp.concatenate([own_ref[...], other_ref[...]], axis=0).astype(jnp.int32)
    n = 2 * TOK
    first = lax.broadcasted_iota(jnp.int32, (n, n), 0)
    second = lax.broadcasted_iota(jnp.int32, (n, n), 1)
    wide = jnp.broadcast_to(column, (n, n))
    line = jnp.sum(jnp.where(first == second, wide, 0), axis=0, keepdims=True)
    same_group = (first < TOK) == (second < TOK)
    before = (wide == line) & (first < second) & same_group
    place = jnp.sum(before.astype(jnp.int32), axis=0, keepdims=True)
    dp = ((line & 3) - pair + 4) & 3
    side = jnp.where(chip == 0, 1, 3)
    step = jnp.where(dp == 0, 0, jnp.where(dp == 2, 3, jnp.where(dp == side, 1, 2)))
    is_other = (lax.broadcasted_iota(jnp.int32, (1, n), 1) >= TOK).astype(jnp.int32)
    row = step * span + is_other * CAP + place
    return jnp.where((line >> 2) == core, row, -1)


def dispatch_kernel(me_ref, own_ids, other_ids, own_ref, other_ref, *outs):
    row = row_numbers(me_ref, own_ids, other_ids, 2 * CAP)
    pick = (lax.broadcasted_iota(jnp.int32, (ROWS, 2 * TOK), 0) == row).astype(BF)
    width = 256
    for j in range(HALF // width):
        parts = []
        for at_col in (j * width, HALF + j * width):
            columns = slice(at_col, at_col + width)
            tokens = jnp.concatenate([own_ref[:, columns], other_ref[:, columns]], axis=0)
            parts.append(jnp.dot(pick, tokens, preferred_element_type=F32))
        for s in range(STEPS):
            rows = slice(s * 2 * CAP, (s + 1) * 2 * CAP)
            block = jnp.concatenate([parts[0][rows], parts[1][rows]], axis=0)
            outs[s][:, j * width : (j + 1) * width] = block.astype(BF)


def join_kernel(*refs):
    out = refs[-1]
    for j in range(HALF // 256):
        columns = slice(j * 256, (j + 1) * 256)
        blocks = [r[:, columns].astype(F32) for r in refs[:-1]]
        low = jnp.concatenate([b[: 2 * CAP] for b in blocks], axis=0)
        high = jnp.concatenate([b[2 * CAP :] for b in blocks], axis=0)
        out[:, columns] = low.astype(BF)
        out[:, HALF + j * 256 : HALF + (j + 1) * 256] = high.astype(BF)


def stacked(refs):
    return jnp.concatenate([r[...] for r in refs], axis=0)


def forward_kernel(x0, x1, x2, x3, gate, up, down, o0, o1, o2, o3):
    rows = stacked((x0, x1, x2, x3))
    pre_gate = jnp.dot(rows, gate[...], preferred_element_type=F32)
    pre_up = jnp.dot(rows, up[...], preferred_element_type=F32)
    hidden = (jax.nn.silu(pre_gate) * pre_up).astype(BF)
    for j in range(D // 512):
        columns = slice(j * 512, (j + 1) * 512)
        part = jnp.dot(hidden, down[:, columns], preferred_element_type=F32).astype(BF)
        for k, o in enumerate((o0, o1, o2, o3)):
            o[:, columns] = part[k * ROWS : (k + 1) * ROWS]


def before_kernel(x0, x1, x2, x3, gate, up, pre_gate, pre_up):
    rows = stacked((x0, x1, x2, x3))
    pre_gate[...] = jnp.dot(rows, gate[...], preferred_element_type=F32)
    pre_up[...] = jnp.dot(rows, up[...], preferred_element_type=F32)


def backward_kernel(g0, g1, g2, g3, pre_gate_ref, pre_up_ref, gate, up, down, o0, o1, o2, o3):
    rows = stacked((g0, g1, g2, g3))
    act_grad = lax.dot_general(rows, down[...], NT, preferred_element_type=F32)
    pre_gate, pre_up = pre_gate_ref[...], pre_up_ref[...]
    sig = jax.nn.sigmoid(pre_gate)
    gate_grad = (act_grad * pre_up * sig * (1.0 + pre_gate * (1.0 - sig))).astype(BF)
    up_grad = (act_grad * pre_gate * sig).astype(BF)
    for j in range(D // 512):
        columns = slice(j * 512, (j + 1) * 512)
        part = lax.dot_general(gate_grad, gate[columns, :], NT, preferred_element_type=F32)
        part = part + lax.dot_general(up_grad, up[columns, :], NT, preferred_element_type=F32)
        part = part.astype(BF)
        for k, o in enumerate((o0, o1, o2, o3)):
            o[:, columns] = part[k * ROWS : (k + 1) * ROWS]


def add_kernel(a, b, o):
    o[...] = (a[...].astype(F32) + b[...].astype(F32)).astype(BF)


def split_kernel(a, b, c, *outs):
    for j in range(HALF // 256):
        parts = []
        for at_col in (j * 256, HALF + j * 256):
            columns = slice(at_col, at_col + 256)
            parts.append(
                a[:, columns].astype(F32) + b[:, columns].astype(F32) + c[:, columns].astype(F32)
            )
        for s in range(STEPS):
            rows = slice(s * 2 * CAP, (s + 1) * 2 * CAP)
            block = jnp.concatenate([parts[0][rows], parts[1][rows]], axis=0)
            outs[s][:, j * 256 : (j + 1) * 256] = block.astype(BF)


def pick_kernel(me_ref, own_ids, other_ids, m0, m1, m2, m3, mine, theirs):
    row = row_numbers(me_ref, own_ids, other_ids, MSG)
    where = lax.broadcasted_iota(jnp.int32, (STEPS * MSG, 2 * TOK), 0)
    low = (where == row).astype(F32).T.astype(BF)
    high = ((where == row + 2 * CAP) & (row >= 0)).astype(F32).T.astype(BF)
    for j in range(HALF // 256):
        columns = slice(j * 256, (j + 1) * 256)
        rows = jnp.concatenate([m[:, columns] for m in (m0, m1, m2, m3)], axis=0)
        for at_col, pick in ((j * 256, low), (HALF + j * 256, high)):
            got = jnp.dot(pick, rows, preferred_element_type=F32).astype(BF)
            mine[:, at_col : at_col + 256] = got[:TOK]
            theirs[:, at_col : at_col + 256] = got[TOK:]


def final_kernel(base, gates, mine, theirs, o):
    weight = gates[...]
    for j in range(D // 512):
        columns = slice(j * 512, (j + 1) * 512)
        row = mine[:, columns].astype(F32) + theirs[:, columns].astype(F32)
        o[:, columns] = (base[:, columns].astype(F32) + weight * row).astype(BF)


def shape(*dims, kind=BF):
    return jax.ShapeDtypeStruct(dims, kind)


def dispatch(me, own_ids, other_ids, own, other):
    outs = [shape(MSG, HALF)] * STEPS
    return call(dispatch_kernel, outs, 4, "dispatch", smem=1)(me, own_ids, other_ids, own, other)


def gather(messages):
    (own,) = call(join_kernel, [shape(ROWS, D)], STEPS, "join")(*messages)
    across = other_chip(own)
    beside = other_core(own)
    return own, beside, across, other_core(across)


def give_back(parts, distance):
    own, beside, across, diagonal = parts
    from_diagonal = other_core(diagonal)
    from_beside = other_core(beside)
    (chip_sum,) = call(add_kernel, [shape(ROWS, D)], 2, "chip_sum")(across, from_diagonal)
    from_across = other_chip(chip_sum)
    messages = call(split_kernel, [shape(MSG, HALF)] * STEPS, 3, "pair_sum")(
        own, from_beside, from_across
    )
    return [
        to_section(m, distance, [(j, i) for i, j in near(s)]) for s, m in enumerate(messages)
    ]


def finish(me, messages, base, meta):
    own_ids, other_ids, gates = meta[:, 0:1], meta[:, 1:2], meta[:, 2:3]
    mine, theirs = call(pick_kernel, [shape(TOK, D)] * 2, 6, "pick", smem=1)(
        me, own_ids, other_ids, *messages
    )
    (out,) = call(final_kernel, [shape(TOK, D)], 4, "final")(base, gates, mine, other_core(theirs))
    return out


def body(x_fwd, routes_fwd, gates_fwd, x_bwd, grad_bwd, routes_bwd, gates_bwd, gate, up, down):
    x_a, x_b, g_b = x_fwd[0], x_bwd[0], grad_bwd[0]
    gate, up, down = gate[0], up[0], down[0]
    me = lax.axis_index("expert").astype(jnp.int32).reshape(1)
    same = [(i, i) for i in range(lax.axis_size("expert"))]

    ids = jnp.concatenate([routes_fwd[0], routes_bwd[0]], axis=1)
    other_ids = other_core(ids)
    ids_a, ids_b = ids[:, 0:1], ids[:, 1:2]
    other_a, other_b = other_ids[:, 0:1], other_ids[:, 1:2]
    meta_a = jnp.concatenate([ids_a.astype(F32), other_a.astype(F32), gates_fwd[0]], axis=1)
    meta_b = jnp.concatenate([ids_b.astype(F32), other_b.astype(F32), gates_bwd[0]], axis=1)

    sent_a = dispatch(me, ids_a, other_a, x_a, other_core(x_a))
    sent_x = dispatch(me, ids_b, other_b, x_b, other_core(x_b))
    sent_g = dispatch(me, ids_b, other_b, g_b, other_core(g_b))
    got_a = [lax.ppermute(m, "expert", near(s)) for s, m in enumerate(sent_a)]
    got_x = [lax.ppermute(m, "expert", near(s)) for s, m in enumerate(sent_x)]
    got_g = [lax.ppermute(m, "expert", near(s)) for s, m in enumerate(sent_g)]

    base_a = to_section(x_a, 1, same)
    base_b = to_section(g_b, -1, same)
    meta_a = to_section(meta_a, 1, same)
    meta_b = to_section(meta_b, -1, same)

    rows_a = gather(got_a)
    rows_x = gather(got_x)
    rows_g = gather(got_g)

    outs = [shape(ROWS, D)] * 4
    parts_a = call(forward_kernel, outs, 7, "expert_fwd", flops=6 * 384 * D * HID)(
        *rows_a, gate, up, down
    )
    pre = call(
        before_kernel, [shape(384, HID, kind=F32)] * 2, 6, "expert_pre", flops=4 * 384 * D * HID
    )(*rows_x, gate, up)
    parts_b = call(backward_kernel, outs, 9, "expert_bwd", flops=6 * 384 * D * HID)(
        *rows_g, *pre, gate, up, down
    )
    back_a = give_back(parts_a, 1)
    back_b = give_back(parts_b, -1)
    fwd_next = finish(me, back_a, base_a, meta_a)
    bwd_next = finish(me, back_b, base_b, meta_b)
    return fwd_next[None], bwd_next[None]


def solution(mesh):
    rows, cols = P("pipe", "expert", None), P("pipe", None, "expert")
    in_specs = (rows,) * 7 + (cols, cols, rows)
    return jax.shard_map(
        body, mesh=mesh, in_specs=in_specs, out_specs=(rows, rows), check_vma=False
    )
```

time: 505 us -> 189 us (0.37)
  waiting for transfers between devices: 366 us -> 51.3 us
  starting transfers between devices: 48.1 us -> 111 us
  local copies, waits for them, and re-layouts: 39.9 us -> 4.18 us
  matrix products: 34.2 us -> 0 us
  Pallas kernels: 0 us -> 17.4 us
  other arithmetic: 10.5 us -> 3.06 us
    all_to_all x5 -> x0, waiting for transfers between devices: 357 us -> none  [the longest x1 84.3 us: body(): lax.all_to_all(send_g, 'expert', split_axis=0, concat_axis=0, tiled=True)]
    ppermute x2 -> x45, starting transfers between devices: 8.28 us -> 111 us  [the longest x12 57.9 us: to_section(): return lax.ppermute(block, ('pipe', 'expert'), route)]
    ppermute x2 -> x45, waiting for transfers between devices: 8.93 us -> 51.3 us  [the longest x4 19.1 us: body(): got_a = [lax.ppermute(m, 'expert', near(s)) for s, m in enumerate(sent_a)]]
    all_to_all x5 -> x0, starting transfers between devices: 39.8 us -> none  [the longest x1 11.2 us: body(): lax.all_to_all(send_a, 'expert', split_axis=0, concat_axis=0, tiled=True)]
    dot_general x11 -> x0, matrix products: 34.2 us -> none  [the longest x1 7.81 us: backward_rows(): lax.dot_general(gate_grad, gate_cols, contract, preferred_element_type=jn...]
    reshape x10 -> x0, local copies, waits for them, and re-layouts: 30.3 us -> none  [the longest x1 5.38 us: backward_rows(): rows_x = received_x.reshape(-1, in_shape[-1])]
    pallas_call x0 -> x17, Pallas kernels: none -> 17.4 us  [the longest x1 4.43 us: body(): call(backward_kernel, outs, 9, 'expert_bwd', flops=6 * 384 * D * HID)]
    reduce_sum x4 -> x0, other arithmetic: 9.39 us -> none  [the longest x2 8.24 us: combine_rows(): jnp.sum(returned.astype(jnp.float32).reshape(experts, HSPLIT, capacity, w...]
  transfers between devices with their start and end apart: 7 -> 45, of which waited for: 6 -> 10; matrix products, arithmetic and copies ran while one was open for 14% -> 3% of each run, Pallas kernels for 0% -> 9%
where the time goes in v2:
time: 189 us; the launch traced here: 188 us
  starting transfers between devices  111 us (59%)
  waiting for transfers between devices  51.3 us (27%)
  Pallas kernels  17.4 us (9%)
  local copies, waits for them, and re-layouts  4.18 us (2%)
  other arithmetic  3.06 us (2%)
    ppermute x12, starting transfers between devices, to_section(): return lax.ppermute(block, ('pipe', 'expert'), route)  57.9 us
    ppermute x4, waiting for transfers between devices, body(): got_a = [lax.ppermute(m, 'expert', near(s)) for s, m in enumerate(sent_a)]  19.1 us
    ppermute x5, waiting for transfers between devices, other_chip(): return lax.ppermute(block, 'expert', pairs)  18.8 us
    ppermute x4, starting transfers between devices, body(): got_x = [lax.ppermute(m, 'expert', near(s)) for s, m in enumerate(sent_x)]  14.2 us
    ppermute x4, starting transfers between devices, body(): got_a = [lax.ppermute(m, 'expert', near(s)) for s, m in enumerate(sent_a)]  13.9 us
    ppermute x4, starting transfers between devices, body(): got_g = [lax.ppermute(m, 'expert', near(s)) for s, m in enumerate(sent_g)]  12.4 us
    ppermute x12, waiting for transfers between devices, to_section(): return lax.ppermute(block, ('pipe', 'expert'), route)  9.66 us
    ppermute x5, starting transfers between devices, other_chip(): return lax.ppermute(block, 'expert', pairs)  6.79 us
  transfers between devices with their start and end apart: 45, of which 10 were waited for; matrix products, arithmetic and copies ran while one was open for 3% of the time, Pallas kernels for 9%

profile of v2, /device:TPU:9, one launch (start us, length us, event | category | flops | bytes accessed | tf_op | source)
XLA Modules:
  0.0 187.9 jit_solution(15892274611411536751)
XLA Ops:
  6.3 4.2 %collective-permute-start.30 = (bf16[48,1792]{1,0:T(8,128)(2,1)S(1)}, bf16[48,1792]{1,0:T(8,128)(2,1)S(1)}, u32[]{:S(2)}, u32[]{:S(2)}) collective-permute-start(bf16[48,1792]{1,0:T(8,128)(2,1)S(1)} %get-tuple-element.54), channel_id=1, source_target_pairs={{0,0},{1,16},{2,2},{3,18},{4,4},{5,20},{6,6},{7,22},{8,8},{9,24},{... | collective-permute-start | bytes 516104 | tf_op jit(solution)/shard_map/ppermute | solution.py:266
  10.5 3.8 %collective-permute-start.31 = (bf16[48,1792]{1,0:T(8,128)(2,1)S(1)}, bf16[48,1792]{1,0:T(8,128)(2,1)S(1)}, u32[]{:S(2)}, u32[]{:S(2)}) collective-permute-start(bf16[48,1792]{1,0:T(8,128)(2,1)S(1)} %get-tuple-element.55), channel_id=1, source_target_pairs={{0,4},{1,20},{2,14},{3,30},{4,8},{5,24},{6,2},{7,18},{8,12},{9,28}... | collective-permute-start | bytes 516104 | tf_op jit(solution)/shard_map/ppermute | solution.py:266
  14.3 5.8 %collective-permute-start.32 = (bf16[48,1792]{1,0:T(8,128)(2,1)S(1)}, bf16[48,1792]{1,0:T(8,128)(2,1)S(1)}, u32[]{:S(2)}, u32[]{:S(2)}) collective-permute-start(bf16[48,1792]{1,0:T(8,128)(2,1)S(1)} %get-tuple-element.56), channel_id=1, source_target_pairs={{0,14},{1,30},{2,4},{3,20},{4,2},{5,18},{6,8},{7,24},{8,6},{9,22},... | collective-permute-start | bytes 516104 | tf_op jit(solution)/shard_map/ppermute | solution.py:266
  22.7 2.9 %collective-permute-start.22 = (bf16[48,1792]{1,0:T(8,128)(2,1)}, bf16[48,1792]{1,0:T(8,128)(2,1)S(1)}, u32[]{:S(2)}, u32[]{:S(2)}) collective-permute-start(bf16[48,1792]{1,0:T(8,128)(2,1)} %get-tuple-element.50), channel_id=1, source_target_pairs={{0,0},{1,16},{2,2},{3,18},{4,4},{5,20},{6,6},{7,22},{8,8},{9,24},{... | collective-permute-start | bytes 516104 | tf_op jit(solution)/shard_map/ppermute | solution.py:267
  25.6 3.6 %collective-permute-start.23 = (bf16[48,1792]{1,0:T(8,128)(2,1)S(1)}, bf16[48,1792]{1,0:T(8,128)(2,1)S(1)}, u32[]{:S(2)}, u32[]{:S(2)}) collective-permute-start(bf16[48,1792]{1,0:T(8,128)(2,1)S(1)} %get-tuple-element.51), channel_id=1, source_target_pairs={{0,4},{1,20},{2,14},{3,30},{4,8},{5,24},{6,2},{7,18},{8,12},{9,28}... | collective-permute-start | bytes 516104 | tf_op jit(solution)/shard_map/ppermute | solution.py:267
  29.2 5.4 %collective-permute-start.24 = (bf16[48,1792]{1,0:T(8,128)(2,1)S(1)}, bf16[48,1792]{1,0:T(8,128)(2,1)S(1)}, u32[]{:S(2)}, u32[]{:S(2)}) collective-permute-start(bf16[48,1792]{1,0:T(8,128)(2,1)S(1)} %get-tuple-element.52), channel_id=1, source_target_pairs={{0,14},{1,30},{2,4},{3,20},{4,2},{5,18},{6,8},{7,24},{8,6},{9,22},... | collective-permute-start | bytes 516104 | tf_op jit(solution)/shard_map/ppermute | solution.py:267
  35.7 4.5 %collective-permute-start.4 = (bf16[48,1792]{1,0:T(8,128)(2,1)S(1)}, bf16[48,1792]{1,0:T(8,128)(2,1)S(1)}, u32[]{:S(2)}, u32[]{:S(2)}) collective-permute-start(bf16[48,1792]{1,0:T(8,128)(2,1)S(1)} %get-tuple-element.36), channel_id=1, source_target_pairs={{0,0},{1,16},{2,2},{3,18},{4,4},{5,20},{6,6},{7,22},{8,8},{9,24},{... | collective-permute-start | bytes 516104 | tf_op jit(solution)/shard_map/ppermute | solution.py:265
  40.3 2.8 %collective-permute-start.35 = (bf16[96,3584]{1,0:T(8,128)(2,1)S(1)}, bf16[96,3584]{1,0:T(8,128)(2,1)S(1)}, u32[]{:S(2)}, u32[]{:S(2)}) collective-permute-start(bf16[96,3584]{1,0:T(8,128)(2,1)S(1)} %join.5.x0), channel_id=1, source_target_pairs={{0,2},{1,3},{2,0},{3,1},{4,6},{5,7},{6,4},{7,5},{8,10},{9,11},{10,... | collective-permute-start | bytes 2064392 | tf_op jit(solution)/shard_map/ppermute | solution.py:54
  43.1 2.2 %collective-permute-done.25.refs_3_ = bf16[48,1792]{1,0:T(8,128)(2,1)S(1)} collective-permute-done((bf16[48,1792]{1,0:T(8,128)(2,1)S(1)}, bf16[48,1792]{1,0:T(8,128)(2,1)S(1)}, u32[]{:S(2)}, u32[]{:S(2)}) %collective-permute-start.25) | collective-permute-done | bytes 172064 | tf_op jit(solution)/shard_map/ppermute | solution.py:267
  45.4 2.5 %collective-permute-start.27 = (bf16[96,3584]{1,0:T(8,128)(2,1)S(1)}, bf16[96,3584]{1,0:T(8,128)(2,1)S(1)}, u32[]{:S(2)}, u32[]{:S(2)}) collective-permute-start(bf16[96,3584]{1,0:T(8,128)(2,1)S(1)} %join.4.g0), channel_id=1, source_target_pairs={{0,2},{1,3},{2,0},{3,1},{4,6},{5,7},{6,4},{7,5},{8,10},{9,11},{10,... | collective-permute-start | bytes 2064392 | tf_op jit(solution)/shard_map/ppermute | solution.py:54
  49.4 4.1 %collective-permute-start.6 = (bf16[48,1792]{1,0:T(8,128)(2,1)S(1)}, bf16[48,1792]{1,0:T(8,128)(2,1)S(1)}, u32[]{:S(2)}, u32[]{:S(2)}) collective-permute-start(bf16[48,1792]{1,0:T(8,128)(2,1)S(1)} %get-tuple-element.38), channel_id=1, source_target_pairs={{0,14},{1,30},{2,4},{3,20},{4,2},{5,18},{6,8},{7,24},{8,6},{9,22},... | collective-permute-start | bytes 516104 | tf_op jit(solution)/shard_map/ppermute | solution.py:265
  53.5 3.7 %collective-permute-start.7 = (bf16[48,1792]{1,0:T(8,128)(2,1)S(1)}, bf16[48,1792]{1,0:T(8,128)(2,1)S(1)}, u32[]{:S(2)}, u32[]{:S(2)}) collective-permute-start(bf16[48,1792]{1,0:T(8,128)(2,1)S(1)} %get-tuple-element.39), channel_id=1, source_target_pairs={{0,10},{1,26},{2,8},{3,24},{4,14},{5,30},{6,12},{7,28},{8,2},{9,18... | collective-permute-start | bytes 516104 | tf_op jit(solution)/shard_map/ppermute | solution.py:265
  57.2 19.1 %collective-permute-done.5.refs_1_ = bf16[48,1792]{1,0:T(8,128)(2,1)S(1)} collective-permute-done((bf16[48,1792]{1,0:T(8,128)(2,1)S(1)}, bf16[48,1792]{1,0:T(8,128)(2,1)S(1)}, u32[]{:S(2)}, u32[]{:S(2)}) %collective-permute-start.5) | collective-permute-done | bytes 172064 | tf_op jit(solution)/shard_map/ppermute | solution.py:265
  78.6 14.4 %collective-permute-done.9.x2 = bf16[96,3584]{1,0:T(8,128)(2,1)S(1)} collective-permute-done((bf16[96,3584]{1,0:T(8,128)(2,1)S(1)}, bf16[96,3584]{1,0:T(8,128)(2,1)S(1)}, u32[]{:S(2)}, u32[]{:S(2)}) %collective-permute-start.9) | collective-permute-done | bytes 688160 | tf_op jit(solution)/shard_map/ppermute | solution.py:54
  96.0 4.4 %expert_bwd.1 = (bf16[96,3584]{1,0:T(8,128)(2,1)S(1)}, bf16[96,3584]{1,0:T(8,128)(2,1)}, bf16[96,3584]{1,0:T(8,128)(2,1)S(1)}, bf16[96,3584]{1,0:T(8,128)(2,1)S(1)}) custom-call(bf16[96,3584]{1,0:T(8,128)(2,1)S(1)} %join.4.g0, bf16[96,3584]{1,0:T(8,128)(2,1)S(1)} %collective-permute-done.26.g1, bf16[96,3584]{1,0:T(8,128)(2,1)S(1)} %collective-permute-done.27.g2, ...), custom_call_target="tpu_custom_call" | custom-call | flops 2113929216 | bytes 4000000 | tf_op jit(solution)/shard_map/expert_bwd/pallas_call | solution.py:285
  100.4 3.2 %expert_fwd.1 = (bf16[96,3584]{1,0:T(8,128)(2,1)S(1)}, bf16[96,3584]{1,0:T(8,128)(2,1)}, bf16[96,3584]{1,0:T(8,128)(2,1)S(1)}, bf16[96,3584]{1,0:T(8,128)(2,1)S(1)}) custom-call(bf16[96,3584]{1,0:T(8,128)(2,1)S(1)} %join.3.x0, bf16[96,3584]{1,0:T(8,128)(2,1)S(1)} %collective-permute-done.8.x1, bf16[96,3584]{1,0:T(8,128)(2,1)S(1)} %collective-permute-done.9.x2, ...), custom_call_target="tpu_custom_call" | custom-call | flops 2113929216 | bytes 4000000 | tf_op jit(solution)/shard_map/expert_fwd/pallas_call | solution.py:279
  109.5 5.3 %collective-permute-start.20 = (f32[64,3]{1,0:T(8,128)S(1)}, f32[64,3]{1,0:T(8,128)S(1)}, u32[]{:S(2)}, u32[]{:S(2)}) collective-permute-start(f32[64,3]{1,0:T(8,128)S(1)} %pad_maximum_fusion.1), channel_id=1, source_target_pairs={{32,0},{33,1},{34,2},{35,3},{36,4},{37,5},{38,6},{39,7},{40,8},{41... | collective-permute-start | bytes 2312 | tf_op jit(solution)/shard_map/ppermute | solution.py:65
  115.7 1.9 %collective-permute-start.2 = (f32[64,3]{1,0:T(8,128)S(1)}, f32[64,3]{1,0:T(8,128)S(1)}, u32[]{:S(2)}, u32[]{:S(2)}) collective-permute-start(f32[64,3]{1,0:T(8,128)S(1)} %pad_maximum_fusion), channel_id=1, source_target_pairs={{0,32},{1,33},{2,34},{3,35},{4,36},{5,37},{6,38},{7,39},{8,40},{9,... | collective-permute-start | bytes 2312 | tf_op jit(solution)/shard_map/ppermute | solution.py:65
  117.6 4.4 %collective-permute-done.39.c = bf16[96,3584]{1,0:T(8,128)(2,1)} collective-permute-done((bf16[96,3584]{1,0:T(8,128)(2,1)}, bf16[96,3584]{1,0:T(8,128)(2,1)}, u32[]{:S(2)}, u32[]{:S(2)}) %collective-permute-start.39) | collective-permute-done | bytes 688160 | tf_op jit(solution)/shard_map/ppermute | solution.py:54
  123.6 8.3 %collective-permute-start.40 = (bf16[48,1792]{1,0:T(8,128)(2,1)S(1)}, bf16[48,1792]{1,0:T(8,128)(2,1)S(1)}, u32[]{:S(2)}, u32[]{:S(2)}) collective-permute-start(bf16[48,1792]{1,0:T(8,128)(2,1)S(1)} %get-tuple-element.64), channel_id=1, source_target_pairs={{32,0},{48,1},{34,2},{50,3},{36,4},{52,5},{38,6},{54,7},{40,8},{56... | collective-permute-start | bytes 516104 | tf_op jit(solution)/shard_map/ppermute | solution.py:65
  132.0 3.6 %collective-permute-start.41 = (bf16[48,1792]{1,0:T(8,128)(2,1)S(1)}, bf16[48,1792]{1,0:T(8,128)(2,1)S(1)}, u32[]{:S(2)}, u32[]{:S(2)}) collective-permute-start(bf16[48,1792]{1,0:T(8,128)(2,1)S(1)} %get-tuple-element.65), channel_id=1, source_target_pairs={{36,0},{52,1},{46,2},{62,3},{40,4},{56,5},{34,6},{50,7},{44,8},{60... | collective-permute-start | bytes 516104 | tf_op jit(solution)/shard_map/ppermute | solution.py:65
  135.6 5.5 %collective-permute-start.42 = (bf16[48,1792]{1,0:T(8,128)(2,1)S(1)}, bf16[48,1792]{1,0:T(8,128)(2,1)S(1)}, u32[]{:S(2)}, u32[]{:S(2)}) collective-permute-start(bf16[48,1792]{1,0:T(8,128)(2,1)S(1)} %get-tuple-element.66), channel_id=1, source_target_pairs={{46,0},{62,1},{36,2},{52,3},{34,4},{50,5},{40,6},{56,7},{38,8},{54... | collective-permute-start | bytes 516104 | tf_op jit(solution)/shard_map/ppermute | solution.py:65
  141.2 8.3 %collective-permute-start.43 = (bf16[48,1792]{1,0:T(8,128)(2,1)S(1)}, bf16[48,1792]{1,0:T(8,128)(2,1)S(1)}, u32[]{:S(2)}, u32[]{:S(2)}) collective-permute-start(bf16[48,1792]{1,0:T(8,128)(2,1)S(1)} %get-tuple-element.67), channel_id=1, source_target_pairs={{42,0},{58,1},{40,2},{56,3},{46,4},{62,5},{44,6},{60,7},{34,8},{50... | collective-permute-start | bytes 516104 | tf_op jit(solution)/shard_map/ppermute | solution.py:65
  149.9 1.9 %collective-permute-start.14 = (bf16[48,1792]{1,0:T(8,128)(2,1)S(1)}, bf16[48,1792]{1,0:T(8,128)(2,1)S(1)}, u32[]{:S(2)}, u32[]{:S(2)}) collective-permute-start(bf16[48,1792]{1,0:T(8,128)(2,1)S(1)} %get-tuple-element.44), channel_id=1, source_target_pairs={{0,32},{16,33},{2,34},{18,35},{4,36},{20,37},{6,38},{22,39},{8,40}... | collective-permute-start | bytes 516104 | tf_op jit(solution)/shard_map/ppermute | solution.py:65
  151.8 7.6 %collective-permute-start.15 = (bf16[48,1792]{1,0:T(8,128)(2,1)S(1)}, bf16[48,1792]{1,0:T(8,128)(2,1)S(1)}, u32[]{:S(2)}, u32[]{:S(2)}) collective-permute-start(bf16[48,1792]{1,0:T(8,128)(2,1)S(1)} %get-tuple-element.45), channel_id=1, source_target_pairs={{4,32},{20,33},{14,34},{30,35},{8,36},{24,37},{2,38},{18,39},{12,4... | collective-permute-start | bytes 516104 | tf_op jit(solution)/shard_map/ppermute | solution.py:65
  159.4 4.0 %collective-permute-start.16 = (bf16[48,1792]{1,0:T(8,128)(2,1)S(1)}, bf16[48,1792]{1,0:T(8,128)(2,1)S(1)}, u32[]{:S(2)}, u32[]{:S(2)}) collective-permute-start(bf16[48,1792]{1,0:T(8,128)(2,1)S(1)} %get-tuple-element.46), channel_id=1, source_target_pairs={{14,32},{30,33},{4,34},{20,35},{2,36},{18,37},{8,38},{24,39},{6,40... | collective-permute-start | bytes 516104 | tf_op jit(solution)/shard_map/ppermute | solution.py:65
  163.5 1.9 %collective-permute-start.17 = (bf16[48,1792]{1,0:T(8,128)(2,1)S(1)}, bf16[48,1792]{1,0:T(8,128)(2,1)S(1)}, u32[]{:S(2)}, u32[]{:S(2)}) collective-permute-start(bf16[48,1792]{1,0:T(8,128)(2,1)S(1)} %get-tuple-element.47), channel_id=1, source_target_pairs={{10,32},{26,33},{8,34},{24,35},{14,36},{30,37},{12,38},{28,39},{2,... | collective-permute-start | bytes 516104 | tf_op jit(solution)/shard_map/ppermute | solution.py:65
  165.5 7.5 %collective-permute-start.19 = (bf16[64,3584]{1,0:T(8,128)(2,1)S(1)}, bf16[64,3584]{1,0:T(8,128)(2,1)S(1)}, u32[]{:S(2)}, u32[]{:S(2)}) collective-permute-start(bf16[64,3584]{1,0:T(8,128)(2,1)S(1)} %bitcast.27), channel_id=1, source_target_pairs={{32,0},{33,1},{34,2},{35,3},{36,4},{37,5},{38,6},{39,7},{40,8},{41... | collective-permute-start | bytes 1376264 | tf_op jit(solution)/shard_map/ppermute | solution.py:65
  173.6 1.9 %collective-permute-start = (bf16[64,3584]{1,0:T(8,128)(2,1)S(1)}, bf16[64,3584]{1,0:T(8,128)(2,1)S(1)}, u32[]{:S(2)}, u32[]{:S(2)}) collective-permute-start(bf16[64,3584]{1,0:T(8,128)(2,1)S(1)} %bitcast.30), channel_id=1, source_target_pairs={{0,32},{1,33},{2,34},{3,35},{4,36},{5,37},{6,38},{7,39},{8,40},{9,... | collective-permute-start | bytes 1376264 | tf_op jit(solution)/shard_map/ppermute | solution.py:65
  175.7 1.7 collective-permute-done.17.m3
  178.0 1.8 collective-permute-done.19.base
  180.8 6.2 %collective-permute-done.base = bf16[64,3584]{1,0:T(8,128)(2,1)S(1)} collective-permute-done((bf16[64,3584]{1,0:T(8,128)(2,1)S(1)}, bf16[64,3584]{1,0:T(8,128)(2,1)S(1)}, u32[]{:S(2)}, u32[]{:S(2)}) %collective-permute-start) | collective-permute-done | bytes 458784 | tf_op jit(solution)/shard_map/ppermute | solution.py:65
  (114 shorter events, 28.4 us)
Async XLA Ops:
  1.4 18.6 %collective-permute-start.21 = (bf16[64,3584]{1,0:T(8,128)(2,1)}, bf16[64,3584]{1,0:T(8,128)(2,1)S(1)}, u32[]{:S(2)}, u32[]{:S(2)}) collective-permute-start(bf16[64,3584]{1,0:T(8,128)(2,1)} %bitcast.25), channel_id=1, source_target_pairs={{0,1},{1,0},{2,3},{3,2},{4,5},{5,4},{6,7},{7,6},{8,9},{9,8},{10,11... | collective-permute-start | bytes 1376264 | tf_op jit(solution)/shard_map/ppermute | solution.py:49
  1.5 21.2 %collective-permute-start.3 = (bf16[64,3584]{1,0:T(8,128)(2,1)}, bf16[64,3584]{1,0:T(8,128)(2,1)S(1)}, u32[]{:S(2)}, u32[]{:S(2)}) collective-permute-start(bf16[64,3584]{1,0:T(8,128)(2,1)} %bitcast.28), channel_id=1, source_target_pairs={{0,1},{1,0},{2,3},{3,2},{4,5},{5,4},{6,7},{7,6},{8,9},{9,8},{10,11... | collective-permute-start | bytes 1376264 | tf_op jit(solution)/shard_map/ppermute | solution.py:49
  6.3 19.2 %collective-permute-start.30 = (bf16[48,1792]{1,0:T(8,128)(2,1)S(1)}, bf16[48,1792]{1,0:T(8,128)(2,1)S(1)}, u32[]{:S(2)}, u32[]{:S(2)}) collective-permute-start(bf16[48,1792]{1,0:T(8,128)(2,1)S(1)} %get-tuple-element.54), channel_id=1, source_target_pairs={{0,0},{1,16},{2,2},{3,18},{4,4},{5,20},{6,6},{7,22},{8,8},{9,24},{... | collective-permute-start | bytes 516104 | tf_op jit(solution)/shard_map/ppermute | solution.py:266
  10.5 18.7 %collective-permute-start.31 = (bf16[48,1792]{1,0:T(8,128)(2,1)S(1)}, bf16[48,1792]{1,0:T(8,128)(2,1)S(1)}, u32[]{:S(2)}, u32[]{:S(2)}) collective-permute-start(bf16[48,1792]{1,0:T(8,128)(2,1)S(1)} %get-tuple-element.55), channel_id=1, source_target_pairs={{0,4},{1,20},{2,14},{3,30},{4,8},{5,24},{6,2},{7,18},{8,12},{9,28}... | collective-permute-start | bytes 516104 | tf_op jit(solution)/shard_map/ppermute | solution.py:266
  14.3 20.3 %collective-permute-start.32 = (bf16[48,1792]{1,0:T(8,128)(2,1)S(1)}, bf16[48,1792]{1,0:T(8,128)(2,1)S(1)}, u32[]{:S(2)}, u32[]{:S(2)}) collective-permute-start(bf16[48,1792]{1,0:T(8,128)(2,1)S(1)} %get-tuple-element.56), channel_id=1, source_target_pairs={{0,14},{1,30},{2,4},{3,20},{4,2},{5,18},{6,8},{7,24},{8,6},{9,22},... | collective-permute-start | bytes 516104 | tf_op jit(solution)/shard_map/ppermute | solution.py:266
  20.0 15.6 %collective-permute-start.33 = (bf16[48,1792]{1,0:T(8,128)(2,1)S(1)}, bf16[48,1792]{1,0:T(8,128)(2,1)S(1)}, u32[]{:S(2)}, u32[]{:S(2)}) collective-permute-start(bf16[48,1792]{1,0:T(8,128)(2,1)S(1)} %get-tuple-element.57), channel_id=1, source_target_pairs={{0,10},{1,26},{2,8},{3,24},{4,14},{5,30},{6,12},{7,28},{8,2},{9,18... | collective-permute-start | bytes 516104 | tf_op jit(solution)/shard_map/ppermute | solution.py:266
  22.7 17.6 %collective-permute-start.22 = (bf16[48,1792]{1,0:T(8,128)(2,1)}, bf16[48,1792]{1,0:T(8,128)(2,1)S(1)}, u32[]{:S(2)}, u32[]{:S(2)}) collective-permute-start(bf16[48,1792]{1,0:T(8,128)(2,1)} %get-tuple-element.50), channel_id=1, source_target_pairs={{0,0},{1,16},{2,2},{3,18},{4,4},{5,20},{6,6},{7,22},{8,8},{9,24},{... | collective-permute-start | bytes 516104 | tf_op jit(solution)/shard_map/ppermute | solution.py:267
  25.6 17.5 %collective-permute-start.23 = (bf16[48,1792]{1,0:T(8,128)(2,1)S(1)}, bf16[48,1792]{1,0:T(8,128)(2,1)S(1)}, u32[]{:S(2)}, u32[]{:S(2)}) collective-permute-start(bf16[48,1792]{1,0:T(8,128)(2,1)S(1)} %get-tuple-element.51), channel_id=1, source_target_pairs={{0,4},{1,20},{2,14},{3,30},{4,8},{5,24},{6,2},{7,18},{8,12},{9,28}... | collective-permute-start | bytes 516104 | tf_op jit(solution)/shard_map/ppermute | solution.py:267
  35.7 17.8 %collective-permute-start.4 = (bf16[48,1792]{1,0:T(8,128)(2,1)S(1)}, bf16[48,1792]{1,0:T(8,128)(2,1)S(1)}, u32[]{:S(2)}, u32[]{:S(2)}) collective-permute-start(bf16[48,1792]{1,0:T(8,128)(2,1)S(1)} %get-tuple-element.36), channel_id=1, source_target_pairs={{0,0},{1,16},{2,2},{3,18},{4,4},{5,20},{6,6},{7,22},{8,8},{9,24},{... | collective-permute-start | bytes 516104 | tf_op jit(solution)/shard_map/ppermute | solution.py:265
  40.3 36.6 %collective-permute-start.35 = (bf16[96,3584]{1,0:T(8,128)(2,1)S(1)}, bf16[96,3584]{1,0:T(8,128)(2,1)S(1)}, u32[]{:S(2)}, u32[]{:S(2)}) collective-permute-start(bf16[96,3584]{1,0:T(8,128)(2,1)S(1)} %join.5.x0), channel_id=1, source_target_pairs={{0,2},{1,3},{2,0},{3,1},{4,6},{5,7},{6,4},{7,5},{8,10},{9,11},{10,... | collective-permute-start | bytes 2064392 | tf_op jit(solution)/shard_map/ppermute | solution.py:54
  45.4 32.3 %collective-permute-start.27 = (bf16[96,3584]{1,0:T(8,128)(2,1)S(1)}, bf16[96,3584]{1,0:T(8,128)(2,1)S(1)}, u32[]{:S(2)}, u32[]{:S(2)}) collective-permute-start(bf16[96,3584]{1,0:T(8,128)(2,1)S(1)} %join.4.g0), channel_id=1, source_target_pairs={{0,2},{1,3},{2,0},{3,1},{4,6},{5,7},{6,4},{7,5},{8,10},{9,11},{10,... | collective-permute-start | bytes 2064392 | tf_op jit(solution)/shard_map/ppermute | solution.py:54
  47.9 28.4 %collective-permute-start.5 = (bf16[48,1792]{1,0:T(8,128)(2,1)S(1)}, bf16[48,1792]{1,0:T(8,128)(2,1)S(1)}, u32[]{:S(2)}, u32[]{:S(2)}) collective-permute-start(bf16[48,1792]{1,0:T(8,128)(2,1)S(1)} %get-tuple-element.37), channel_id=1, source_target_pairs={{0,4},{1,20},{2,14},{3,30},{4,8},{5,24},{6,2},{7,18},{8,12},{9,28}... | collective-permute-start | bytes 516104 | tf_op jit(solution)/shard_map/ppermute | solution.py:265
  49.4 26.9 %collective-permute-start.6 = (bf16[48,1792]{1,0:T(8,128)(2,1)S(1)}, bf16[48,1792]{1,0:T(8,128)(2,1)S(1)}, u32[]{:S(2)}, u32[]{:S(2)}) collective-permute-start(bf16[48,1792]{1,0:T(8,128)(2,1)S(1)} %get-tuple-element.38), channel_id=1, source_target_pairs={{0,14},{1,30},{2,4},{3,20},{4,2},{5,18},{6,8},{7,24},{8,6},{9,22},... | collective-permute-start | bytes 516104 | tf_op jit(solution)/shard_map/ppermute | solution.py:265
  53.5 22.8 %collective-permute-start.7 = (bf16[48,1792]{1,0:T(8,128)(2,1)S(1)}, bf16[48,1792]{1,0:T(8,128)(2,1)S(1)}, u32[]{:S(2)}, u32[]{:S(2)}) collective-permute-start(bf16[48,1792]{1,0:T(8,128)(2,1)S(1)} %get-tuple-element.39), channel_id=1, source_target_pairs={{0,10},{1,26},{2,8},{3,24},{4,14},{5,30},{6,12},{7,28},{8,2},{9,18... | collective-permute-start | bytes 516104 | tf_op jit(solution)/shard_map/ppermute | solution.py:265
  76.4 16.6 %collective-permute-start.9 = (bf16[96,3584]{1,0:T(8,128)(2,1)S(1)}, bf16[96,3584]{1,0:T(8,128)(2,1)S(1)}, u32[]{:S(2)}, u32[]{:S(2)}) collective-permute-start(bf16[96,3584]{1,0:T(8,128)(2,1)S(1)} %join.3.x0), channel_id=1, source_target_pairs={{0,2},{1,3},{2,0},{3,1},{4,6},{5,7},{6,4},{7,5},{8,10},{9,11},{10,... | collective-permute-start | bytes 2064392 | tf_op jit(solution)/shard_map/ppermute | solution.py:54
  76.9 17.5 %collective-permute-start.36 = (bf16[96,3584]{1,0:T(8,128)(2,1)S(1)}, bf16[96,3584]{1,0:T(8,128)(2,1)S(1)}, u32[]{:S(2)}, u32[]{:S(2)}) collective-permute-start(bf16[96,3584]{1,0:T(8,128)(2,1)S(1)} %collective-permute-done.35.x2), channel_id=1, source_target_pairs={{0,1},{1,0},{2,3},{3,2},{4,5},{5,4},{6,7},{7,6},{8,9},{9,8},{10,11... | collective-permute-start | bytes 2064392 | tf_op jit(solution)/shard_map/ppermute | solution.py:49
  77.6 18.3 %collective-permute-start.26 = (bf16[96,3584]{1,0:T(8,128)(2,1)S(1)}, bf16[96,3584]{1,0:T(8,128)(2,1)S(1)}, u32[]{:S(2)}, u32[]{:S(2)}) collective-permute-start(bf16[96,3584]{1,0:T(8,128)(2,1)S(1)} %join.4.g0), channel_id=1, source_target_pairs={{0,1},{1,0},{2,3},{3,2},{4,5},{5,4},{6,7},{7,6},{8,9},{9,8},{10,11... | collective-permute-start | bytes 2064392 | tf_op jit(solution)/shard_map/ppermute | solution.py:49
  77.7 18.3 %collective-permute-start.28 = (bf16[96,3584]{1,0:T(8,128)(2,1)S(1)}, bf16[96,3584]{1,0:T(8,128)(2,1)S(1)}, u32[]{:S(2)}, u32[]{:S(2)}) collective-permute-start(bf16[96,3584]{1,0:T(8,128)(2,1)S(1)} %collective-permute-done.27.g2), channel_id=1, source_target_pairs={{0,1},{1,0},{2,3},{3,2},{4,5},{5,4},{6,7},{7,6},{8,9},{9,8},{10,11... | collective-permute-start | bytes 2064392 | tf_op jit(solution)/shard_map/ppermute | solution.py:49
  78.5 21.9 %collective-permute-start.8 = (bf16[96,3584]{1,0:T(8,128)(2,1)S(1)}, bf16[96,3584]{1,0:T(8,128)(2,1)S(1)}, u32[]{:S(2)}, u32[]{:S(2)}) collective-permute-start(bf16[96,3584]{1,0:T(8,128)(2,1)S(1)} %join.3.x0), channel_id=1, source_target_pairs={{0,1},{1,0},{2,3},{3,2},{4,5},{5,4},{6,7},{7,6},{8,9},{9,8},{10,11... | collective-permute-start | bytes 2064392 | tf_op jit(solution)/shard_map/ppermute | solution.py:49
  105.2 16.8 %collective-permute-start.39 = (bf16[96,3584]{1,0:T(8,128)(2,1)}, bf16[96,3584]{1,0:T(8,128)(2,1)}, u32[]{:S(2)}, u32[]{:S(2)}) collective-permute-start(bf16[96,3584]{1,0:T(8,128)(2,1)} %chip_sum.3), channel_id=1, source_target_pairs={{0,2},{1,3},{2,0},{3,1},{4,6},{5,7},{6,4},{7,5},{8,10},{9,11},{10,... | collective-permute-start | bytes 2064392 | tf_op jit(solution)/shard_map/ppermute | solution.py:54
  105.5 30.1 %collective-permute-start.11 = (bf16[96,3584]{1,0:T(8,128)(2,1)}, bf16[96,3584]{1,0:T(8,128)(2,1)S(1)}, u32[]{:S(2)}, u32[]{:S(2)}) collective-permute-start(bf16[96,3584]{1,0:T(8,128)(2,1)} %get-tuple-element.41), channel_id=1, source_target_pairs={{0,1},{1,0},{2,3},{3,2},{4,5},{5,4},{6,7},{7,6},{8,9},{9,8},{10,11... | collective-permute-start | bytes 2064392 | tf_op jit(solution)/shard_map/ppermute | solution.py:49
  107.0 34.2 %collective-permute-start.13 = (bf16[96,3584]{1,0:T(8,128)(2,1)S(1)}, bf16[96,3584]{1,0:T(8,128)(2,1)S(1)}, u32[]{:S(2)}, u32[]{:S(2)}) collective-permute-start(bf16[96,3584]{1,0:T(8,128)(2,1)S(1)} %chip_sum.2), channel_id=1, source_target_pairs={{0,2},{1,3},{2,0},{3,1},{4,6},{5,7},{6,4},{7,5},{8,10},{9,11},{10,... | collective-permute-start | bytes 2064392 | tf_op jit(solution)/shard_map/ppermute | solution.py:54
  109.5 22.4 %collective-permute-start.20 = (f32[64,3]{1,0:T(8,128)S(1)}, f32[64,3]{1,0:T(8,128)S(1)}, u32[]{:S(2)}, u32[]{:S(2)}) collective-permute-start(f32[64,3]{1,0:T(8,128)S(1)} %pad_maximum_fusion.1), channel_id=1, source_target_pairs={{32,0},{33,1},{34,2},{35,3},{36,4},{37,5},{38,6},{39,7},{40,8},{41... | collective-permute-start | bytes 2312 | tf_op jit(solution)/shard_map/ppermute | solution.py:65
  115.7 34.2 %collective-permute-start.2 = (f32[64,3]{1,0:T(8,128)S(1)}, f32[64,3]{1,0:T(8,128)S(1)}, u32[]{:S(2)}, u32[]{:S(2)}) collective-permute-start(f32[64,3]{1,0:T(8,128)S(1)} %pad_maximum_fusion), channel_id=1, source_target_pairs={{0,32},{1,33},{2,34},{3,35},{4,36},{5,37},{6,38},{7,39},{8,40},{9,... | collective-permute-start | bytes 2312 | tf_op jit(solution)/shard_map/ppermute | solution.py:65
  123.6 28.2 %collective-permute-start.40 = (bf16[48,1792]{1,0:T(8,128)(2,1)S(1)}, bf16[48,1792]{1,0:T(8,128)(2,1)S(1)}, u32[]{:S(2)}, u32[]{:S(2)}) collective-permute-start(bf16[48,1792]{1,0:T(8,128)(2,1)S(1)} %get-tuple-element.64), channel_id=1, source_target_pairs={{32,0},{48,1},{34,2},{50,3},{36,4},{52,5},{38,6},{54,7},{40,8},{56... | collective-permute-start | bytes 516104 | tf_op jit(solution)/shard_map/ppermute | solution.py:65
  132.0 27.4 %collective-permute-start.41 = (bf16[48,1792]{1,0:T(8,128)(2,1)S(1)}, bf16[48,1792]{1,0:T(8,128)(2,1)S(1)}, u32[]{:S(2)}, u32[]{:S(2)}) collective-permute-start(bf16[48,1792]{1,0:T(8,128)(2,1)S(1)} %get-tuple-element.65), channel_id=1, source_target_pairs={{36,0},{52,1},{46,2},{62,3},{40,4},{56,5},{34,6},{50,7},{44,8},{60... | collective-permute-start | bytes 516104 | tf_op jit(solution)/shard_map/ppermute | solution.py:65
  135.6 27.8 %collective-permute-start.42 = (bf16[48,1792]{1,0:T(8,128)(2,1)S(1)}, bf16[48,1792]{1,0:T(8,128)(2,1)S(1)}, u32[]{:S(2)}, u32[]{:S(2)}) collective-permute-start(bf16[48,1792]{1,0:T(8,128)(2,1)S(1)} %get-tuple-element.66), channel_id=1, source_target_pairs={{46,0},{62,1},{36,2},{52,3},{34,4},{50,5},{40,6},{56,7},{38,8},{54... | collective-permute-start | bytes 516104 | tf_op jit(solution)/shard_map/ppermute | solution.py:65
  141.2 24.2 %collective-permute-start.43 = (bf16[48,1792]{1,0:T(8,128)(2,1)S(1)}, bf16[48,1792]{1,0:T(8,128)(2,1)S(1)}, u32[]{:S(2)}, u32[]{:S(2)}) collective-permute-start(bf16[48,1792]{1,0:T(8,128)(2,1)S(1)} %get-tuple-element.67), channel_id=1, source_target_pairs={{42,0},{58,1},{40,2},{56,3},{46,4},{62,5},{44,6},{60,7},{34,8},{50... | collective-permute-start | bytes 516104 | tf_op jit(solution)/shard_map/ppermute | solution.py:65
  149.9 23.7 %collective-permute-start.14 = (bf16[48,1792]{1,0:T(8,128)(2,1)S(1)}, bf16[48,1792]{1,0:T(8,128)(2,1)S(1)}, u32[]{:S(2)}, u32[]{:S(2)}) collective-permute-start(bf16[48,1792]{1,0:T(8,128)(2,1)S(1)} %get-tuple-element.44), channel_id=1, source_target_pairs={{0,32},{16,33},{2,34},{18,35},{4,36},{20,37},{6,38},{22,39},{8,40}... | collective-permute-start | bytes 516104 | tf_op jit(solution)/shard_map/ppermute | solution.py:65
  151.8 23.7 %collective-permute-start.15 = (bf16[48,1792]{1,0:T(8,128)(2,1)S(1)}, bf16[48,1792]{1,0:T(8,128)(2,1)S(1)}, u32[]{:S(2)}, u32[]{:S(2)}) collective-permute-start(bf16[48,1792]{1,0:T(8,128)(2,1)S(1)} %get-tuple-element.45), channel_id=1, source_target_pairs={{4,32},{20,33},{14,34},{30,35},{8,36},{24,37},{2,38},{18,39},{12,4... | collective-permute-start | bytes 516104 | tf_op jit(solution)/shard_map/ppermute | solution.py:65
  159.4 16.3 %collective-permute-start.16 = (bf16[48,1792]{1,0:T(8,128)(2,1)S(1)}, bf16[48,1792]{1,0:T(8,128)(2,1)S(1)}, u32[]{:S(2)}, u32[]{:S(2)}) collective-permute-start(bf16[48,1792]{1,0:T(8,128)(2,1)S(1)} %get-tuple-element.46), channel_id=1, source_target_pairs={{14,32},{30,33},{4,34},{20,35},{2,36},{18,37},{8,38},{24,39},{6,40... | collective-permute-start | bytes 516104 | tf_op jit(solution)/shard_map/ppermute | solution.py:65
  165.5 14.3 %collective-permute-start.19 = (bf16[64,3584]{1,0:T(8,128)(2,1)S(1)}, bf16[64,3584]{1,0:T(8,128)(2,1)S(1)}, u32[]{:S(2)}, u32[]{:S(2)}) collective-permute-start(bf16[64,3584]{1,0:T(8,128)(2,1)S(1)} %bitcast.27), channel_id=1, source_target_pairs={{32,0},{33,1},{34,2},{35,3},{36,4},{37,5},{38,6},{39,7},{40,8},{41... | collective-permute-start | bytes 1376264 | tf_op jit(solution)/shard_map/ppermute | solution.py:65
  (25 other events, 388.9 us)

commit v3 on v2

v3 whole, which is shorter than its diff:
```python
import jax
import jax.numpy as jnp
from jax import lax
from jax.experimental import pallas as pl
from jax.experimental.pallas import tpu as pltpu
from jax.sharding import PartitionSpec as P

D = 3584
HALF = D // 2
HID = 256
TOK = 64
CAP = 12
MSG = 4 * CAP
ROWS = 8 * CAP
PAIRS = 4
STEPS = 4
BF = jnp.bfloat16
F32 = jnp.float32
NT = (((1,), (1,)), ((), ()))


def at(y, p, b, c):
    return ((y * PAIRS + p) * 2 + b) * 2 + c


def places_of():
    return [
        (y, p, b, c) for y in range(2) for p in range(PAIRS) for b in range(2) for c in range(2)
    ]


def near(step):
    pairs = []
    for y, p, b, c in places_of():
        if step == 0:
            dp, nb = 2, 1 - b
        elif step == 3:
            dp, nb = 0, b
        elif (step == 1) == (b == 0):
            dp, nb = 1, 0
        else:
            dp, nb = -1, 1
        pairs.append((at(y, p, b, c), at(c, (p + dp) % PAIRS, nb, y)))
    return pairs


def other_core(block):
    pairs = [(at(y, p, b, c), at(y, p, b, 1 - c)) for y, p, b, c in places_of()]
    return lax.ppermute(block, "expert", pairs)


def other_chip(block):
    pairs = [(at(y, p, b, c), at(y, p, 1 - b, c)) for y, p, b, c in places_of()]
    return lax.ppermute(block, "expert", pairs)


def to_section(block, distance, pairs):
    sections, members = lax.axis_size("pipe"), lax.axis_size("expert")
    route = [
        (s * members + i, (s + distance) * members + j)
        for s in range(sections)
        if 0 <= s + distance < sections
        for i, j in pairs
    ]
    return lax.ppermute(block, ("pipe", "expert"), route)


def vmem(n):
    return [pl.BlockSpec(memory_space=pltpu.VMEM)] * n


def call(kernel, outs, n_in, name, smem=0, flops=0, scratch=(), limit=40):
    return pl.pallas_call(
        kernel,
        out_shape=outs,
        in_specs=[pl.BlockSpec(memory_space=pltpu.SMEM)] * smem + vmem(n_in),
        out_specs=tuple(vmem(len(outs))),
        scratch_shapes=scratch,
        compiler_params=pltpu.CompilerParams(vmem_limit_bytes=limit * 2**20),
        cost_estimate=pl.CostEstimate(flops=flops, bytes_accessed=0, transcendentals=0),
        name=name,
    )


def token_rows(me_ref, own_ref, other_ref):
    me = me_ref[0]
    core, chip, pair = me % 2, (me // 2) % 2, (me // 4) % PAIRS
    line = jnp.concatenate([own_ref[...], other_ref[...]], axis=1)
    n = 2 * TOK
    first = lax.broadcasted_iota(jnp.int32, (n, n), 0)
    second = lax.broadcasted_iota(jnp.int32, (n, n), 1)
    wide = jnp.broadcast_to(line, (n, n))
    column = jnp.sum(jnp.where(first == second, wide, 0), axis=1, keepdims=True)
    same_group = (first < TOK) == (second < TOK)
    before = (column == wide) & (first < second) & same_group
    place = jnp.sum(before.astype(jnp.int32), axis=0, keepdims=True)
    dp = ((line & 3) - pair + 4) & 3
    side = jnp.where(chip == 0, 1, 3)
    step = jnp.where(dp == 0, 3, jnp.where(dp == 2, 0, jnp.where(dp == side, 1, 2)))
    is_other = (lax.broadcasted_iota(jnp.int32, (1, n), 1) >= TOK).astype(jnp.int32)
    row = step * 2 * CAP + is_other * CAP + place
    return jnp.where((line >> 2) == core, row, -1)


def dispatch_kernel(me_ref, own_ids, other_ids, gates_ref, *refs):
    tokens, meta_ref, outs = refs[: -STEPS - 1], refs[-STEPS - 1], refs[-STEPS:]
    row = token_rows(me_ref, own_ids, other_ids)
    gates = jnp.concatenate([gates_ref[...], gates_ref[...]], axis=1)
    which = lax.broadcasted_iota(jnp.int32, (8, 2 * TOK), 0)
    meta_ref[...] = jnp.where(which == 0, row.astype(F32), jnp.where(which == 1, gates, 0.0))
    pick = (lax.broadcasted_iota(jnp.int32, (ROWS, 2 * TOK), 0) == row).astype(BF)
    width = 256
    for k in range(len(tokens) // 2):
        own_ref, other_ref = tokens[2 * k], tokens[2 * k + 1]
        for j in range(HALF // width):
            parts = []
            for at_col in (j * width, HALF + j * width):
                columns = slice(at_col, at_col + width)
                both = jnp.concatenate([own_ref[:, columns], other_ref[:, columns]], axis=0)
                parts.append(jnp.dot(pick, both, preferred_element_type=F32))
            for s in range(STEPS):
                rows = slice(s * 2 * CAP, (s + 1) * 2 * CAP)
                block = jnp.concatenate([parts[0][rows], parts[1][rows]], axis=0)
                outs[s][k * MSG : (k + 1) * MSG, j * width : (j + 1) * width] = block.astype(BF)


def join_kernel(*refs):
    out = refs[-1]
    for k in range(out.shape[0] // ROWS):
        at_row = slice(k * ROWS, (k + 1) * ROWS)
        for j in range(HALF // 256):
            columns = slice(j * 256, (j + 1) * 256)
            blocks = [r[k * MSG : (k + 1) * MSG, columns].astype(F32) for r in refs[:-1]]
            low = jnp.concatenate([b[: 2 * CAP] for b in blocks], axis=0)
            high = jnp.concatenate([b[2 * CAP :] for b in blocks], axis=0)
            out[at_row, columns] = low.astype(BF)
            out[at_row, HALF + j * 256 : HALF + (j + 1) * 256] = high.astype(BF)


def stacked(refs):
    return jnp.concatenate([r[...] for r in refs], axis=0)


def forward_kernel(x0, x1, x2, x3, gate, up, down, o0, o1, o2, o3):
    rows = stacked((x0, x1, x2, x3))
    pre_gate = jnp.dot(rows, gate[...], preferred_element_type=F32)
    pre_up = jnp.dot(rows, up[...], preferred_element_type=F32)
    hidden = (jax.nn.silu(pre_gate) * pre_up).astype(BF)
    for j in range(D // 512):
        columns = slice(j * 512, (j + 1) * 512)
        part = jnp.dot(hidden, down[:, columns], preferred_element_type=F32).astype(BF)
        for k, o in enumerate((o0, o1, o2, o3)):
            o[:, columns] = part[k * ROWS : (k + 1) * ROWS]


def backward_kernel(r0, r1, r2, r3, gate, up, down, o0, o1, o2, o3):
    rows_x = jnp.concatenate([r[:ROWS] for r in (r0, r1, r2, r3)], axis=0)
    pre_gate = jnp.dot(rows_x, gate[...], preferred_element_type=F32)
    pre_up = jnp.dot(rows_x, up[...], preferred_element_type=F32)
    rows_g = jnp.concatenate([r[ROWS:] for r in (r0, r1, r2, r3)], axis=0)
    act_grad = lax.dot_general(rows_g, down[...], NT, preferred_element_type=F32)
    sig = jax.nn.sigmoid(pre_gate)
    gate_grad = (act_grad * pre_up * sig * (1.0 + pre_gate * (1.0 - sig))).astype(BF)
    up_grad = (act_grad * pre_gate * sig).astype(BF)
    for j in range(D // 512):
        columns = slice(j * 512, (j + 1) * 512)
        part = lax.dot_general(gate_grad, gate[columns, :], NT, preferred_element_type=F32)
        part = part + lax.dot_general(up_grad, up[columns, :], NT, preferred_element_type=F32)
        part = part.astype(BF)
        for k, o in enumerate((o0, o1, o2, o3)):
            o[:, columns] = part[k * ROWS : (k + 1) * ROWS]


def add_kernel(a, b, o):
    o[...] = (a[...].astype(F32) + b[...].astype(F32)).astype(BF)


def split_kernel(a, b, c, *outs):
    for j in range(HALF // 256):
        parts = []
        for at_col in (j * 256, HALF + j * 256):
            columns = slice(at_col, at_col + 256)
            parts.append(
                a[:, columns].astype(F32) + b[:, columns].astype(F32) + c[:, columns].astype(F32)
            )
        for s in range(STEPS):
            rows = slice(s * 2 * CAP, (s + 1) * 2 * CAP)
            block = jnp.concatenate([parts[0][rows], parts[1][rows]], axis=0)
            outs[s][:, j * 256 : (j + 1) * 256] = block.astype(BF)


def pick_kernel(meta_ref, m0, m1, m2, m3, mine, theirs):
    row = meta_ref[0:1, :].astype(jnp.int32)
    step = jnp.where(row < 2 * CAP, 0, jnp.where(row < 4 * CAP, 1, jnp.where(row < 6 * CAP, 2, 3)))
    row = jnp.where(row < 0, -MSG, row + step * 2 * CAP)
    where = lax.broadcasted_iota(jnp.int32, (STEPS * MSG, 2 * TOK), 0)
    low = (where == row).astype(F32).T.astype(BF)
    high = (where == row + 2 * CAP).astype(F32).T.astype(BF)
    for j in range(HALF // 256):
        columns = slice(j * 256, (j + 1) * 256)
        rows = jnp.concatenate([m[:, columns] for m in (m0, m1, m2, m3)], axis=0)
        for at_col, pick in ((j * 256, low), (HALF + j * 256, high)):
            got = jnp.dot(pick, rows, preferred_element_type=F32).astype(BF)
            mine[:, at_col : at_col + 256] = got[:TOK]
            theirs[:, at_col : at_col + 256] = got[TOK:]


def final_kernel(meta_ref, base, mine, theirs, o):
    n = 2 * TOK
    diagonal = lax.broadcasted_iota(jnp.int32, (TOK, n), 0) == lax.broadcasted_iota(
        jnp.int32, (TOK, n), 1
    )
    gates = jnp.broadcast_to(meta_ref[1:2, :], (TOK, n))
    weight = jnp.sum(jnp.where(diagonal, gates, 0.0), axis=1, keepdims=True)
    for j in range(D // 512):
        columns = slice(j * 512, (j + 1) * 512)
        row = mine[:, columns].astype(F32) + theirs[:, columns].astype(F32)
        o[:, columns] = (base[:, columns].astype(F32) + weight * row).astype(BF)


def shape(*dims, kind=BF):
    return jax.ShapeDtypeStruct(dims, kind)


def after(value, *earlier):
    return lax.optimization_barrier((value, earlier))[0]


def dispatch(me, own_ids, other_ids, gates, *tokens):
    outs = [shape(8, 2 * TOK, kind=F32)] + [shape(MSG * (len(tokens) // 2), HALF)] * STEPS
    meta, *messages = call(dispatch_kernel, outs, 3 + len(tokens), "dispatch", smem=1)(
        me, own_ids, other_ids, gates, *tokens
    )
    return meta, messages


def send(messages, distance=0):
    if distance:
        return [to_section(m, distance, [(j, i) for i, j in near(s)]) for s, m in enumerate(messages)]
    return [lax.ppermute(m, "expert", near(s)) for s, m in enumerate(messages)]


def join(messages):
    rows = messages[0].shape[0] * 2
    (own,) = call(join_kernel, [shape(rows, D)], STEPS, "join")(*messages)
    return own


def core_sums(parts, *earlier):
    own, beside, across, diagonal = parts
    diagonal = after(diagonal, *earlier)
    from_diagonal = other_core(diagonal)
    from_beside = other_core(beside)
    (chip_sum,) = call(add_kernel, [shape(ROWS, D)], 2, "chip_sum")(across, from_diagonal)
    return own, from_beside, chip_sum


def pair_sums(own, from_beside, from_across):
    return call(split_kernel, [shape(MSG, HALF)] * STEPS, 3, "pair_sum")(
        own, from_beside, from_across
    )


def finish(messages, base, meta):
    mine, theirs = call(pick_kernel, [shape(TOK, D)] * 2, 5, "pick")(meta, *messages)
    (out,) = call(final_kernel, [shape(TOK, D)], 4, "final")(meta, base, mine, other_core(theirs))
    return out


def body(x_fwd, routes_fwd, gates_fwd, x_bwd, grad_bwd, routes_bwd, gates_bwd, gate, up, down):
    x_a, x_b, g_b = x_fwd[0], x_bwd[0], grad_bwd[0]
    gate, up, down = gate[0], up[0], down[0]
    me = lax.axis_index("expert").astype(jnp.int32).reshape(1)
    same = [(i, i) for i in range(lax.axis_size("expert"))]
    ids_a, ids_b = routes_fwd.reshape(1, TOK), routes_bwd.reshape(1, TOK)
    gates_a, gates_b = gates_fwd.reshape(1, TOK), gates_bwd.reshape(1, TOK)

    other_a, x_a_other = other_core(ids_a), other_core(x_a)
    others_b = other_core(ids_b), other_core(x_b), other_core(g_b)
    meta_a, sent_a = dispatch(me, ids_a, other_a, gates_a, x_a, x_a_other)
    meta_b, sent_b = dispatch(me, ids_b, others_b[0], gates_b, x_b, others_b[1], g_b, others_b[2])
    got_a = send([*sent_a[:2], *after(sent_a[2:], meta_b)])
    got_b = send(after(sent_b, *got_a[1:]))

    own_a = join(got_a)
    across_a = other_chip(own_a)
    rows_a = (own_a, other_core(after(own_a, got_b[3])), across_a, other_core(across_a))
    own_b = join(got_b)
    across_b = other_chip(own_b)
    x_a, g_b, meta_a, meta_b = after((x_a, g_b, meta_a, meta_b), across_a, own_b)
    base_a = to_section(x_a, 1, same)
    base_b = to_section(g_b, -1, same)
    meta_a = to_section(meta_a, 1, same)
    meta_b = to_section(meta_b, -1, same)

    outs = [shape(ROWS, D)] * 4
    work = 6 * 384 * D * HID
    parts_a = call(forward_kernel, outs, 7, "expert_fwd", flops=work)(*rows_a, gate, up, down)
    own_a, beside_a, chip_a = core_sums(parts_a)
    across_b = after(across_b, chip_a, meta_a, meta_b, base_a, base_b)
    rows_b = (own_b, other_core(after(own_b, chip_a)), across_b, other_core(across_b))
    across_a = other_chip(after(chip_a, across_b))
    parts_b = call(backward_kernel, outs, 7, "expert_bwd", flops=2 * work)(*rows_b, gate, up, down)
    own_b, beside_b, chip_b = core_sums(parts_b, across_a)
    across_b = other_chip(after(chip_b, across_a))
    back_a = send(pair_sums(own_a, beside_a, across_a), 1)
    back_b = send(pair_sums(own_b, beside_b, across_b), -1)
    fwd_next = finish(back_a, base_a, meta_a)
    bwd_next = finish(back_b, base_b, meta_b)
    return fwd_next[None], bwd_next[None]


def solution(mesh):
    rows, cols = P("pipe", "expert", None), P("pipe", None, "expert")
    in_specs = (rows,) * 7 + (cols, cols, rows)
    return jax.shard_map(
        body, mesh=mesh, in_specs=in_specs, out_specs=(rows, rows), check_vma=False
    )
```

time: 189 us -> 174 us (0.921)
  starting transfers between devices: 111 us -> 89 us
  waiting for transfers between devices: 51.3 us -> 64 us
  Pallas kernels: 17.4 us -> 12.4 us
  other arithmetic: 3.06 us -> 0 us
    ppermute x5 -> x4, waiting for transfers between devices: 18.8 us -> 34.5 us  [other_chip(): return lax.ppermute(block, 'expert', pairs)]
    ppermute x12 -> x8, starting transfers between devices: 40.5 us -> 27.2 us  [send(): return [lax.ppermute(m, 'expert', near(s)) for s, m in enumerate(messages)]]
    ppermute x16 -> x15, waiting for transfers between devices: 1.51 us -> 7.51 us  [other_core(): return lax.ppermute(block, 'expert', pairs)]
    ppermute x12 -> x8, waiting for transfers between devices: 21.3 us -> 16.1 us  [send(): return [lax.ppermute(m, 'expert', near(s)) for s, m in enumerate(messages)]]
    ppermute x5 -> x4, starting transfers between devices: 6.79 us -> 1.67 us  [other_chip(): return lax.ppermute(block, 'expert', pairs)]
    pallas_call x15 -> x12, Pallas kernels: 15.4 us -> 10.4 us  [the longest x1 5 us: body(): call(backward_kernel, outs, 7, 'expert_bwd', flops=2 * work)]
    ppermute x12, starting transfers between devices: 57.9 us -> 53.4 us  [to_section(): return lax.ppermute(block, ('pipe', 'expert'), route)]
    ppermute x12, waiting for transfers between devices: 9.66 us -> 5.93 us  [to_section(): return lax.ppermute(block, ('pipe', 'expert'), route)]
  transfers between devices with their start and end apart: 45 -> 39, of which waited for: 10 -> 17; matrix products, arithmetic and copies ran while one was open for 3% -> 0% of each run, Pallas kernels for 9% -> 7%
where the time goes in v3:
time: 174 us; the launch traced here: 172 us
  starting transfers between devices  89 us (51%)
  waiting for transfers between devices  64 us (37%)
  Pallas kernels  12.4 us (7%)
  local copies, waits for them, and re-layouts  5.69 us (3%)
    ppermute x12, starting transfers between devices, to_section(): return lax.ppermute(block, ('pipe', 'expert'), route)  53.4 us
    ppermute x4, waiting for transfers between devices, other_chip(): return lax.ppermute(block, 'expert', pairs)  34.5 us
    ppermute x8, starting transfers between devices, send(): return [lax.ppermute(m, 'expert', near(s)) for s, m in enumerate(messages)]  27.2 us
    ppermute x8, waiting for transfers between devices, send(): return [lax.ppermute(m, 'expert', near(s)) for s, m in enumerate(messages)]  16.1 us
    ppermute x15, waiting for transfers between devices, other_core(): return lax.ppermute(block, 'expert', pairs)  7.51 us
    ppermute x15, starting transfers between devices, other_core(): return lax.ppermute(block, 'expert', pairs)  6.71 us
    ppermute x12, waiting for transfers between devices, to_section(): return lax.ppermute(block, ('pipe', 'expert'), route)  5.93 us
    unnamed x24, local copies, waits for them, and re-layouts  5.69 us
  transfers between devices with their start and end apart: 39, of which 17 were waited for; matrix products, arithmetic and copies ran while one was open for 0% of the time, Pallas kernels for 7%

profile of v3, /device:TPU:9, one launch (start us, length us, event | category | flops | bytes accessed | tf_op | source)
XLA Modules:
  0.0 172.1 jit_solution(5769802673952149322)
XLA Ops:
  2.4 1.9 %collective-permute-done.other_ids = s32[1,64]{1,0:T(1,128)S(1)} collective-permute-done((s32[1,64]{1,0:T(1,128)}, s32[1,64]{1,0:T(1,128)S(1)}, u32[]{:S(2)}, u32[]{:S(2)}) %collective-permute-start) | collective-permute-done | bytes 288 | tf_op jit(solution)/shard_map/ppermute | solution.py:49
  7.2 8.5 %collective-permute-start.5 = (bf16[48,1792]{1,0:T(8,128)(2,1)S(1)}, bf16[48,1792]{1,0:T(8,128)(2,1)S(1)}, u32[]{:S(2)}, u32[]{:S(2)}) collective-permute-start(bf16[48,1792]{1,0:T(8,128)(2,1)S(1)} %get-tuple-element.50), channel_id=1, source_target_pairs={{0,10},{1,26},{2,8},{3,24},{4,14},{5,30},{6,12},{7,28},{8,2},{9,18... | collective-permute-start | bytes 516104 | tf_op jit(solution)/shard_map/ppermute | solution.py:240
  15.8 1.9 %collective-permute-start.6 = (bf16[48,1792]{1,0:T(8,128)(2,1)S(1)}, bf16[48,1792]{1,0:T(8,128)(2,1)S(1)}, u32[]{:S(2)}, u32[]{:S(2)}) collective-permute-start(bf16[48,1792]{1,0:T(8,128)(2,1)S(1)} %get-tuple-element.51), channel_id=1, source_target_pairs={{0,4},{1,20},{2,14},{3,30},{4,8},{5,24},{6,2},{7,18},{8,12},{9,28}... | collective-permute-start | bytes 516104 | tf_op jit(solution)/shard_map/ppermute | solution.py:240
  21.8 4.2 %collective-permute-start.8 = (bf16[48,1792]{1,0:T(8,128)(2,1)S(1)}, bf16[48,1792]{1,0:T(8,128)(2,1)S(1)}, u32[]{:S(2)}, u32[]{:S(2)}) collective-permute-start(bf16[48,1792]{1,0:T(8,128)(2,1)S(1)} %get-tuple-element.55), channel_id=1, source_target_pairs={{0,0},{1,16},{2,2},{3,18},{4,4},{5,20},{6,6},{7,22},{8,8},{9,24},{... | collective-permute-start | bytes 516104 | tf_op jit(solution)/shard_map/ppermute | solution.py:240
  26.6 3.8 %collective-permute-done.7.refs_2_ = bf16[48,1792]{1,0:T(8,128)(2,1)S(1)} collective-permute-done((bf16[48,1792]{1,0:T(8,128)(2,1)S(1)}, bf16[48,1792]{1,0:T(8,128)(2,1)S(1)}, u32[]{:S(2)}, u32[]{:S(2)}) %collective-permute-start.7) | collective-permute-done | bytes 172064 | tf_op jit(solution)/shard_map/ppermute | solution.py:240
  30.4 1.5 collective-permute-done.8.refs_3_
  32.5 4.2 %collective-permute-start.13 = (bf16[96,1792]{1,0:T(8,128)(2,1)S(1)}, bf16[96,1792]{1,0:T(8,128)(2,1)S(1)}, u32[]{:S(2)}, u32[]{:S(2)}) collective-permute-start(bf16[96,1792]{1,0:T(8,128)(2,1)S(1)} %get-tuple-element.63), channel_id=1, source_target_pairs={{0,0},{1,16},{2,2},{3,18},{4,4},{5,20},{6,6},{7,22},{8,8},{9,24},{... | collective-permute-start | bytes 1032200 | tf_op jit(solution)/shard_map/ppermute | solution.py:240
  36.8 5.6 %collective-permute-start.10 = (bf16[96,1792]{1,0:T(8,128)(2,1)S(1)}, bf16[96,1792]{1,0:T(8,128)(2,1)S(1)}, u32[]{:S(2)}, u32[]{:S(2)}) collective-permute-start(bf16[96,1792]{1,0:T(8,128)(2,1)S(1)} %get-tuple-element.60), channel_id=1, source_target_pairs={{0,10},{1,26},{2,8},{3,24},{4,14},{5,30},{6,12},{7,28},{8,2},{9,18... | collective-permute-start | bytes 1032200 | tf_op jit(solution)/shard_map/ppermute | solution.py:240
  42.4 2.5 %collective-permute-start.11 = (bf16[96,1792]{1,0:T(8,128)(2,1)S(1)}, bf16[96,1792]{1,0:T(8,128)(2,1)S(1)}, u32[]{:S(2)}, u32[]{:S(2)}) collective-permute-start(bf16[96,1792]{1,0:T(8,128)(2,1)S(1)} %get-tuple-element.61), channel_id=1, source_target_pairs={{0,4},{1,20},{2,14},{3,30},{4,8},{5,24},{6,2},{7,18},{8,12},{9,28}... | collective-permute-start | bytes 1032200 | tf_op jit(solution)/shard_map/ppermute | solution.py:240
  45.1 11.3 %collective-permute-done.9.x2 = bf16[96,3584]{1,0:T(8,128)(2,1)S(1)} collective-permute-done((bf16[96,3584]{1,0:T(8,128)(2,1)S(1)}, bf16[96,3584]{1,0:T(8,128)(2,1)S(1)}, u32[]{:S(2)}, u32[]{:S(2)}) %collective-permute-start.9) | collective-permute-done | bytes 688160 | tf_op jit(solution)/shard_map/ppermute | solution.py:54
  57.5 9.1 %collective-permute-done.11.refs_1_ = bf16[96,1792]{1,0:T(8,128)(2,1)S(1)} collective-permute-done((bf16[96,1792]{1,0:T(8,128)(2,1)S(1)}, bf16[96,1792]{1,0:T(8,128)(2,1)S(1)}, u32[]{:S(2)}, u32[]{:S(2)}) %collective-permute-start.11) | collective-permute-done | bytes 344096 | tf_op jit(solution)/shard_map/ppermute | solution.py:240
  67.7 2.4 %expert_fwd.1 = (bf16[96,3584]{1,0:T(8,128)(2,1)S(1)}, bf16[96,3584]{1,0:T(8,128)(2,1)S(1)}, bf16[96,3584]{1,0:T(8,128)(2,1)S(1)}, bf16[96,3584]{1,0:T(8,128)(2,1)S(1)}) custom-call(bf16[96,3584]{1,0:T(8,128)(2,1)S(1)} %join.2.x0, bf16[96,3584]{1,0:T(8,128)(2,1)S(1)} %collective-permute-done.16.x1, bf16[96,3584]{1,0:T(8,128)(2,1)S(1)} %collective-permute-done.9.x2, ...), custom_call_target="tpu_custom_call" | custom-call | flops 2113929216 | tf_op jit(solution)/shard_map/expert_fwd/pallas_call | solution.py:298
  70.4 3.1 %collective-permute-start.15 = (bf16[64,3584]{1,0:T(8,128)(2,1)S(1)}, bf16[64,3584]{1,0:T(8,128)(2,1)S(1)}, u32[]{:S(2)}, u32[]{:S(2)}) collective-permute-start(bf16[64,3584]{1,0:T(8,128)(2,1)S(1)} %bitcast.21), channel_id=1, source_target_pairs={{0,32},{1,33},{2,34},{3,35},{4,36},{5,37},{6,38},{7,39},{8,40},{9,... | collective-permute-start | bytes 1376264 | tf_op jit(solution)/shard_map/ppermute | solution.py:65
  73.5 4.3 %collective-permute-start.22 = (bf16[64,3584]{1,0:T(8,128)(2,1)S(1)}, bf16[64,3584]{1,0:T(8,128)(2,1)S(1)}, u32[]{:S(2)}, u32[]{:S(2)}) collective-permute-start(bf16[64,3584]{1,0:T(8,128)(2,1)S(1)} %bitcast.26), channel_id=1, source_target_pairs={{32,0},{33,1},{34,2},{35,3},{36,4},{37,5},{38,6},{39,7},{40,8},{41... | collective-permute-start | bytes 1376264 | tf_op jit(solution)/shard_map/ppermute | solution.py:65
  77.8 1.9 %collective-permute-start.14 = (f32[8,128]{1,0:T(8,128)S(1)}, f32[8,128]{1,0:T(8,128)S(1)}, u32[]{:S(2)}, u32[]{:S(2)}) collective-permute-start(f32[8,128]{1,0:T(8,128)S(1)} %get-tuple-element.64), channel_id=1, source_target_pairs={{0,32},{1,33},{2,34},{3,35},{4,36},{5,37},{6,38},{7,39},{8,40},{9,... | collective-permute-start | bytes 12296 | tf_op jit(solution)/shard_map/ppermute | solution.py:65
  79.8 5.5 %collective-permute-start.21 = (f32[8,128]{1,0:T(8,128)S(1)}, f32[8,128]{1,0:T(8,128)S(1)}, u32[]{:S(2)}, u32[]{:S(2)}) collective-permute-start(f32[8,128]{1,0:T(8,128)S(1)} %get-tuple-element.71), channel_id=1, source_target_pairs={{32,0},{33,1},{34,2},{35,3},{36,4},{37,5},{38,6},{39,7},{40,8},{41... | collective-permute-start | bytes 12296 | tf_op jit(solution)/shard_map/ppermute | solution.py:65
  87.4 9.7 %collective-permute-done.20.r2 = bf16[192,3584]{1,0:T(8,128)(2,1)S(1)} collective-permute-done((bf16[192,3584]{1,0:T(8,128)(2,1)S(1)}, bf16[192,3584]{1,0:T(8,128)(2,1)S(1)}, u32[]{:S(2)}, u32[]{:S(2)}) %collective-permute-start.20) | collective-permute-done | bytes 1376288 | tf_op jit(solution)/shard_map/ppermute | solution.py:54
  97.2 3.1 %collective-permute-done.30.r3 = bf16[192,3584]{1,0:T(8,128)(2,1)S(1)} collective-permute-done((bf16[192,3584]{1,0:T(8,128)(2,1)S(1)}, bf16[192,3584]{1,0:T(8,128)(2,1)S(1)}, u32[]{:S(2)}, u32[]{:S(2)}) %collective-permute-start.30) | collective-permute-done | bytes 1376288 | tf_op jit(solution)/shard_map/ppermute | solution.py:49
  100.3 5.0 %expert_bwd.1 = (bf16[96,3584]{1,0:T(8,128)(2,1)S(1)}, bf16[96,3584]{1,0:T(8,128)(2,1)S(1)}, bf16[96,3584]{1,0:T(8,128)(2,1)S(1)}, bf16[96,3584]{1,0:T(8,128)(2,1)S(1)}) custom-call(bf16[192,3584]{1,0:T(8,128)(2,1)S(1)} %join.3.r0, bf16[192,3584]{1,0:T(8,128)(2,1)S(1)} %collective-permute-done.29.r1, bf16[192,3584]{1,0:T(8,128)(2,1)S(1)} %collective-permute-done.20.r2, ...), custom_call_target="tpu_custom_call" | custom-call | flops 4227858432 | tf_op jit(solution)/shard_map/expert_bwd/pallas_call | solution.py:303
  105.3 8.4 %collective-permute-done.23.c = bf16[96,3584]{1,0:T(8,128)(2,1)S(1)} collective-permute-done((bf16[96,3584]{1,0:T(8,128)(2,1)S(1)}, bf16[96,3584]{1,0:T(8,128)(2,1)S(1)}, u32[]{:S(2)}, u32[]{:S(2)}) %collective-permute-start.23) | collective-permute-done | bytes 688160 | tf_op jit(solution)/shard_map/ppermute | solution.py:54
  118.0 5.1 %collective-permute-start.24 = (bf16[48,1792]{1,0:T(8,128)(2,1)S(1)}, bf16[48,1792]{1,0:T(8,128)(2,1)S(1)}, u32[]{:S(2)}, u32[]{:S(2)}) collective-permute-start(bf16[48,1792]{1,0:T(8,128)(2,1)S(1)} %get-tuple-element.75), channel_id=1, source_target_pairs={{10,32},{26,33},{8,34},{24,35},{14,36},{30,37},{12,38},{28,39},{2,... | collective-permute-start | bytes 516104 | tf_op jit(solution)/shard_map/ppermute | solution.py:65
  123.2 6.9 %collective-permute-start.25 = (bf16[48,1792]{1,0:T(8,128)(2,1)S(1)}, bf16[48,1792]{1,0:T(8,128)(2,1)S(1)}, u32[]{:S(2)}, u32[]{:S(2)}) collective-permute-start(bf16[48,1792]{1,0:T(8,128)(2,1)S(1)} %get-tuple-element.76), channel_id=1, source_target_pairs={{4,32},{20,33},{14,34},{30,35},{8,36},{24,37},{2,38},{18,39},{12,4... | collective-permute-start | bytes 516104 | tf_op jit(solution)/shard_map/ppermute | solution.py:65
  130.1 4.0 %collective-permute-start.26 = (bf16[48,1792]{1,0:T(8,128)(2,1)S(1)}, bf16[48,1792]{1,0:T(8,128)(2,1)S(1)}, u32[]{:S(2)}, u32[]{:S(2)}) collective-permute-start(bf16[48,1792]{1,0:T(8,128)(2,1)S(1)} %get-tuple-element.77), channel_id=1, source_target_pairs={{14,32},{30,33},{4,34},{20,35},{2,36},{18,37},{8,38},{24,39},{6,40... | collective-permute-start | bytes 516104 | tf_op jit(solution)/shard_map/ppermute | solution.py:65
  134.1 1.9 %collective-permute-start.27 = (bf16[48,1792]{1,0:T(8,128)(2,1)S(1)}, bf16[48,1792]{1,0:T(8,128)(2,1)S(1)}, u32[]{:S(2)}, u32[]{:S(2)}) collective-permute-start(bf16[48,1792]{1,0:T(8,128)(2,1)S(1)} %get-tuple-element.78), channel_id=1, source_target_pairs={{0,32},{16,33},{2,34},{18,35},{4,36},{20,37},{6,38},{22,39},{8,40}... | collective-permute-start | bytes 516104 | tf_op jit(solution)/shard_map/ppermute | solution.py:65
  136.0 5.1 %collective-permute-done.33.c = bf16[96,3584]{1,0:T(8,128)(2,1)S(1)} collective-permute-done((bf16[96,3584]{1,0:T(8,128)(2,1)S(1)}, bf16[96,3584]{1,0:T(8,128)(2,1)S(1)}, u32[]{:S(2)}, u32[]{:S(2)}) %collective-permute-start.33) | collective-permute-done | bytes 688160 | tf_op jit(solution)/shard_map/ppermute | solution.py:54
  141.3 6.8 %collective-permute-start.34 = (bf16[48,1792]{1,0:T(8,128)(2,1)S(1)}, bf16[48,1792]{1,0:T(8,128)(2,1)S(1)}, u32[]{:S(2)}, u32[]{:S(2)}) collective-permute-start(bf16[48,1792]{1,0:T(8,128)(2,1)S(1)} %get-tuple-element.88), channel_id=1, source_target_pairs={{42,0},{58,1},{40,2},{56,3},{46,4},{62,5},{44,6},{60,7},{34,8},{50... | collective-permute-start | bytes 516104 | tf_op jit(solution)/shard_map/ppermute | solution.py:65
  148.2 4.8 %collective-permute-start.35 = (bf16[48,1792]{1,0:T(8,128)(2,1)S(1)}, bf16[48,1792]{1,0:T(8,128)(2,1)S(1)}, u32[]{:S(2)}, u32[]{:S(2)}) collective-permute-start(bf16[48,1792]{1,0:T(8,128)(2,1)S(1)} %get-tuple-element.89), channel_id=1, source_target_pairs={{36,0},{52,1},{46,2},{62,3},{40,4},{56,5},{34,6},{50,7},{44,8},{60... | collective-permute-start | bytes 516104 | tf_op jit(solution)/shard_map/ppermute | solution.py:65
  153.0 5.7 %collective-permute-start.36 = (bf16[48,1792]{1,0:T(8,128)(2,1)S(1)}, bf16[48,1792]{1,0:T(8,128)(2,1)S(1)}, u32[]{:S(2)}, u32[]{:S(2)}) collective-permute-start(bf16[48,1792]{1,0:T(8,128)(2,1)S(1)} %get-tuple-element.90), channel_id=1, source_target_pairs={{46,0},{62,1},{36,2},{52,3},{34,4},{50,5},{40,6},{56,7},{38,8},{54... | collective-permute-start | bytes 516104 | tf_op jit(solution)/shard_map/ppermute | solution.py:65
  158.8 3.3 %collective-permute-start.37 = (bf16[48,1792]{1,0:T(8,128)(2,1)S(1)}, bf16[48,1792]{1,0:T(8,128)(2,1)S(1)}, u32[]{:S(2)}, u32[]{:S(2)}) collective-permute-start(bf16[48,1792]{1,0:T(8,128)(2,1)S(1)} %get-tuple-element.91), channel_id=1, source_target_pairs={{32,0},{48,1},{34,2},{50,3},{36,4},{52,5},{38,6},{54,7},{40,8},{56... | collective-permute-start | bytes 516104 | tf_op jit(solution)/shard_map/ppermute | solution.py:65
  162.7 1.7 collective-permute-done.36.m2
  164.3 3.6 %collective-permute-done.37.m3 = bf16[48,1792]{1,0:T(8,128)(2,1)S(1)} collective-permute-done((bf16[48,1792]{1,0:T(8,128)(2,1)S(1)}, bf16[48,1792]{1,0:T(8,128)(2,1)S(1)}, u32[]{:S(2)}, u32[]{:S(2)}) %collective-permute-start.37) | collective-permute-done | bytes 172064 | tf_op jit(solution)/shard_map/ppermute | solution.py:65
  168.3 1.4 collective-permute-start.38
  (84 shorter events, 22.9 us)
Async XLA Ops:
  1.4 16.3 %collective-permute-start.3 = (bf16[64,3584]{1,0:T(8,128)(2,1)}, bf16[64,3584]{1,0:T(8,128)(2,1)S(1)}, u32[]{:S(2)}, u32[]{:S(2)}) collective-permute-start(bf16[64,3584]{1,0:T(8,128)(2,1)} %bitcast.22), channel_id=1, source_target_pairs={{0,1},{1,0},{2,3},{3,2},{4,5},{5,4},{6,7},{7,6},{8,9},{9,8},{10,11... | collective-permute-start | bytes 1376264 | tf_op jit(solution)/shard_map/ppermute | solution.py:49
  1.5 16.2 %collective-permute-start.4 = (bf16[64,3584]{1,0:T(8,128)(2,1)}, bf16[64,3584]{1,0:T(8,128)(2,1)S(1)}, u32[]{:S(2)}, u32[]{:S(2)}) collective-permute-start(bf16[64,3584]{1,0:T(8,128)(2,1)} %bitcast.24), channel_id=1, source_target_pairs={{0,1},{1,0},{2,3},{3,2},{4,5},{5,4},{6,7},{7,6},{8,9},{9,8},{10,11... | collective-permute-start | bytes 1376264 | tf_op jit(solution)/shard_map/ppermute | solution.py:49
  2.0 15.6 %collective-permute-start.2 = (s32[1,64]{1,0:T(1,128)}, s32[1,64]{1,0:T(1,128)S(1)}, u32[]{:S(2)}, u32[]{:S(2)}) collective-permute-start(s32[1,64]{1,0:T(1,128)} %bitcast.30), channel_id=1, source_target_pairs={{0,1},{1,0},{2,3},{3,2},{4,5},{5,4},{6,7},{7,6},{8,9},{9,8},{10,11... | collective-permute-start | bytes 776 | tf_op jit(solution)/shard_map/ppermute | solution.py:49
  7.2 19.4 %collective-permute-start.5 = (bf16[48,1792]{1,0:T(8,128)(2,1)S(1)}, bf16[48,1792]{1,0:T(8,128)(2,1)S(1)}, u32[]{:S(2)}, u32[]{:S(2)}) collective-permute-start(bf16[48,1792]{1,0:T(8,128)(2,1)S(1)} %get-tuple-element.50), channel_id=1, source_target_pairs={{0,10},{1,26},{2,8},{3,24},{4,14},{5,30},{6,12},{7,28},{8,2},{9,18... | collective-permute-start | bytes 516104 | tf_op jit(solution)/shard_map/ppermute | solution.py:240
  15.8 10.8 %collective-permute-start.6 = (bf16[48,1792]{1,0:T(8,128)(2,1)S(1)}, bf16[48,1792]{1,0:T(8,128)(2,1)S(1)}, u32[]{:S(2)}, u32[]{:S(2)}) collective-permute-start(bf16[48,1792]{1,0:T(8,128)(2,1)S(1)} %get-tuple-element.51), channel_id=1, source_target_pairs={{0,4},{1,20},{2,14},{3,30},{4,8},{5,24},{6,2},{7,18},{8,12},{9,28}... | collective-permute-start | bytes 516104 | tf_op jit(solution)/shard_map/ppermute | solution.py:240
  21.7 8.7 %collective-permute-start.7 = (bf16[48,1792]{1,0:T(8,128)(2,1)S(1)}, bf16[48,1792]{1,0:T(8,128)(2,1)S(1)}, u32[]{:S(2)}, u32[]{:S(2)}) collective-permute-start(bf16[48,1792]{1,0:T(8,128)(2,1)S(1)} %get-tuple-element.54), channel_id=1, source_target_pairs={{0,14},{1,30},{2,4},{3,20},{4,2},{5,18},{6,8},{7,24},{8,6},{9,22},... | collective-permute-start | bytes 516104 | tf_op jit(solution)/shard_map/ppermute | solution.py:240
  21.8 10.1 %collective-permute-start.8 = (bf16[48,1792]{1,0:T(8,128)(2,1)S(1)}, bf16[48,1792]{1,0:T(8,128)(2,1)S(1)}, u32[]{:S(2)}, u32[]{:S(2)}) collective-permute-start(bf16[48,1792]{1,0:T(8,128)(2,1)S(1)} %get-tuple-element.55), channel_id=1, source_target_pairs={{0,0},{1,16},{2,2},{3,18},{4,4},{5,20},{6,6},{7,22},{8,8},{9,24},{... | collective-permute-start | bytes 516104 | tf_op jit(solution)/shard_map/ppermute | solution.py:240
  31.9 24.4 %collective-permute-start.9 = (bf16[96,3584]{1,0:T(8,128)(2,1)S(1)}, bf16[96,3584]{1,0:T(8,128)(2,1)S(1)}, u32[]{:S(2)}, u32[]{:S(2)}) collective-permute-start(bf16[96,3584]{1,0:T(8,128)(2,1)S(1)} %join.2.x0), channel_id=1, source_target_pairs={{0,2},{1,3},{2,0},{3,1},{4,6},{5,7},{6,4},{7,5},{8,10},{9,11},{10,... | collective-permute-start | bytes 2064392 | tf_op jit(solution)/shard_map/ppermute | solution.py:54
  32.5 12.5 %collective-permute-start.13 = (bf16[96,1792]{1,0:T(8,128)(2,1)S(1)}, bf16[96,1792]{1,0:T(8,128)(2,1)S(1)}, u32[]{:S(2)}, u32[]{:S(2)}) collective-permute-start(bf16[96,1792]{1,0:T(8,128)(2,1)S(1)} %get-tuple-element.63), channel_id=1, source_target_pairs={{0,0},{1,16},{2,2},{3,18},{4,4},{5,20},{6,6},{7,22},{8,8},{9,24},{... | collective-permute-start | bytes 1032200 | tf_op jit(solution)/shard_map/ppermute | solution.py:240
  36.8 20.7 %collective-permute-start.10 = (bf16[96,1792]{1,0:T(8,128)(2,1)S(1)}, bf16[96,1792]{1,0:T(8,128)(2,1)S(1)}, u32[]{:S(2)}, u32[]{:S(2)}) collective-permute-start(bf16[96,1792]{1,0:T(8,128)(2,1)S(1)} %get-tuple-element.60), channel_id=1, source_target_pairs={{0,10},{1,26},{2,8},{3,24},{4,14},{5,30},{6,12},{7,28},{8,2},{9,18... | collective-permute-start | bytes 1032200 | tf_op jit(solution)/shard_map/ppermute | solution.py:240
  42.4 24.3 %collective-permute-start.11 = (bf16[96,1792]{1,0:T(8,128)(2,1)S(1)}, bf16[96,1792]{1,0:T(8,128)(2,1)S(1)}, u32[]{:S(2)}, u32[]{:S(2)}) collective-permute-start(bf16[96,1792]{1,0:T(8,128)(2,1)S(1)} %get-tuple-element.61), channel_id=1, source_target_pairs={{0,4},{1,20},{2,14},{3,30},{4,8},{5,24},{6,2},{7,18},{8,12},{9,28}... | collective-permute-start | bytes 1032200 | tf_op jit(solution)/shard_map/ppermute | solution.py:240
  44.8 21.8 %collective-permute-start.12 = (bf16[96,1792]{1,0:T(8,128)(2,1)S(1)}, bf16[96,1792]{1,0:T(8,128)(2,1)S(1)}, u32[]{:S(2)}, u32[]{:S(2)}) collective-permute-start(bf16[96,1792]{1,0:T(8,128)(2,1)S(1)} %get-tuple-element.62), channel_id=1, source_target_pairs={{0,14},{1,30},{2,4},{3,20},{4,2},{5,18},{6,8},{7,24},{8,6},{9,22},... | collective-permute-start | bytes 1032200 | tf_op jit(solution)/shard_map/ppermute | solution.py:240
  45.1 22.6 %collective-permute-start.16 = (bf16[96,3584]{1,0:T(8,128)(2,1)S(1)}, bf16[96,3584]{1,0:T(8,128)(2,1)S(1)}, u32[]{:S(2)}, u32[]{:S(2)}) collective-permute-start(bf16[96,3584]{1,0:T(8,128)(2,1)S(1)} %join.2.x0), channel_id=1, source_target_pairs={{0,1},{1,0},{2,3},{3,2},{4,5},{5,4},{6,7},{7,6},{8,9},{9,8},{10,11... | collective-permute-start | bytes 2064392 | tf_op jit(solution)/shard_map/ppermute | solution.py:49
  56.4 11.3 %collective-permute-start.17 = (bf16[96,3584]{1,0:T(8,128)(2,1)S(1)}, bf16[96,3584]{1,0:T(8,128)(2,1)S(1)}, u32[]{:S(2)}, u32[]{:S(2)}) collective-permute-start(bf16[96,3584]{1,0:T(8,128)(2,1)S(1)} %collective-permute-done.9.x2), channel_id=1, source_target_pairs={{0,1},{1,0},{2,3},{3,2},{4,5},{5,4},{6,7},{7,6},{8,9},{9,8},{10,11... | collective-permute-start | bytes 2064392 | tf_op jit(solution)/shard_map/ppermute | solution.py:49
  66.7 30.5 %collective-permute-start.20 = (bf16[192,3584]{1,0:T(8,128)(2,1)S(1)}, bf16[192,3584]{1,0:T(8,128)(2,1)S(1)}, u32[]{:S(2)}, u32[]{:S(2)}) collective-permute-start(bf16[192,3584]{1,0:T(8,128)(2,1)S(1)} %join.3.r0), channel_id=1, source_target_pairs={{0,2},{1,3},{2,0},{3,1},{4,6},{5,7},{6,4},{7,5},{8,10},{9,11},{10,... | collective-permute-start | bytes 4128776 | tf_op jit(solution)/shard_map/ppermute | solution.py:54
  70.1 9.6 %collective-permute-start.19 = (bf16[96,3584]{1,0:T(8,128)(2,1)S(1)}, bf16[96,3584]{1,0:T(8,128)(2,1)S(1)}, u32[]{:S(2)}, u32[]{:S(2)}) collective-permute-start(bf16[96,3584]{1,0:T(8,128)(2,1)S(1)} %get-tuple-element.70), channel_id=1, source_target_pairs={{0,1},{1,0},{2,3},{3,2},{4,5},{5,4},{6,7},{7,6},{8,9},{9,8},{10,11... | collective-permute-start | bytes 2064392 | tf_op jit(solution)/shard_map/ppermute | solution.py:49
  70.4 17.0 %collective-permute-start.15 = (bf16[64,3584]{1,0:T(8,128)(2,1)S(1)}, bf16[64,3584]{1,0:T(8,128)(2,1)S(1)}, u32[]{:S(2)}, u32[]{:S(2)}) collective-permute-start(bf16[64,3584]{1,0:T(8,128)(2,1)S(1)} %bitcast.21), channel_id=1, source_target_pairs={{0,32},{1,33},{2,34},{3,35},{4,36},{5,37},{6,38},{7,39},{8,40},{9,... | collective-permute-start | bytes 1376264 | tf_op jit(solution)/shard_map/ppermute | solution.py:65
  73.5 13.9 %collective-permute-start.22 = (bf16[64,3584]{1,0:T(8,128)(2,1)S(1)}, bf16[64,3584]{1,0:T(8,128)(2,1)S(1)}, u32[]{:S(2)}, u32[]{:S(2)}) collective-permute-start(bf16[64,3584]{1,0:T(8,128)(2,1)S(1)} %bitcast.26), channel_id=1, source_target_pairs={{32,0},{33,1},{34,2},{35,3},{36,4},{37,5},{38,6},{39,7},{40,8},{41... | collective-permute-start | bytes 1376264 | tf_op jit(solution)/shard_map/ppermute | solution.py:65
  77.8 8.3 %collective-permute-start.14 = (f32[8,128]{1,0:T(8,128)S(1)}, f32[8,128]{1,0:T(8,128)S(1)}, u32[]{:S(2)}, u32[]{:S(2)}) collective-permute-start(f32[8,128]{1,0:T(8,128)S(1)} %get-tuple-element.64), channel_id=1, source_target_pairs={{0,32},{1,33},{2,34},{3,35},{4,36},{5,37},{6,38},{7,39},{8,40},{9,... | collective-permute-start | bytes 12296 | tf_op jit(solution)/shard_map/ppermute | solution.py:65
  79.8 7.7 %collective-permute-start.21 = (f32[8,128]{1,0:T(8,128)S(1)}, f32[8,128]{1,0:T(8,128)S(1)}, u32[]{:S(2)}, u32[]{:S(2)}) collective-permute-start(f32[8,128]{1,0:T(8,128)S(1)} %get-tuple-element.71), channel_id=1, source_target_pairs={{32,0},{33,1},{34,2},{35,3},{36,4},{37,5},{38,6},{39,7},{40,8},{41... | collective-permute-start | bytes 12296 | tf_op jit(solution)/shard_map/ppermute | solution.py:65
  86.1 11.1 %collective-permute-start.29 = (bf16[192,3584]{1,0:T(8,128)(2,1)S(1)}, bf16[192,3584]{1,0:T(8,128)(2,1)S(1)}, u32[]{:S(2)}, u32[]{:S(2)}) collective-permute-start(bf16[192,3584]{1,0:T(8,128)(2,1)S(1)} %join.3.r0), channel_id=1, source_target_pairs={{0,1},{1,0},{2,3},{3,2},{4,5},{5,4},{6,7},{7,6},{8,9},{9,8},{10,11... | collective-permute-start | bytes 4128776 | tf_op jit(solution)/shard_map/ppermute | solution.py:49
  97.2 16.5 %collective-permute-start.23 = (bf16[96,3584]{1,0:T(8,128)(2,1)S(1)}, bf16[96,3584]{1,0:T(8,128)(2,1)S(1)}, u32[]{:S(2)}, u32[]{:S(2)}) collective-permute-start(bf16[96,3584]{1,0:T(8,128)(2,1)S(1)} %chip_sum.2), channel_id=1, source_target_pairs={{0,2},{1,3},{2,0},{3,1},{4,6},{5,7},{6,4},{7,5},{8,10},{9,11},{10,... | collective-permute-start | bytes 2064392 | tf_op jit(solution)/shard_map/ppermute | solution.py:54
  115.0 19.0 %collective-permute-start.31 = (bf16[96,3584]{1,0:T(8,128)(2,1)S(1)}, bf16[96,3584]{1,0:T(8,128)(2,1)S(1)}, u32[]{:S(2)}, u32[]{:S(2)}) collective-permute-start(bf16[96,3584]{1,0:T(8,128)(2,1)S(1)} %get-tuple-element.83), channel_id=1, source_target_pairs={{0,1},{1,0},{2,3},{3,2},{4,5},{5,4},{6,7},{7,6},{8,9},{9,8},{10,11... | collective-permute-start | bytes 2064392 | tf_op jit(solution)/shard_map/ppermute | solution.py:49
  117.0 24.1 %collective-permute-start.33 = (bf16[96,3584]{1,0:T(8,128)(2,1)S(1)}, bf16[96,3584]{1,0:T(8,128)(2,1)S(1)}, u32[]{:S(2)}, u32[]{:S(2)}) collective-permute-start(bf16[96,3584]{1,0:T(8,128)(2,1)S(1)} %chip_sum.3), channel_id=1, source_target_pairs={{0,2},{1,3},{2,0},{3,1},{4,6},{5,7},{6,4},{7,5},{8,10},{9,11},{10,... | collective-permute-start | bytes 2064392 | tf_op jit(solution)/shard_map/ppermute | solution.py:54
  118.0 30.1 %collective-permute-start.24 = (bf16[48,1792]{1,0:T(8,128)(2,1)S(1)}, bf16[48,1792]{1,0:T(8,128)(2,1)S(1)}, u32[]{:S(2)}, u32[]{:S(2)}) collective-permute-start(bf16[48,1792]{1,0:T(8,128)(2,1)S(1)} %get-tuple-element.75), channel_id=1, source_target_pairs={{10,32},{26,33},{8,34},{24,35},{14,36},{30,37},{12,38},{28,39},{2,... | collective-permute-start | bytes 516104 | tf_op jit(solution)/shard_map/ppermute | solution.py:65
  123.2 29.8 %collective-permute-start.25 = (bf16[48,1792]{1,0:T(8,128)(2,1)S(1)}, bf16[48,1792]{1,0:T(8,128)(2,1)S(1)}, u32[]{:S(2)}, u32[]{:S(2)}) collective-permute-start(bf16[48,1792]{1,0:T(8,128)(2,1)S(1)} %get-tuple-element.76), channel_id=1, source_target_pairs={{4,32},{20,33},{14,34},{30,35},{8,36},{24,37},{2,38},{18,39},{12,4... | collective-permute-start | bytes 516104 | tf_op jit(solution)/shard_map/ppermute | solution.py:65
  130.1 28.7 %collective-permute-start.26 = (bf16[48,1792]{1,0:T(8,128)(2,1)S(1)}, bf16[48,1792]{1,0:T(8,128)(2,1)S(1)}, u32[]{:S(2)}, u32[]{:S(2)}) collective-permute-start(bf16[48,1792]{1,0:T(8,128)(2,1)S(1)} %get-tuple-element.77), channel_id=1, source_target_pairs={{14,32},{30,33},{4,34},{20,35},{2,36},{18,37},{8,38},{24,39},{6,40... | collective-permute-start | bytes 516104 | tf_op jit(solution)/shard_map/ppermute | solution.py:65
  134.1 28.0 %collective-permute-start.27 = (bf16[48,1792]{1,0:T(8,128)(2,1)S(1)}, bf16[48,1792]{1,0:T(8,128)(2,1)S(1)}, u32[]{:S(2)}, u32[]{:S(2)}) collective-permute-start(bf16[48,1792]{1,0:T(8,128)(2,1)S(1)} %get-tuple-element.78), channel_id=1, source_target_pairs={{0,32},{16,33},{2,34},{18,35},{4,36},{20,37},{6,38},{22,39},{8,40}... | collective-permute-start | bytes 516104 | tf_op jit(solution)/shard_map/ppermute | solution.py:65
  141.3 21.3 %collective-permute-start.34 = (bf16[48,1792]{1,0:T(8,128)(2,1)S(1)}, bf16[48,1792]{1,0:T(8,128)(2,1)S(1)}, u32[]{:S(2)}, u32[]{:S(2)}) collective-permute-start(bf16[48,1792]{1,0:T(8,128)(2,1)S(1)} %get-tuple-element.88), channel_id=1, source_target_pairs={{42,0},{58,1},{40,2},{56,3},{46,4},{62,5},{44,6},{60,7},{34,8},{50... | collective-permute-start | bytes 516104 | tf_op jit(solution)/shard_map/ppermute | solution.py:65
  148.2 14.5 %collective-permute-start.35 = (bf16[48,1792]{1,0:T(8,128)(2,1)S(1)}, bf16[48,1792]{1,0:T(8,128)(2,1)S(1)}, u32[]{:S(2)}, u32[]{:S(2)}) collective-permute-start(bf16[48,1792]{1,0:T(8,128)(2,1)S(1)} %get-tuple-element.89), channel_id=1, source_target_pairs={{36,0},{52,1},{46,2},{62,3},{40,4},{56,5},{34,6},{50,7},{44,8},{60... | collective-permute-start | bytes 516104 | tf_op jit(solution)/shard_map/ppermute | solution.py:65
  153.0 11.3 %collective-permute-start.36 = (bf16[48,1792]{1,0:T(8,128)(2,1)S(1)}, bf16[48,1792]{1,0:T(8,128)(2,1)S(1)}, u32[]{:S(2)}, u32[]{:S(2)}) collective-permute-start(bf16[48,1792]{1,0:T(8,128)(2,1)S(1)} %get-tuple-element.90), channel_id=1, source_target_pairs={{46,0},{62,1},{36,2},{52,3},{34,4},{50,5},{40,6},{56,7},{38,8},{54... | collective-permute-start | bytes 516104 | tf_op jit(solution)/shard_map/ppermute | solution.py:65
  158.8 9.1 %collective-permute-start.37 = (bf16[48,1792]{1,0:T(8,128)(2,1)S(1)}, bf16[48,1792]{1,0:T(8,128)(2,1)S(1)}, u32[]{:S(2)}, u32[]{:S(2)}) collective-permute-start(bf16[48,1792]{1,0:T(8,128)(2,1)S(1)} %get-tuple-element.91), channel_id=1, source_target_pairs={{32,0},{48,1},{34,2},{50,3},{36,4},{52,5},{38,6},{54,7},{40,8},{56... | collective-permute-start | bytes 516104 | tf_op jit(solution)/shard_map/ppermute | solution.py:65
  (19 other events, 157.0 us)

commit v4 on v3

--- a/solution.py
+++ b/solution.py
@@ -1,3 +1,5 @@
+import functools
+
 import jax
 import jax.numpy as jnp
 from jax import lax
@@ -57,9 +59,8 @@
 def to_section(block, distance, pairs):
     sections, members = lax.axis_size("pipe"), lax.axis_size("expert")
     route = [
-        (s * members + i, (s + distance) * members + j)
+        (s * members + i, (s + distance) % sections * members + j)
         for s in range(sections)
-        if 0 <= s + distance < sections
         for i, j in pairs
     ]
     return lax.ppermute(block, ("pipe", "expert"), route)
@@ -70,10 +71,11 @@
 
 
 def call(kernel, outs, n_in, name, smem=0, flops=0, scratch=(), limit=40):
+    scalars = [pl.BlockSpec(memory_space=pltpu.SMEM)] * smem
     return pl.pallas_call(
         kernel,
         out_shape=outs,
-        in_specs=[pl.BlockSpec(memory_space=pltpu.SMEM)] * smem + vmem(n_in),
+        in_specs=scalars + vmem(n_in),
         out_specs=tuple(vmem(len(outs))),
         scratch_shapes=scratch,
         compiler_params=pltpu.CompilerParams(vmem_limit_bytes=limit * 2**20),
@@ -125,39 +127,44 @@
 
 
 def join_kernel(*refs):
-    out = refs[-1]
-    for k in range(out.shape[0] // ROWS):
-        at_row = slice(k * ROWS, (k + 1) * ROWS)
+    messages, out = refs[:-1], refs[-1]
+    size = 2 * CAP * len(messages)
+    for k in range(out.shape[0] // size):
+        at_row = slice(k * size, (k + 1) * size)
         for j in range(HALF // 256):
             columns = slice(j * 256, (j + 1) * 256)
-            blocks = [r[k * MSG : (k + 1) * MSG, columns].astype(F32) for r in refs[:-1]]
+            blocks = [r[k * MSG : (k + 1) * MSG, columns].astype(F32) for r in messages]
             low = jnp.concatenate([b[: 2 * CAP] for b in blocks], axis=0)
             high = jnp.concatenate([b[2 * CAP :] for b in blocks], axis=0)
             out[at_row, columns] = low.astype(BF)
             out[at_row, HALF + j * 256 : HALF + (j + 1) * 256] = high.astype(BF)
 
 
-def stacked(refs):
-    return jnp.concatenate([r[...] for r in refs], axis=0)
-
-
-def forward_kernel(x0, x1, x2, x3, gate, up, down, o0, o1, o2, o3):
-    rows = stacked((x0, x1, x2, x3))
+def stacked(refs, start=0):
+    return jnp.concatenate([r[start : start + ROWS] for r in refs], axis=0)
+
+
+def forward_kernel(*refs):
+    gate, up, down, *outs = refs[4:]
+    rows = stacked(refs[:4])
     pre_gate = jnp.dot(rows, gate[...], preferred_element_type=F32)
     pre_up = jnp.dot(rows, up[...], preferred_element_type=F32)
     hidden = (jax.nn.silu(pre_gate) * pre_up).astype(BF)
     for j in range(D // 512):
         columns = slice(j * 512, (j + 1) * 512)
         part = jnp.dot(hidden, down[:, columns], preferred_element_type=F32).astype(BF)
-        for k, o in enumerate((o0, o1, o2, o3)):
-            o[:, columns] = part[k * ROWS : (k + 1) * ROWS]
-
-
-def backward_kernel(r0, r1, r2, r3, gate, up, down, o0, o1, o2, o3):
-    rows_x = jnp.concatenate([r[:ROWS] for r in (r0, r1, r2, r3)], axis=0)
+        start = 0
+        for o in outs:
+            o[:, columns] = part[start : start + o.shape[0]]
+            start += o.shape[0]
+
+
+def backward_kernel(*refs):
+    gate, up, down, *outs = refs[4:]
+    rows_x = stacked(refs[:4])
     pre_gate = jnp.dot(rows_x, gate[...], preferred_element_type=F32)
     pre_up = jnp.dot(rows_x, up[...], preferred_element_type=F32)
-    rows_g = jnp.concatenate([r[ROWS:] for r in (r0, r1, r2, r3)], axis=0)
+    rows_g = stacked(refs[:4], ROWS)
     act_grad = lax.dot_general(rows_g, down[...], NT, preferred_element_type=F32)
     sig = jax.nn.sigmoid(pre_gate)
     gate_grad = (act_grad * pre_up * sig * (1.0 + pre_gate * (1.0 - sig))).astype(BF)
@@ -167,26 +174,28 @@
         part = lax.dot_general(gate_grad, gate[columns, :], NT, preferred_element_type=F32)
         part = part + lax.dot_general(up_grad, up[columns, :], NT, preferred_element_type=F32)
         part = part.astype(BF)
-        for k, o in enumerate((o0, o1, o2, o3)):
-            o[:, columns] = part[k * ROWS : (k + 1) * ROWS]
+        start = 0
+        for o in outs:
+            o[:, columns] = part[start : start + o.shape[0]]
+            start += o.shape[0]
 
 
 def add_kernel(a, b, o):
     o[...] = (a[...].astype(F32) + b[...].astype(F32)).astype(BF)
 
 
-def split_kernel(a, b, c, *outs):
+def split_kernel(start, a, b, c, *outs):
+    mine = slice(start, start + c.shape[0])
     for j in range(HALF // 256):
         parts = []
         for at_col in (j * 256, HALF + j * 256):
             columns = slice(at_col, at_col + 256)
-            parts.append(
-                a[:, columns].astype(F32) + b[:, columns].astype(F32) + c[:, columns].astype(F32)
-            )
-        for s in range(STEPS):
+            both = a[mine, columns].astype(F32) + b[mine, columns].astype(F32)
+            parts.append(both + c[:, columns].astype(F32))
+        for s, o in enumerate(outs):
             rows = slice(s * 2 * CAP, (s + 1) * 2 * CAP)
             block = jnp.concatenate([parts[0][rows], parts[1][rows]], axis=0)
-            outs[s][:, j * 256 : (j + 1) * 256] = block.astype(BF)
+            o[:, j * 256 : (j + 1) * 256] = block.astype(BF)
 
 
 def pick_kernel(meta_ref, m0, m1, m2, m3, mine, theirs):
@@ -205,7 +214,8 @@
             theirs[:, at_col : at_col + 256] = got[TOK:]
 
 
-def final_kernel(meta_ref, base, mine, theirs, o):
+def final_kernel(keep_ref, meta_ref, base, mine, theirs, o):
+    keep = keep_ref[0] != 0
     n = 2 * TOK
     diagonal = lax.broadcasted_iota(jnp.int32, (TOK, n), 0) == lax.broadcasted_iota(
         jnp.int32, (TOK, n), 1
@@ -215,7 +225,8 @@
     for j in range(D // 512):
         columns = slice(j * 512, (j + 1) * 512)
         row = mine[:, columns].astype(F32) + theirs[:, columns].astype(F32)
-        o[:, columns] = (base[:, columns].astype(F32) + weight * row).astype(BF)
+        total = base[:, columns].astype(F32) + weight * row
+        o[:, columns] = jnp.where(keep, total, 0.0).astype(BF)
 
 
 def shape(*dims, kind=BF):
@@ -234,36 +245,42 @@
     return meta, messages
 
 
-def send(messages, distance=0):
+def send(messages, steps, distance=0):
     if distance:
-        return [to_section(m, distance, [(j, i) for i, j in near(s)]) for s, m in enumerate(messages)]
-    return [lax.ppermute(m, "expert", near(s)) for s, m in enumerate(messages)]
+        routes = [[(j, i) for i, j in near(s)] for s in steps]
+        return [to_section(m, distance, route) for m, route in zip(messages, routes)]
+    return [lax.ppermute(m, "expert", near(s)) for m, s in zip(messages, steps)]
 
 
 def join(messages):
-    rows = messages[0].shape[0] * 2
-    (own,) = call(join_kernel, [shape(rows, D)], STEPS, "join")(*messages)
+    rows = messages[0].shape[0] // MSG * 2 * CAP * len(messages)
+    (own,) = call(join_kernel, [shape(rows, D)], len(messages), "join")(*messages)
     return own
 
 
-def core_sums(parts, *earlier):
-    own, beside, across, diagonal = parts
-    diagonal = after(diagonal, *earlier)
-    from_diagonal = other_core(diagonal)
+def core_sums(parts):
+    own, beside, *rest = parts
+    n = len(rest) // 2
+    from_diagonal = [other_core(piece) for piece in rest[n:]]
     from_beside = other_core(beside)
-    (chip_sum,) = call(add_kernel, [shape(ROWS, D)], 2, "chip_sum")(across, from_diagonal)
-    return own, from_beside, chip_sum
-
-
-def pair_sums(own, from_beside, from_across):
-    return call(split_kernel, [shape(MSG, HALF)] * STEPS, 3, "pair_sum")(
-        own, from_beside, from_across
-    )
-
-
-def finish(messages, base, meta):
+    sums = [
+        call(add_kernel, [shape(*a.shape)], 2, "chip_sum")(a, b)[0]
+        for a, b in zip(rest, from_diagonal)
+    ]
+    return own, from_beside, sums
+
+
+def pair_sums(steps, own, from_beside, from_across):
+    kernel = functools.partial(split_kernel, steps.start * 2 * CAP)
+    outs = [shape(MSG, HALF)] * (steps.stop - steps.start)
+    return call(kernel, outs, 3, "pair_sum")(own, from_beside, from_across)
+
+
+def finish(keep, messages, base, meta):
     mine, theirs = call(pick_kernel, [shape(TOK, D)] * 2, 5, "pick")(meta, *messages)
-    (out,) = call(final_kernel, [shape(TOK, D)], 4, "final")(meta, base, mine, other_core(theirs))
+    (out,) = call(final_kernel, [shape(TOK, D)], 4, "final", smem=1)(
+        keep, meta, base, mine, other_core(theirs)
+    )
     return out
 
 
@@ -271,6 +288,9 @@
     x_a, x_b, g_b = x_fwd[0], x_bwd[0], grad_bwd[0]
     gate, up, down = gate[0], up[0], down[0]
     me = lax.axis_index("expert").astype(jnp.int32).reshape(1)
+    section = lax.axis_index("pipe").astype(jnp.int32).reshape(1)
+    last = lax.axis_size("pipe") - 1
+    keep_a, keep_b = (section != 0).astype(jnp.int32), (section != last).astype(jnp.int32)
     same = [(i, i) for i in range(lax.axis_size("expert"))]
     ids_a, ids_b = routes_fwd.reshape(1, TOK), routes_bwd.reshape(1, TOK)
     gates_a, gates_b = gates_fwd.reshape(1, TOK), gates_bwd.reshape(1, TOK)
@@ -279,8 +299,8 @@
     others_b = other_core(ids_b), other_core(x_b), other_core(g_b)
     meta_a, sent_a = dispatch(me, ids_a, other_a, gates_a, x_a, x_a_other)
     meta_b, sent_b = dispatch(me, ids_b, others_b[0], gates_b, x_b, others_b[1], g_b, others_b[2])
-    got_a = send([*sent_a[:2], *after(sent_a[2:], meta_b)])
-    got_b = send(after(sent_b, *got_a[1:]))
+    got_a = send([*sent_a[:2], *after(sent_a[2:], meta_b)], range(STEPS))
+    got_b = send(after(sent_b, *got_a[1:]), range(STEPS))
 
     own_a = join(got_a)
     across_a = other_chip(own_a)
@@ -297,16 +317,21 @@
     work = 6 * 384 * D * HID
     parts_a = call(forward_kernel, outs, 7, "expert_fwd", flops=work)(*rows_a, gate, up, down)
     own_a, beside_a, chip_a = core_sums(parts_a)
-    across_b = after(across_b, chip_a, meta_a, meta_b, base_a, base_b)
-    rows_b = (own_b, other_core(after(own_b, chip_a)), across_b, other_core(across_b))
-    across_a = other_chip(after(chip_a, across_b))
+    across_b = after(across_b, *chip_a, meta_a, meta_b, base_a, base_b)
+    rows_b = (own_b, other_core(after(own_b, *chip_a)), across_b, other_core(across_b))
+    back_a = other_chip(after(chip_a[0], across_b))
+    outs = outs[:2] + [shape(ROWS // 2, D)] * 4
     parts_b = call(backward_kernel, outs, 7, "expert_bwd", flops=2 * work)(*rows_b, gate, up, down)
-    own_b, beside_b, chip_b = core_sums(parts_b, across_a)
-    across_b = other_chip(after(chip_b, across_a))
-    back_a = send(pair_sums(own_a, beside_a, across_a), 1)
-    back_b = send(pair_sums(own_b, beside_b, across_b), -1)
-    fwd_next = finish(back_a, base_a, meta_a)
-    bwd_next = finish(back_b, base_b, meta_b)
+    own_b, beside_b, chip_b = core_sums(parts_b)
+    back_b0 = other_chip(chip_b[0])
+    sums_a = pair_sums(slice(0, STEPS), after(own_a, *chip_b), beside_a, back_a)
+    back_b1 = other_chip(after(chip_b[1], back_b0, sums_a[0]))
+    got_a = send(sums_a[:1], (0,), 1)
+    got_a += send(after(sums_a[1:], back_b0, got_a[0]), (1, 2, 3), 1)
+    got_b = send(pair_sums(slice(0, 2), own_b, beside_b, back_b0), (0, 1), -1)
+    got_b += send(pair_sums(slice(2, 4), own_b, beside_b, back_b1), (2, 3), -1)
+    fwd_next = finish(keep_a, got_a, base_a, meta_a)
+    bwd_next = finish(keep_b, got_b, base_b, meta_b)
     return fwd_next[None], bwd_next[None]
 
 

time: 174 us -> 171 us (0.983)
  starting transfers between devices: 89 us -> 72.9 us
  waiting for transfers between devices: 64 us -> 74.9 us
    ppermute x12, starting transfers between devices: 53.4 us -> 29.2 us  [to_section(): return lax.ppermute(block, ('pipe', 'expert'), route)]
    ppermute x12, waiting for transfers between devices: 5.93 us -> 15.4 us  [to_section(): return lax.ppermute(block, ('pipe', 'expert'), route)]
    ppermute x4 -> x5, starting transfers between devices: 1.67 us -> 8.04 us  [other_chip(): return lax.ppermute(block, 'expert', pairs)]
    ppermute x4 -> x5, waiting for transfers between devices: 34.5 us -> 39.6 us  [other_chip(): return lax.ppermute(block, 'expert', pairs)]
    ppermute x8, starting transfers between devices: 27.2 us -> 29.8 us  [send(): return [lax.ppermute(m, 'expert', near(s)) for m, s in zip(messages, steps)]]
    ppermute x15 -> x16, waiting for transfers between devices: 7.51 us -> 5.55 us  [other_core(): return lax.ppermute(block, 'expert', pairs)]
    ppermute x15 -> x16, starting transfers between devices: 6.71 us -> 5.78 us  [other_core(): return lax.ppermute(block, 'expert', pairs)]
  transfers between devices with their start and end apart: 39 -> 41, of which waited for: 17 -> 20; matrix products, arithmetic and copies ran while one was open for 0% -> 0% of each run, Pallas kernels for 7% -> 7%
where the time goes in v4:
time: 171 us; the launch traced here: 168 us
  waiting for transfers between devices  74.9 us (44%)
  starting transfers between devices  72.9 us (43%)
  Pallas kernels  13.2 us (8%)
  local copies, waits for them, and re-layouts  5.69 us (3%)
    ppermute x5, waiting for transfers between devices, other_chip(): return lax.ppermute(block, 'expert', pairs)  39.6 us
    ppermute x8, starting transfers between devices, send(): return [lax.ppermute(m, 'expert', near(s)) for m, s in zip(messages, steps)]  29.8 us
    ppermute x12, starting transfers between devices, to_section(): return lax.ppermute(block, ('pipe', 'expert'), route)  29.2 us
    ppermute x12, waiting for transfers between devices, to_section(): return lax.ppermute(block, ('pipe', 'expert'), route)  15.4 us
    ppermute x8, waiting for transfers between devices, send(): return [lax.ppermute(m, 'expert', near(s)) for m, s in zip(messages, steps)]  14.4 us
    ppermute x5, starting transfers between devices, other_chip(): return lax.ppermute(block, 'expert', pairs)  8.04 us
    ppermute x16, starting transfers between devices, other_core(): return lax.ppermute(block, 'expert', pairs)  5.78 us
    unnamed x24, local copies, waits for them, and re-layouts  5.69 us
  transfers between devices with their start and end apart: 41, of which 20 were waited for; matrix products, arithmetic and copies ran while one was open for 0% of the time, Pallas kernels for 7%

profile of v4, /device:TPU:9, one launch (start us, length us, event | category | flops | bytes accessed | tf_op | source)
XLA Modules:
  0.0 167.6 jit_solution(637396280496921725)
XLA Ops:
  2.4 1.9 %collective-permute-done.other_ids = s32[1,64]{1,0:T(1,128)S(1)} collective-permute-done((s32[1,64]{1,0:T(1,128)}, s32[1,64]{1,0:T(1,128)S(1)}, u32[]{:S(2)}, u32[]{:S(2)}) %collective-permute-start) | collective-permute-done | bytes 288 | tf_op jit(solution)/shard_map/ppermute | solution.py:51
  11.3 7.7 %collective-permute-start.7 = (bf16[48,1792]{1,0:T(8,128)(2,1)S(1)}, bf16[48,1792]{1,0:T(8,128)(2,1)S(1)}, u32[]{:S(2)}, u32[]{:S(2)}) collective-permute-start(bf16[48,1792]{1,0:T(8,128)(2,1)S(1)} %get-tuple-element.59), channel_id=1, source_target_pairs={{0,14},{1,30},{2,4},{3,20},{4,2},{5,18},{6,8},{7,24},{8,6},{9,22},... | collective-permute-start | bytes 516104 | tf_op jit(solution)/shard_map/ppermute | solution.py:252
  19.0 2.9 %collective-permute-start.8 = (bf16[48,1792]{1,0:T(8,128)(2,1)S(1)}, bf16[48,1792]{1,0:T(8,128)(2,1)S(1)}, u32[]{:S(2)}, u32[]{:S(2)}) collective-permute-start(bf16[48,1792]{1,0:T(8,128)(2,1)S(1)} %get-tuple-element.60), channel_id=1, source_target_pairs={{0,0},{1,16},{2,2},{3,18},{4,4},{5,20},{6,6},{7,22},{8,8},{9,24},{... | collective-permute-start | bytes 516104 | tf_op jit(solution)/shard_map/ppermute | solution.py:252
  21.9 6.7 %collective-permute-start.5 = (bf16[48,1792]{1,0:T(8,128)(2,1)S(1)}, bf16[48,1792]{1,0:T(8,128)(2,1)S(1)}, u32[]{:S(2)}, u32[]{:S(2)}) collective-permute-start(bf16[48,1792]{1,0:T(8,128)(2,1)S(1)} %get-tuple-element.55), channel_id=1, source_target_pairs={{0,10},{1,26},{2,8},{3,24},{4,14},{5,30},{6,12},{7,28},{8,2},{9,18... | collective-permute-start | bytes 516104 | tf_op jit(solution)/shard_map/ppermute | solution.py:252
  28.6 2.7 %collective-permute-done.6.refs_1_ = bf16[48,1792]{1,0:T(8,128)(2,1)S(1)} collective-permute-done((bf16[48,1792]{1,0:T(8,128)(2,1)S(1)}, bf16[48,1792]{1,0:T(8,128)(2,1)S(1)}, u32[]{:S(2)}, u32[]{:S(2)}) %collective-permute-start.6) | collective-permute-done | bytes 172064 | tf_op jit(solution)/shard_map/ppermute | solution.py:252
  31.4 3.3 %collective-permute-done.5.refs_0_ = bf16[48,1792]{1,0:T(8,128)(2,1)S(1)} collective-permute-done((bf16[48,1792]{1,0:T(8,128)(2,1)S(1)}, bf16[48,1792]{1,0:T(8,128)(2,1)S(1)}, u32[]{:S(2)}, u32[]{:S(2)}) %collective-permute-start.5) | collective-permute-done | bytes 172064 | tf_op jit(solution)/shard_map/ppermute | solution.py:252
  34.7 2.1 %collective-permute-start.9 = (bf16[96,3584]{1,0:T(8,128)(2,1)S(1)}, bf16[96,3584]{1,0:T(8,128)(2,1)S(1)}, u32[]{:S(2)}, u32[]{:S(2)}) collective-permute-start(bf16[96,3584]{1,0:T(8,128)(2,1)S(1)} %join.2.refs_0_), channel_id=1, source_target_pairs={{0,2},{1,3},{2,0},{3,1},{4,6},{5,7},{6,4},{7,5},{8,10},{9,11},{10,... | collective-permute-start | bytes 2064392 | tf_op jit(solution)/shard_map/ppermute | solution.py:56
  36.8 4.9 %collective-permute-start.13 = (bf16[96,1792]{1,0:T(8,128)(2,1)S(1)}, bf16[96,1792]{1,0:T(8,128)(2,1)S(1)}, u32[]{:S(2)}, u32[]{:S(2)}) collective-permute-start(bf16[96,1792]{1,0:T(8,128)(2,1)S(1)} %get-tuple-element.68), channel_id=1, source_target_pairs={{0,0},{1,16},{2,2},{3,18},{4,4},{5,20},{6,6},{7,22},{8,8},{9,24},{... | collective-permute-start | bytes 1032200 | tf_op jit(solution)/shard_map/ppermute | solution.py:252
  41.7 3.5 %collective-permute-start.10 = (bf16[96,1792]{1,0:T(8,128)(2,1)S(1)}, bf16[96,1792]{1,0:T(8,128)(2,1)S(1)}, u32[]{:S(2)}, u32[]{:S(2)}) collective-permute-start(bf16[96,1792]{1,0:T(8,128)(2,1)S(1)} %get-tuple-element.65), channel_id=1, source_target_pairs={{0,10},{1,26},{2,8},{3,24},{4,14},{5,30},{6,12},{7,28},{8,2},{9,18... | collective-permute-start | bytes 1032200 | tf_op jit(solution)/shard_map/ppermute | solution.py:252
  45.2 3.2 %collective-permute-start.11 = (bf16[96,1792]{1,0:T(8,128)(2,1)S(1)}, bf16[96,1792]{1,0:T(8,128)(2,1)S(1)}, u32[]{:S(2)}, u32[]{:S(2)}) collective-permute-start(bf16[96,1792]{1,0:T(8,128)(2,1)S(1)} %get-tuple-element.66), channel_id=1, source_target_pairs={{0,4},{1,20},{2,14},{3,30},{4,8},{5,24},{6,2},{7,18},{8,12},{9,28}... | collective-permute-start | bytes 1032200 | tf_op jit(solution)/shard_map/ppermute | solution.py:252
  49.3 10.9 %collective-permute-done.9.refs_2_ = bf16[96,3584]{1,0:T(8,128)(2,1)S(1)} collective-permute-done((bf16[96,3584]{1,0:T(8,128)(2,1)S(1)}, bf16[96,3584]{1,0:T(8,128)(2,1)S(1)}, u32[]{:S(2)}, u32[]{:S(2)}) %collective-permute-start.9) | collective-permute-done | bytes 688160 | tf_op jit(solution)/shard_map/ppermute | solution.py:56
  60.2 5.6 %collective-permute-done.11.refs_1_ = bf16[96,1792]{1,0:T(8,128)(2,1)S(1)} collective-permute-done((bf16[96,1792]{1,0:T(8,128)(2,1)S(1)}, bf16[96,1792]{1,0:T(8,128)(2,1)S(1)}, u32[]{:S(2)}, u32[]{:S(2)}) %collective-permute-start.11) | collective-permute-done | bytes 344096 | tf_op jit(solution)/shard_map/ppermute | solution.py:252
  65.8 2.8 %collective-permute-done.12.refs_2_ = bf16[96,1792]{1,0:T(8,128)(2,1)S(1)} collective-permute-done((bf16[96,1792]{1,0:T(8,128)(2,1)S(1)}, bf16[96,1792]{1,0:T(8,128)(2,1)S(1)}, u32[]{:S(2)}, u32[]{:S(2)}) %collective-permute-start.12) | collective-permute-done | bytes 344096 | tf_op jit(solution)/shard_map/ppermute | solution.py:252
  68.7 1.8 %collective-permute-start.20 = (bf16[192,3584]{1,0:T(8,128)(2,1)S(1)}, bf16[192,3584]{1,0:T(8,128)(2,1)S(1)}, u32[]{:S(2)}, u32[]{:S(2)}) collective-permute-start(bf16[192,3584]{1,0:T(8,128)(2,1)S(1)} %join.3.refs_0_), channel_id=1, source_target_pairs={{0,2},{1,3},{2,0},{3,1},{4,6},{5,7},{6,4},{7,5},{8,10},{9,11},{10,... | collective-permute-start | bytes 4128776 | tf_op jit(solution)/shard_map/ppermute | solution.py:56
  70.5 2.4 %expert_fwd.1 = (bf16[96,3584]{1,0:T(8,128)(2,1)S(1)}, bf16[96,3584]{1,0:T(8,128)(2,1)S(1)}, bf16[96,3584]{1,0:T(8,128)(2,1)S(1)}, bf16[96,3584]{1,0:T(8,128)(2,1)S(1)}) custom-call(bf16[96,3584]{1,0:T(8,128)(2,1)S(1)} %join.2.refs_0_, bf16[96,3584]{1,0:T(8,128)(2,1)S(1)} %collective-permute-done.16.refs_1_, ...), custom_call_target="tpu_custom_call" | custom-call | flops 2113929216 | tf_op jit(solution)/shard_map/expert_fwd/pallas_call | solution.py:318
  74.5 2.4 %collective-permute-start.22 = (bf16[64,3584]{1,0:T(8,128)(2,1)S(1)}, bf16[64,3584]{1,0:T(8,128)(2,1)S(1)}, u32[]{:S(2)}, u32[]{:S(2)}) collective-permute-start(bf16[64,3584]{1,0:T(8,128)(2,1)S(1)} %bitcast.28), channel_id=1, source_target_pairs={{0,224},{1,225},{2,226},{3,227},{4,228},{5,229},{6,230},{7,231},{8... | collective-permute-start | bytes 1376264 | tf_op jit(solution)/shard_map/ppermute | solution.py:66
  76.8 3.6 %collective-permute-start.21 = (f32[8,128]{1,0:T(8,128)S(1)}, f32[8,128]{1,0:T(8,128)S(1)}, u32[]{:S(2)}, u32[]{:S(2)}) collective-permute-start(f32[8,128]{1,0:T(8,128)S(1)} %get-tuple-element.76), channel_id=1, source_target_pairs={{0,224},{1,225},{2,226},{3,227},{4,228},{5,229},{6,230},{7,231},{8... | collective-permute-start | bytes 12296 | tf_op jit(solution)/shard_map/ppermute | solution.py:66
  80.6 6.6 %collective-permute-done.14.meta_ref = f32[8,128]{1,0:T(8,128)S(1)} collective-permute-done((f32[8,128]{1,0:T(8,128)S(1)}, f32[8,128]{1,0:T(8,128)S(1)}, u32[]{:S(2)}, u32[]{:S(2)}) %collective-permute-start.14) | collective-permute-done | bytes 4128 | tf_op jit(solution)/shard_map/ppermute | solution.py:66
  87.2 13.5 %collective-permute-done.20.refs_2_ = bf16[192,3584]{1,0:T(8,128)(2,1)S(1)} collective-permute-done((bf16[192,3584]{1,0:T(8,128)(2,1)S(1)}, bf16[192,3584]{1,0:T(8,128)(2,1)S(1)}, u32[]{:S(2)}, u32[]{:S(2)}) %collective-permute-start.20) | collective-permute-done | bytes 1376288 | tf_op jit(solution)/shard_map/ppermute | solution.py:56
  101.6 2.0 %collective-permute-start.27 = (bf16[96,3584]{1,0:T(8,128)(2,1)S(1)}, bf16[96,3584]{1,0:T(8,128)(2,1)S(1)}, u32[]{:S(2)}, u32[]{:S(2)}) collective-permute-start(bf16[96,3584]{1,0:T(8,128)(2,1)S(1)} %chip_sum.3), channel_id=1, source_target_pairs={{0,2},{1,3},{2,0},{3,1},{4,6},{5,7},{6,4},{7,5},{8,10},{9,11},{10,... | collective-permute-start | bytes 2064392 | tf_op jit(solution)/shard_map/ppermute | solution.py:56
  103.8 2.0 %collective-permute-done.19.refs_1_ = bf16[192,3584]{1,0:T(8,128)(2,1)S(1)} collective-permute-done((bf16[192,3584]{1,0:T(8,128)(2,1)S(1)}, bf16[192,3584]{1,0:T(8,128)(2,1)S(1)}, u32[]{:S(2)}, u32[]{:S(2)}) %collective-permute-start.19) | collective-permute-done | bytes 1376288 | tf_op jit(solution)/shard_map/ppermute | solution.py:51
  105.8 5.0 %expert_bwd.1 = (bf16[96,3584]{1,0:T(8,128)(2,1)S(1)}, bf16[96,3584]{1,0:T(8,128)(2,1)S(1)}, bf16[48,3584]{1,0:T(8,128)(2,1)S(1)}, bf16[48,3584]{1,0:T(8,128)(2,...) custom-call(bf16[192,3584]{1,0:T(8,128)(2,1)S(1)} %join.3.refs_0_, ...), custom_call_target="tpu_custom_call" | custom-call | flops 4227858432 | tf_op jit(solution)/shard_map/expert_bwd/pallas_call | solution.py:324
  112.6 2.1 %collective-permute-start.29 = (bf16[48,3584]{1,0:T(8,128)(2,1)S(1)}, bf16[48,3584]{1,0:T(8,128)(2,1)S(1)}, u32[]{:S(2)}, u32[]{:S(2)}) collective-permute-start(bf16[48,3584]{1,0:T(8,128)(2,1)S(1)} %chip_sum.4), channel_id=1, source_target_pairs={{0,2},{1,3},{2,0},{3,1},{4,6},{5,7},{6,4},{7,5},{8,10},{9,11},{10,... | collective-permute-start | bytes 1032200 | tf_op jit(solution)/shard_map/ppermute | solution.py:56
  114.8 4.5 %collective-permute-done.27.c = bf16[96,3584]{1,0:T(8,128)(2,1)S(1)} collective-permute-done((bf16[96,3584]{1,0:T(8,128)(2,1)S(1)}, bf16[96,3584]{1,0:T(8,128)(2,1)S(1)}, u32[]{:S(2)}, u32[]{:S(2)}) %collective-permute-start.27) | collective-permute-done | bytes 688160 | tf_op jit(solution)/shard_map/ppermute | solution.py:56
  119.6 10.7 %collective-permute-done.29.c = bf16[48,3584]{1,0:T(8,128)(2,1)S(1)} collective-permute-done((bf16[48,3584]{1,0:T(8,128)(2,1)S(1)}, bf16[48,3584]{1,0:T(8,128)(2,1)S(1)}, u32[]{:S(2)}, u32[]{:S(2)}) %collective-permute-start.29) | collective-permute-done | bytes 344096 | tf_op jit(solution)/shard_map/ppermute | solution.py:56
  131.5 2.4 %collective-permute-start.30 = (bf16[48,1792]{1,0:T(8,128)(2,1)S(1)}, bf16[48,1792]{1,0:T(8,128)(2,1)S(1)}, u32[]{:S(2)}, u32[]{:S(2)}) collective-permute-start(bf16[48,1792]{1,0:T(8,128)(2,1)S(1)} %get-tuple-element.90), channel_id=1, source_target_pairs={{4,32},{20,33},{14,34},{30,35},{8,36},{24,37},{2,38},{18,39},{12,4... | collective-permute-start | bytes 516104 | tf_op jit(solution)/shard_map/ppermute | solution.py:66
  133.9 8.8 %collective-permute-start.31 = (bf16[48,1792]{1,0:T(8,128)(2,1)S(1)}, bf16[48,1792]{1,0:T(8,128)(2,1)S(1)}, u32[]{:S(2)}, u32[]{:S(2)}) collective-permute-start(bf16[48,1792]{1,0:T(8,128)(2,1)S(1)} %get-tuple-element.91), channel_id=1, source_target_pairs={{14,32},{30,33},{4,34},{20,35},{2,36},{18,37},{8,38},{24,39},{6,40... | collective-permute-start | bytes 516104 | tf_op jit(solution)/shard_map/ppermute | solution.py:66
  142.9 4.8 %collective-permute-start.36 = (bf16[48,1792]{1,0:T(8,128)(2,1)S(1)}, bf16[48,1792]{1,0:T(8,128)(2,1)S(1)}, u32[]{:S(2)}, u32[]{:S(2)}) collective-permute-start(bf16[48,1792]{1,0:T(8,128)(2,1)S(1)} %get-tuple-element.98), channel_id=1, source_target_pairs={{4,224},{20,225},{14,226},{30,227},{8,228},{24,229},{2,230},{18,23... | collective-permute-start | bytes 516104 | tf_op jit(solution)/shard_map/ppermute | solution.py:66
  147.8 4.5 %collective-permute-start.38 = (bf16[48,1792]{1,0:T(8,128)(2,1)S(1)}, bf16[48,1792]{1,0:T(8,128)(2,1)S(1)}, u32[]{:S(2)}, u32[]{:S(2)}) collective-permute-start(bf16[48,1792]{1,0:T(8,128)(2,1)S(1)} %get-tuple-element.100), channel_id=1, source_target_pairs={{14,224},{30,225},{4,226},{20,227},{2,228},{18,229},{8,230},{24,23... | collective-permute-start | bytes 516104 | tf_op jit(solution)/shard_map/ppermute | solution.py:66
  153.7 2.4 %collective-permute-done.32.m3 = bf16[48,1792]{1,0:T(8,128)(2,1)S(1)} collective-permute-done((bf16[48,1792]{1,0:T(8,128)(2,1)S(1)}, bf16[48,1792]{1,0:T(8,128)(2,1)S(1)}, u32[]{:S(2)}, u32[]{:S(2)}) %collective-permute-start.32) | collective-permute-done | bytes 172064 | tf_op jit(solution)/shard_map/ppermute | solution.py:66
  158.2 1.9 %collective-permute-done.38.m2 = bf16[48,1792]{1,0:T(8,128)(2,1)S(1)} collective-permute-done((bf16[48,1792]{1,0:T(8,128)(2,1)S(1)}, bf16[48,1792]{1,0:T(8,128)(2,1)S(1)}, u32[]{:S(2)}, u32[]{:S(2)}) %collective-permute-start.38) | collective-permute-done | bytes 172064 | tf_op jit(solution)/shard_map/ppermute | solution.py:66
  163.1 1.8 %collective-permute-start.40 = (bf16[64,3584]{1,0:T(8,128)(2,1)}, bf16[64,3584]{1,0:T(8,128)(2,1)S(1)}, u32[]{:S(2)}, u32[]{:S(2)}) collective-permute-start(bf16[64,3584]{1,0:T(8,128)(2,1)} %get-tuple-element.103), channel_id=1, source_target_pairs={{0,1},{1,0},{2,3},{3,2},{4,5},{5,4},{6,7},{7,6},{8,9},{9,8},{10,11... | collective-permute-start | bytes 1376264 | tf_op jit(solution)/shard_map/ppermute | solution.py:51
  (90 shorter events, 25.7 us)
Async XLA Ops:
  1.4 5.8 %collective-permute-start.4 = (bf16[64,3584]{1,0:T(8,128)(2,1)}, bf16[64,3584]{1,0:T(8,128)(2,1)S(1)}, u32[]{:S(2)}, u32[]{:S(2)}) collective-permute-start(bf16[64,3584]{1,0:T(8,128)(2,1)} %bitcast.26), channel_id=1, source_target_pairs={{0,1},{1,0},{2,3},{3,2},{4,5},{5,4},{6,7},{7,6},{8,9},{9,8},{10,11... | collective-permute-start | bytes 1376264 | tf_op jit(solution)/shard_map/ppermute | solution.py:51
  1.5 5.7 %collective-permute-start.3 = (bf16[64,3584]{1,0:T(8,128)(2,1)}, bf16[64,3584]{1,0:T(8,128)(2,1)S(1)}, u32[]{:S(2)}, u32[]{:S(2)}) collective-permute-start(bf16[64,3584]{1,0:T(8,128)(2,1)} %bitcast.24), channel_id=1, source_target_pairs={{0,1},{1,0},{2,3},{3,2},{4,5},{5,4},{6,7},{7,6},{8,9},{9,8},{10,11... | collective-permute-start | bytes 1376264 | tf_op jit(solution)/shard_map/ppermute | solution.py:51
  11.3 17.3 %collective-permute-start.7 = (bf16[48,1792]{1,0:T(8,128)(2,1)S(1)}, bf16[48,1792]{1,0:T(8,128)(2,1)S(1)}, u32[]{:S(2)}, u32[]{:S(2)}) collective-permute-start(bf16[48,1792]{1,0:T(8,128)(2,1)S(1)} %get-tuple-element.59), channel_id=1, source_target_pairs={{0,14},{1,30},{2,4},{3,20},{4,2},{5,18},{6,8},{7,24},{8,6},{9,22},... | collective-permute-start | bytes 516104 | tf_op jit(solution)/shard_map/ppermute | solution.py:252
  19.0 9.7 %collective-permute-start.8 = (bf16[48,1792]{1,0:T(8,128)(2,1)S(1)}, bf16[48,1792]{1,0:T(8,128)(2,1)S(1)}, u32[]{:S(2)}, u32[]{:S(2)}) collective-permute-start(bf16[48,1792]{1,0:T(8,128)(2,1)S(1)} %get-tuple-element.60), channel_id=1, source_target_pairs={{0,0},{1,16},{2,2},{3,18},{4,4},{5,20},{6,6},{7,22},{8,8},{9,24},{... | collective-permute-start | bytes 516104 | tf_op jit(solution)/shard_map/ppermute | solution.py:252
  21.8 9.5 %collective-permute-start.6 = (bf16[48,1792]{1,0:T(8,128)(2,1)S(1)}, bf16[48,1792]{1,0:T(8,128)(2,1)S(1)}, u32[]{:S(2)}, u32[]{:S(2)}) collective-permute-start(bf16[48,1792]{1,0:T(8,128)(2,1)S(1)} %get-tuple-element.56), channel_id=1, source_target_pairs={{0,4},{1,20},{2,14},{3,30},{4,8},{5,24},{6,2},{7,18},{8,12},{9,28}... | collective-permute-start | bytes 516104 | tf_op jit(solution)/shard_map/ppermute | solution.py:252
  21.9 12.7 %collective-permute-start.5 = (bf16[48,1792]{1,0:T(8,128)(2,1)S(1)}, bf16[48,1792]{1,0:T(8,128)(2,1)S(1)}, u32[]{:S(2)}, u32[]{:S(2)}) collective-permute-start(bf16[48,1792]{1,0:T(8,128)(2,1)S(1)} %get-tuple-element.55), channel_id=1, source_target_pairs={{0,10},{1,26},{2,8},{3,24},{4,14},{5,30},{6,12},{7,28},{8,2},{9,18... | collective-permute-start | bytes 516104 | tf_op jit(solution)/shard_map/ppermute | solution.py:252
  34.7 25.5 %collective-permute-start.9 = (bf16[96,3584]{1,0:T(8,128)(2,1)S(1)}, bf16[96,3584]{1,0:T(8,128)(2,1)S(1)}, u32[]{:S(2)}, u32[]{:S(2)}) collective-permute-start(bf16[96,3584]{1,0:T(8,128)(2,1)S(1)} %join.2.refs_0_), channel_id=1, source_target_pairs={{0,2},{1,3},{2,0},{3,1},{4,6},{5,7},{6,4},{7,5},{8,10},{9,11},{10,... | collective-permute-start | bytes 2064392 | tf_op jit(solution)/shard_map/ppermute | solution.py:56
  36.8 12.5 %collective-permute-start.13 = (bf16[96,1792]{1,0:T(8,128)(2,1)S(1)}, bf16[96,1792]{1,0:T(8,128)(2,1)S(1)}, u32[]{:S(2)}, u32[]{:S(2)}) collective-permute-start(bf16[96,1792]{1,0:T(8,128)(2,1)S(1)} %get-tuple-element.68), channel_id=1, source_target_pairs={{0,0},{1,16},{2,2},{3,18},{4,4},{5,20},{6,6},{7,22},{8,8},{9,24},{... | collective-permute-start | bytes 1032200 | tf_op jit(solution)/shard_map/ppermute | solution.py:252
  41.7 18.5 %collective-permute-start.10 = (bf16[96,1792]{1,0:T(8,128)(2,1)S(1)}, bf16[96,1792]{1,0:T(8,128)(2,1)S(1)}, u32[]{:S(2)}, u32[]{:S(2)}) collective-permute-start(bf16[96,1792]{1,0:T(8,128)(2,1)S(1)} %get-tuple-element.65), channel_id=1, source_target_pairs={{0,10},{1,26},{2,8},{3,24},{4,14},{5,30},{6,12},{7,28},{8,2},{9,18... | collective-permute-start | bytes 1032200 | tf_op jit(solution)/shard_map/ppermute | solution.py:252
  45.2 20.6 %collective-permute-start.11 = (bf16[96,1792]{1,0:T(8,128)(2,1)S(1)}, bf16[96,1792]{1,0:T(8,128)(2,1)S(1)}, u32[]{:S(2)}, u32[]{:S(2)}) collective-permute-start(bf16[96,1792]{1,0:T(8,128)(2,1)S(1)} %get-tuple-element.66), channel_id=1, source_target_pairs={{0,4},{1,20},{2,14},{3,30},{4,8},{5,24},{6,2},{7,18},{8,12},{9,28}... | collective-permute-start | bytes 1032200 | tf_op jit(solution)/shard_map/ppermute | solution.py:252
  48.4 20.2 %collective-permute-start.12 = (bf16[96,1792]{1,0:T(8,128)(2,1)S(1)}, bf16[96,1792]{1,0:T(8,128)(2,1)S(1)}, u32[]{:S(2)}, u32[]{:S(2)}) collective-permute-start(bf16[96,1792]{1,0:T(8,128)(2,1)S(1)} %get-tuple-element.67), channel_id=1, source_target_pairs={{0,14},{1,30},{2,4},{3,20},{4,2},{5,18},{6,8},{7,24},{8,6},{9,22},... | collective-permute-start | bytes 1032200 | tf_op jit(solution)/shard_map/ppermute | solution.py:252
  49.3 21.1 %collective-permute-start.16 = (bf16[96,3584]{1,0:T(8,128)(2,1)S(1)}, bf16[96,3584]{1,0:T(8,128)(2,1)S(1)}, u32[]{:S(2)}, u32[]{:S(2)}) collective-permute-start(bf16[96,3584]{1,0:T(8,128)(2,1)S(1)} %join.2.refs_0_), channel_id=1, source_target_pairs={{0,1},{1,0},{2,3},{3,2},{4,5},{5,4},{6,7},{7,6},{8,9},{9,8},{10,11... | collective-permute-start | bytes 2064392 | tf_op jit(solution)/shard_map/ppermute | solution.py:51
  60.2 10.3 %collective-permute-start.17 = (bf16[96,3584]{1,0:T(8,128)(2,1)S(1)}, bf16[96,3584]{1,0:T(8,128)(2,1)S(1)}, u32[]{:S(2)}, u32[]{:S(2)}) collective-permute-start(bf16[96,3584]{1,0:T(8,128)(2,1)S(1)} %collective-permute-done.9.refs_2_), channel_id=1, source_target_pairs={{0,1},{1,0},{2,3},{3,2},{4,5},{5,4},{6,7},{7,6},{8,9},{9,8},{10,11... | collective-permute-start | bytes 2064392 | tf_op jit(solution)/shard_map/ppermute | solution.py:51
  68.7 32.0 %collective-permute-start.20 = (bf16[192,3584]{1,0:T(8,128)(2,1)S(1)}, bf16[192,3584]{1,0:T(8,128)(2,1)S(1)}, u32[]{:S(2)}, u32[]{:S(2)}) collective-permute-start(bf16[192,3584]{1,0:T(8,128)(2,1)S(1)} %join.3.refs_0_), channel_id=1, source_target_pairs={{0,2},{1,3},{2,0},{3,1},{4,6},{5,7},{6,4},{7,5},{8,10},{9,11},{10,... | collective-permute-start | bytes 4128776 | tf_op jit(solution)/shard_map/ppermute | solution.py:56
  73.2 14.0 %collective-permute-start.15 = (bf16[64,3584]{1,0:T(8,128)(2,1)S(1)}, bf16[64,3584]{1,0:T(8,128)(2,1)S(1)}, u32[]{:S(2)}, u32[]{:S(2)}) collective-permute-start(bf16[64,3584]{1,0:T(8,128)(2,1)S(1)} %bitcast.23), channel_id=1, source_target_pairs={{0,32},{1,33},{2,34},{3,35},{4,36},{5,37},{6,38},{7,39},{8,40},{9,... | collective-permute-start | bytes 1376264 | tf_op jit(solution)/shard_map/ppermute | solution.py:66
  74.5 12.7 %collective-permute-start.22 = (bf16[64,3584]{1,0:T(8,128)(2,1)S(1)}, bf16[64,3584]{1,0:T(8,128)(2,1)S(1)}, u32[]{:S(2)}, u32[]{:S(2)}) collective-permute-start(bf16[64,3584]{1,0:T(8,128)(2,1)S(1)} %bitcast.28), channel_id=1, source_target_pairs={{0,224},{1,225},{2,226},{3,227},{4,228},{5,229},{6,230},{7,231},{8... | collective-permute-start | bytes 1376264 | tf_op jit(solution)/shard_map/ppermute | solution.py:66
  76.8 10.3 %collective-permute-start.14 = (f32[8,128]{1,0:T(8,128)S(1)}, f32[8,128]{1,0:T(8,128)S(1)}, u32[]{:S(2)}, u32[]{:S(2)}) collective-permute-start(f32[8,128]{1,0:T(8,128)S(1)} %get-tuple-element.69), channel_id=1, source_target_pairs={{0,32},{1,33},{2,34},{3,35},{4,36},{5,37},{6,38},{7,39},{8,40},{9,... | collective-permute-start | bytes 12296 | tf_op jit(solution)/shard_map/ppermute | solution.py:66
  76.8 10.3 %collective-permute-start.21 = (f32[8,128]{1,0:T(8,128)S(1)}, f32[8,128]{1,0:T(8,128)S(1)}, u32[]{:S(2)}, u32[]{:S(2)}) collective-permute-start(f32[8,128]{1,0:T(8,128)S(1)} %get-tuple-element.76), channel_id=1, source_target_pairs={{0,224},{1,225},{2,226},{3,227},{4,228},{5,229},{6,230},{7,231},{8... | collective-permute-start | bytes 12296 | tf_op jit(solution)/shard_map/ppermute | solution.py:66
  101.2 13.6 %collective-permute-start.26 = (bf16[96,3584]{1,0:T(8,128)(2,1)S(1)}, bf16[96,3584]{1,0:T(8,128)(2,1)S(1)}, u32[]{:S(2)}, u32[]{:S(2)}) collective-permute-start(bf16[96,3584]{1,0:T(8,128)(2,1)S(1)} %get-tuple-element.84), channel_id=1, source_target_pairs={{0,1},{1,0},{2,3},{3,2},{4,5},{5,4},{6,7},{7,6},{8,9},{9,8},{10,11... | collective-permute-start | bytes 2064392 | tf_op jit(solution)/shard_map/ppermute | solution.py:51
  101.6 17.7 %collective-permute-start.27 = (bf16[96,3584]{1,0:T(8,128)(2,1)S(1)}, bf16[96,3584]{1,0:T(8,128)(2,1)S(1)}, u32[]{:S(2)}, u32[]{:S(2)}) collective-permute-start(bf16[96,3584]{1,0:T(8,128)(2,1)S(1)} %chip_sum.3), channel_id=1, source_target_pairs={{0,2},{1,3},{2,0},{3,1},{4,6},{5,7},{6,4},{7,5},{8,10},{9,11},{10,... | collective-permute-start | bytes 2064392 | tf_op jit(solution)/shard_map/ppermute | solution.py:56
  111.4 31.3 %collective-permute-start.34 = (bf16[96,3584]{1,0:T(8,128)(2,1)S(1)}, bf16[96,3584]{1,0:T(8,128)(2,1)S(1)}, u32[]{:S(2)}, u32[]{:S(2)}) collective-permute-start(bf16[96,3584]{1,0:T(8,128)(2,1)S(1)} %get-tuple-element.96), channel_id=1, source_target_pairs={{0,1},{1,0},{2,3},{3,2},{4,5},{5,4},{6,7},{7,6},{8,9},{9,8},{10,11... | collective-permute-start | bytes 2064392 | tf_op jit(solution)/shard_map/ppermute | solution.py:51
  112.6 17.7 %collective-permute-start.29 = (bf16[48,3584]{1,0:T(8,128)(2,1)S(1)}, bf16[48,3584]{1,0:T(8,128)(2,1)S(1)}, u32[]{:S(2)}, u32[]{:S(2)}) collective-permute-start(bf16[48,3584]{1,0:T(8,128)(2,1)S(1)} %chip_sum.4), channel_id=1, source_target_pairs={{0,2},{1,3},{2,0},{3,1},{4,6},{5,7},{6,4},{7,5},{8,10},{9,11},{10,... | collective-permute-start | bytes 1032200 | tf_op jit(solution)/shard_map/ppermute | solution.py:56
  119.5 12.0 %collective-permute-start.28 = (bf16[48,1792]{1,0:T(8,128)(2,1)S(1)}, bf16[48,1792]{1,0:T(8,128)(2,1)S(1)}, u32[]{:S(2)}, u32[]{:S(2)}) collective-permute-start(bf16[48,1792]{1,0:T(8,128)(2,1)S(1)} %get-tuple-element.86), channel_id=1, source_target_pairs={{10,32},{26,33},{8,34},{24,35},{14,36},{30,37},{12,38},{28,39},{2,... | collective-permute-start | bytes 516104 | tf_op jit(solution)/shard_map/ppermute | solution.py:66
  130.3 17.3 %collective-permute-start.37 = (bf16[48,3584]{1,0:T(8,128)(2,1)S(1)}, bf16[48,3584]{1,0:T(8,128)(2,1)S(1)}, u32[]{:S(2)}, u32[]{:S(2)}) collective-permute-start(bf16[48,3584]{1,0:T(8,128)(2,1)S(1)} %chip_sum.5), channel_id=1, source_target_pairs={{0,2},{1,3},{2,0},{3,1},{4,6},{5,7},{6,4},{7,5},{8,10},{9,11},{10,... | collective-permute-start | bytes 1032200 | tf_op jit(solution)/shard_map/ppermute | solution.py:56
  131.5 16.3 %collective-permute-start.30 = (bf16[48,1792]{1,0:T(8,128)(2,1)S(1)}, bf16[48,1792]{1,0:T(8,128)(2,1)S(1)}, u32[]{:S(2)}, u32[]{:S(2)}) collective-permute-start(bf16[48,1792]{1,0:T(8,128)(2,1)S(1)} %get-tuple-element.90), channel_id=1, source_target_pairs={{4,32},{20,33},{14,34},{30,35},{8,36},{24,37},{2,38},{18,39},{12,4... | collective-permute-start | bytes 516104 | tf_op jit(solution)/shard_map/ppermute | solution.py:66
  133.9 18.4 %collective-permute-start.31 = (bf16[48,1792]{1,0:T(8,128)(2,1)S(1)}, bf16[48,1792]{1,0:T(8,128)(2,1)S(1)}, u32[]{:S(2)}, u32[]{:S(2)}) collective-permute-start(bf16[48,1792]{1,0:T(8,128)(2,1)S(1)} %get-tuple-element.91), channel_id=1, source_target_pairs={{14,32},{30,33},{4,34},{20,35},{2,36},{18,37},{8,38},{24,39},{6,40... | collective-permute-start | bytes 516104 | tf_op jit(solution)/shard_map/ppermute | solution.py:66
  142.8 14.7 %collective-permute-start.35 = (bf16[48,1792]{1,0:T(8,128)(2,1)S(1)}, bf16[48,1792]{1,0:T(8,128)(2,1)S(1)}, u32[]{:S(2)}, u32[]{:S(2)}) collective-permute-start(bf16[48,1792]{1,0:T(8,128)(2,1)S(1)} %get-tuple-element.97), channel_id=1, source_target_pairs={{10,224},{26,225},{8,226},{24,227},{14,228},{30,229},{12,230},{28,... | collective-permute-start | bytes 516104 | tf_op jit(solution)/shard_map/ppermute | solution.py:66
  142.9 15.4 %collective-permute-start.36 = (bf16[48,1792]{1,0:T(8,128)(2,1)S(1)}, bf16[48,1792]{1,0:T(8,128)(2,1)S(1)}, u32[]{:S(2)}, u32[]{:S(2)}) collective-permute-start(bf16[48,1792]{1,0:T(8,128)(2,1)S(1)} %get-tuple-element.98), channel_id=1, source_target_pairs={{4,224},{20,225},{14,226},{30,227},{8,228},{24,229},{2,230},{18,23... | collective-permute-start | bytes 516104 | tf_op jit(solution)/shard_map/ppermute | solution.py:66
  147.6 8.5 %collective-permute-start.32 = (bf16[48,1792]{1,0:T(8,128)(2,1)S(1)}, bf16[48,1792]{1,0:T(8,128)(2,1)S(1)}, u32[]{:S(2)}, u32[]{:S(2)}) collective-permute-start(bf16[48,1792]{1,0:T(8,128)(2,1)S(1)} %get-tuple-element.92), channel_id=1, source_target_pairs={{0,32},{16,33},{2,34},{18,35},{4,36},{20,37},{6,38},{22,39},{8,40}... | collective-permute-start | bytes 516104 | tf_op jit(solution)/shard_map/ppermute | solution.py:66
  147.8 12.4 %collective-permute-start.38 = (bf16[48,1792]{1,0:T(8,128)(2,1)S(1)}, bf16[48,1792]{1,0:T(8,128)(2,1)S(1)}, u32[]{:S(2)}, u32[]{:S(2)}) collective-permute-start(bf16[48,1792]{1,0:T(8,128)(2,1)S(1)} %get-tuple-element.100), channel_id=1, source_target_pairs={{14,224},{30,225},{4,226},{20,227},{2,228},{18,229},{8,230},{24,23... | collective-permute-start | bytes 516104 | tf_op jit(solution)/shard_map/ppermute | solution.py:66
  152.3 9.6 %collective-permute-start.39 = (bf16[48,1792]{1,0:T(8,128)(2,1)S(1)}, bf16[48,1792]{1,0:T(8,128)(2,1)S(1)}, u32[]{:S(2)}, u32[]{:S(2)}) collective-permute-start(bf16[48,1792]{1,0:T(8,128)(2,1)S(1)} %get-tuple-element.101), channel_id=1, source_target_pairs={{0,224},{16,225},{2,226},{18,227},{4,228},{20,229},{6,230},{22,231... | collective-permute-start | bytes 516104 | tf_op jit(solution)/shard_map/ppermute | solution.py:66
  156.6 8.3 %collective-permute-start.33 = (bf16[64,3584]{1,0:T(8,128)(2,1)S(1)}, bf16[64,3584]{1,0:T(8,128)(2,1)S(1)}, u32[]{:S(2)}, u32[]{:S(2)}) collective-permute-start(bf16[64,3584]{1,0:T(8,128)(2,1)S(1)} %get-tuple-element.94), channel_id=1, source_target_pairs={{0,1},{1,0},{2,3},{3,2},{4,5},{5,4},{6,7},{7,6},{8,9},{9,8},{10,11... | collective-permute-start | bytes 1376264 | tf_op jit(solution)/shard_map/ppermute | solution.py:51
  (21 other events, 173.6 us)

commit v5 on v4

--- a/solution.py
+++ b/solution.py
@@ -297,12 +297,14 @@
 
     other_a, x_a_other = other_core(ids_a), other_core(x_a)
     others_b = other_core(ids_b), other_core(x_b), other_core(g_b)
-    meta_a, sent_a = dispatch(me, ids_a, other_a, gates_a, x_a, x_a_other)
-    meta_b, sent_b = dispatch(me, ids_b, others_b[0], gates_b, x_b, others_b[1], g_b, others_b[2])
-    got_a = send([*sent_a[:2], *after(sent_a[2:], meta_b)], range(STEPS))
+    me_a = after(me, *others_b)
+    meta_a, sent_a = dispatch(me_a, ids_a, other_a, gates_a, x_a, x_a_other)
+    got_a = send(sent_a, range(STEPS))
+    late = after(ids_b, got_a[3])
+    meta_b, sent_b = dispatch(me, late, others_b[0], gates_b, x_b, others_b[1], g_b, others_b[2])
     got_b = send(after(sent_b, *got_a[1:]), range(STEPS))
 
-    own_a = join(got_a)
+    own_a = join(after(got_a, meta_b))
     across_a = other_chip(own_a)
     rows_a = (own_a, other_core(after(own_a, got_b[3])), across_a, other_core(across_a))
     own_b = join(got_b)

time: 171 us -> 167 us (0.977); the launches traced: 168 us -> 165 us
    ppermute x8, starting transfers between devices: 29.8 us -> 26.8 us  [send(): return [lax.ppermute(m, 'expert', near(s)) for m, s in zip(messages, steps)]]
  transfers between devices with their start and end apart: 41 -> 41, of which waited for: 20 -> 19; matrix products, arithmetic and copies ran while one was open for 0% -> 0% of each run, Pallas kernels for 7% -> 7%
where the time goes in v5:
time: 167 us; the launch traced here: 165 us
  waiting for transfers between devices  74.4 us (45%)
  starting transfers between devices  71.3 us (43%)
  Pallas kernels  13.3 us (8%)
  local copies, waits for them, and re-layouts  5.69 us (3%)
    ppermute x5, waiting for transfers between devices, other_chip(): return lax.ppermute(block, 'expert', pairs)  38.2 us
    ppermute x12, starting transfers between devices, to_section(): return lax.ppermute(block, ('pipe', 'expert'), route)  29.4 us
    ppermute x8, starting transfers between devices, send(): return [lax.ppermute(m, 'expert', near(s)) for m, s in zip(messages, steps)]  26.8 us
    ppermute x8, waiting for transfers between devices, send(): return [lax.ppermute(m, 'expert', near(s)) for m, s in zip(messages, steps)]  15.6 us
    ppermute x12, waiting for transfers between devices, to_section(): return lax.ppermute(block, ('pipe', 'expert'), route)  14.9 us
    ppermute x5, starting transfers between devices, other_chip(): return lax.ppermute(block, 'expert', pairs)  8.26 us
    ppermute x16, starting transfers between devices, other_core(): return lax.ppermute(block, 'expert', pairs)  6.91 us
    unnamed x24, local copies, waits for them, and re-layouts  5.69 us
  transfers between devices with their start and end apart: 41, of which 19 were waited for; matrix products, arithmetic and copies ran while one was open for 0% of the time, Pallas kernels for 7%

profile of v5, /device:TPU:9, one launch (start us, length us, event | category | flops | bytes accessed | tf_op | source)
XLA Modules:
  0.0 165.5 jit_solution(14178696179404704363)
XLA Ops:
  2.4 1.9 %collective-permute-done.other_ids = s32[1,64]{1,0:T(1,128)S(1)} collective-permute-done((s32[1,64]{1,0:T(1,128)}, s32[1,64]{1,0:T(1,128)S(1)}, u32[]{:S(2)}, u32[]{:S(2)}) %collective-permute-start) | collective-permute-done | bytes 288 | tf_op jit(solution)/shard_map/ppermute | solution.py:51
  7.2 4.2 %collective-permute-start.5 = (bf16[48,1792]{1,0:T(8,128)(2,1)S(1)}, bf16[48,1792]{1,0:T(8,128)(2,1)S(1)}, u32[]{:S(2)}, u32[]{:S(2)}) collective-permute-start(bf16[48,1792]{1,0:T(8,128)(2,1)S(1)} %get-tuple-element.59), channel_id=1, source_target_pairs={{0,0},{1,16},{2,2},{3,18},{4,4},{5,20},{6,6},{7,22},{8,8},{9,24},{... | collective-permute-start | bytes 516104 | tf_op jit(solution)/shard_map/ppermute | solution.py:252
  11.4 3.8 %collective-permute-start.7 = (bf16[48,1792]{1,0:T(8,128)(2,1)S(1)}, bf16[48,1792]{1,0:T(8,128)(2,1)S(1)}, u32[]{:S(2)}, u32[]{:S(2)}) collective-permute-start(bf16[48,1792]{1,0:T(8,128)(2,1)S(1)} %get-tuple-element.63), channel_id=1, source_target_pairs={{0,4},{1,20},{2,14},{3,30},{4,8},{5,24},{6,2},{7,18},{8,12},{9,28}... | collective-permute-start | bytes 516104 | tf_op jit(solution)/shard_map/ppermute | solution.py:252
  15.2 5.7 %collective-permute-start.8 = (bf16[48,1792]{1,0:T(8,128)(2,1)S(1)}, bf16[48,1792]{1,0:T(8,128)(2,1)S(1)}, u32[]{:S(2)}, u32[]{:S(2)}) collective-permute-start(bf16[48,1792]{1,0:T(8,128)(2,1)S(1)} %get-tuple-element.64), channel_id=1, source_target_pairs={{0,14},{1,30},{2,4},{3,20},{4,2},{5,18},{6,8},{7,24},{8,6},{9,22},... | collective-permute-start | bytes 516104 | tf_op jit(solution)/shard_map/ppermute | solution.py:252
  25.6 2.8 %collective-permute-done.8.refs_2_ = bf16[48,1792]{1,0:T(8,128)(2,1)S(1)} collective-permute-done((bf16[48,1792]{1,0:T(8,128)(2,1)S(1)}, bf16[48,1792]{1,0:T(8,128)(2,1)S(1)}, u32[]{:S(2)}, u32[]{:S(2)}) %collective-permute-start.8) | collective-permute-done | bytes 172064 | tf_op jit(solution)/shard_map/ppermute | solution.py:252
  28.4 3.4 %collective-permute-done.6.refs_0_ = bf16[48,1792]{1,0:T(8,128)(2,1)S(1)} collective-permute-done((bf16[48,1792]{1,0:T(8,128)(2,1)S(1)}, bf16[48,1792]{1,0:T(8,128)(2,1)S(1)}, u32[]{:S(2)}, u32[]{:S(2)}) %collective-permute-start.6) | collective-permute-done | bytes 172064 | tf_op jit(solution)/shard_map/ppermute | solution.py:252
  31.9 2.1 %collective-permute-start.9 = (bf16[96,3584]{1,0:T(8,128)(2,1)S(1)}, bf16[96,3584]{1,0:T(8,128)(2,1)S(1)}, u32[]{:S(2)}, u32[]{:S(2)}) collective-permute-start(bf16[96,3584]{1,0:T(8,128)(2,1)S(1)} %join.2.refs_0_), channel_id=1, source_target_pairs={{0,2},{1,3},{2,0},{3,1},{4,6},{5,7},{6,4},{7,5},{8,10},{9,11},{10,... | collective-permute-start | bytes 2064392 | tf_op jit(solution)/shard_map/ppermute | solution.py:56
  34.0 4.1 %collective-permute-start.13 = (bf16[96,1792]{1,0:T(8,128)(2,1)S(1)}, bf16[96,1792]{1,0:T(8,128)(2,1)S(1)}, u32[]{:S(2)}, u32[]{:S(2)}) collective-permute-start(bf16[96,1792]{1,0:T(8,128)(2,1)S(1)} %get-tuple-element.76), channel_id=1, source_target_pairs={{0,0},{1,16},{2,2},{3,18},{4,4},{5,20},{6,6},{7,22},{8,8},{9,24},{... | collective-permute-start | bytes 1032200 | tf_op jit(solution)/shard_map/ppermute | solution.py:252
  38.2 3.7 %collective-permute-start.10 = (bf16[96,1792]{1,0:T(8,128)(2,1)S(1)}, bf16[96,1792]{1,0:T(8,128)(2,1)S(1)}, u32[]{:S(2)}, u32[]{:S(2)}) collective-permute-start(bf16[96,1792]{1,0:T(8,128)(2,1)S(1)} %get-tuple-element.73), channel_id=1, source_target_pairs={{0,10},{1,26},{2,8},{3,24},{4,14},{5,30},{6,12},{7,28},{8,2},{9,18... | collective-permute-start | bytes 1032200 | tf_op jit(solution)/shard_map/ppermute | solution.py:252
  41.9 4.0 %collective-permute-start.11 = (bf16[96,1792]{1,0:T(8,128)(2,1)S(1)}, bf16[96,1792]{1,0:T(8,128)(2,1)S(1)}, u32[]{:S(2)}, u32[]{:S(2)}) collective-permute-start(bf16[96,1792]{1,0:T(8,128)(2,1)S(1)} %get-tuple-element.74), channel_id=1, source_target_pairs={{0,4},{1,20},{2,14},{3,30},{4,8},{5,24},{6,2},{7,18},{8,12},{9,28}... | collective-permute-start | bytes 1032200 | tf_op jit(solution)/shard_map/ppermute | solution.py:252
  46.6 10.1 %collective-permute-done.9.refs_2_ = bf16[96,3584]{1,0:T(8,128)(2,1)S(1)} collective-permute-done((bf16[96,3584]{1,0:T(8,128)(2,1)S(1)}, bf16[96,3584]{1,0:T(8,128)(2,1)S(1)}, u32[]{:S(2)}, u32[]{:S(2)}) %collective-permute-start.9) | collective-permute-done | bytes 688160 | tf_op jit(solution)/shard_map/ppermute | solution.py:56
  56.7 3.9 %collective-permute-done.10.refs_0_ = bf16[96,1792]{1,0:T(8,128)(2,1)S(1)} collective-permute-done((bf16[96,1792]{1,0:T(8,128)(2,1)S(1)}, bf16[96,1792]{1,0:T(8,128)(2,1)S(1)}, u32[]{:S(2)}, u32[]{:S(2)}) %collective-permute-start.10) | collective-permute-done | bytes 344096 | tf_op jit(solution)/shard_map/ppermute | solution.py:252
  61.9 4.2 %collective-permute-done.12.refs_2_ = bf16[96,1792]{1,0:T(8,128)(2,1)S(1)} collective-permute-done((bf16[96,1792]{1,0:T(8,128)(2,1)S(1)}, bf16[96,1792]{1,0:T(8,128)(2,1)S(1)}, u32[]{:S(2)}, u32[]{:S(2)}) %collective-permute-start.12) | collective-permute-done | bytes 344096 | tf_op jit(solution)/shard_map/ppermute | solution.py:252
  66.8 2.4 %expert_fwd.1 = (bf16[96,3584]{1,0:T(8,128)(2,1)S(1)}, bf16[96,3584]{1,0:T(8,128)(2,1)S(1)}, bf16[96,3584]{1,0:T(8,128)(2,1)S(1)}, bf16[96,3584]{1,0:T(8,128)(2,1)S(1)}) custom-call(bf16[96,3584]{1,0:T(8,128)(2,1)S(1)} %join.2.refs_0_, bf16[96,3584]{1,0:T(8,128)(2,1)S(1)} %collective-permute-done.16.refs_1_, ...), custom_call_target="tpu_custom_call" | custom-call | flops 2113929216 | tf_op jit(solution)/shard_map/expert_fwd/pallas_call | solution.py:320
  70.7 2.4 %collective-permute-start.22 = (bf16[64,3584]{1,0:T(8,128)(2,1)S(1)}, bf16[64,3584]{1,0:T(8,128)(2,1)S(1)}, u32[]{:S(2)}, u32[]{:S(2)}) collective-permute-start(bf16[64,3584]{1,0:T(8,128)(2,1)S(1)} %bitcast.28), channel_id=1, source_target_pairs={{0,224},{1,225},{2,226},{3,227},{4,228},{5,229},{6,230},{7,231},{8... | collective-permute-start | bytes 1376264 | tf_op jit(solution)/shard_map/ppermute | solution.py:66
  73.1 3.6 %collective-permute-start.21 = (f32[8,128]{1,0:T(8,128)S(1)}, f32[8,128]{1,0:T(8,128)S(1)}, u32[]{:S(2)}, u32[]{:S(2)}) collective-permute-start(f32[8,128]{1,0:T(8,128)S(1)} %get-tuple-element.84), channel_id=1, source_target_pairs={{0,224},{1,225},{2,226},{3,227},{4,228},{5,229},{6,230},{7,231},{8... | collective-permute-start | bytes 12296 | tf_op jit(solution)/shard_map/ppermute | solution.py:66
  76.8 6.6 %collective-permute-done.14.meta_ref = f32[8,128]{1,0:T(8,128)S(1)} collective-permute-done((f32[8,128]{1,0:T(8,128)S(1)}, f32[8,128]{1,0:T(8,128)S(1)}, u32[]{:S(2)}, u32[]{:S(2)}) %collective-permute-start.14) | collective-permute-done | bytes 4128 | tf_op jit(solution)/shard_map/ppermute | solution.py:66
  83.4 13.5 %collective-permute-done.20.refs_2_ = bf16[192,3584]{1,0:T(8,128)(2,1)S(1)} collective-permute-done((bf16[192,3584]{1,0:T(8,128)(2,1)S(1)}, bf16[192,3584]{1,0:T(8,128)(2,1)S(1)}, u32[]{:S(2)}, u32[]{:S(2)}) %collective-permute-start.20) | collective-permute-done | bytes 1376288 | tf_op jit(solution)/shard_map/ppermute | solution.py:56
  97.6 2.2 %collective-permute-start.27 = (bf16[96,3584]{1,0:T(8,128)(2,1)S(1)}, bf16[96,3584]{1,0:T(8,128)(2,1)S(1)}, u32[]{:S(2)}, u32[]{:S(2)}) collective-permute-start(bf16[96,3584]{1,0:T(8,128)(2,1)S(1)} %chip_sum.3), channel_id=1, source_target_pairs={{0,2},{1,3},{2,0},{3,1},{4,6},{5,7},{6,4},{7,5},{8,10},{9,11},{10,... | collective-permute-start | bytes 2064392 | tf_op jit(solution)/shard_map/ppermute | solution.py:56
  100.0 2.0 %collective-permute-done.19.refs_1_ = bf16[192,3584]{1,0:T(8,128)(2,1)S(1)} collective-permute-done((bf16[192,3584]{1,0:T(8,128)(2,1)S(1)}, bf16[192,3584]{1,0:T(8,128)(2,1)S(1)}, u32[]{:S(2)}, u32[]{:S(2)}) %collective-permute-start.19) | collective-permute-done | bytes 1376288 | tf_op jit(solution)/shard_map/ppermute | solution.py:51
  102.0 5.0 %expert_bwd.1 = (bf16[96,3584]{1,0:T(8,128)(2,1)S(1)}, bf16[96,3584]{1,0:T(8,128)(2,1)S(1)}, bf16[48,3584]{1,0:T(8,128)(2,1)S(1)}, bf16[48,3584]{1,0:T(8,128)(2,...) custom-call(bf16[192,3584]{1,0:T(8,128)(2,1)S(1)} %join.3.refs_0_, ...), custom_call_target="tpu_custom_call" | custom-call | flops 4227858432 | tf_op jit(solution)/shard_map/expert_bwd/pallas_call | solution.py:326
  108.8 2.1 %collective-permute-start.29 = (bf16[48,3584]{1,0:T(8,128)(2,1)S(1)}, bf16[48,3584]{1,0:T(8,128)(2,1)S(1)}, u32[]{:S(2)}, u32[]{:S(2)}) collective-permute-start(bf16[48,3584]{1,0:T(8,128)(2,1)S(1)} %chip_sum.4), channel_id=1, source_target_pairs={{0,2},{1,3},{2,0},{3,1},{4,6},{5,7},{6,4},{7,5},{8,10},{9,11},{10,... | collective-permute-start | bytes 1032200 | tf_op jit(solution)/shard_map/ppermute | solution.py:56
  111.0 4.5 %collective-permute-done.27.c = bf16[96,3584]{1,0:T(8,128)(2,1)S(1)} collective-permute-done((bf16[96,3584]{1,0:T(8,128)(2,1)S(1)}, bf16[96,3584]{1,0:T(8,128)(2,1)S(1)}, u32[]{:S(2)}, u32[]{:S(2)}) %collective-permute-start.27) | collective-permute-done | bytes 688160 | tf_op jit(solution)/shard_map/ppermute | solution.py:56
  116.5 10.1 %collective-permute-done.29.c = bf16[48,3584]{1,0:T(8,128)(2,1)S(1)} collective-permute-done((bf16[48,3584]{1,0:T(8,128)(2,1)S(1)}, bf16[48,3584]{1,0:T(8,128)(2,1)S(1)}, u32[]{:S(2)}, u32[]{:S(2)}) %collective-permute-start.29) | collective-permute-done | bytes 344096 | tf_op jit(solution)/shard_map/ppermute | solution.py:56
  128.8 9.3 %collective-permute-start.31 = (bf16[48,1792]{1,0:T(8,128)(2,1)S(1)}, bf16[48,1792]{1,0:T(8,128)(2,1)S(1)}, u32[]{:S(2)}, u32[]{:S(2)}) collective-permute-start(bf16[48,1792]{1,0:T(8,128)(2,1)S(1)} %get-tuple-element.99), channel_id=1, source_target_pairs={{14,32},{30,33},{4,34},{20,35},{2,36},{18,37},{8,38},{24,39},{6,40... | collective-permute-start | bytes 516104 | tf_op jit(solution)/shard_map/ppermute | solution.py:66
  138.3 1.5 collective-permute-start.36
  139.8 3.0 %collective-permute-start.32 = (bf16[48,1792]{1,0:T(8,128)(2,1)S(1)}, bf16[48,1792]{1,0:T(8,128)(2,1)S(1)}, u32[]{:S(2)}, u32[]{:S(2)}) collective-permute-start(bf16[48,1792]{1,0:T(8,128)(2,1)S(1)} %get-tuple-element.100), channel_id=1, source_target_pairs={{0,32},{16,33},{2,34},{18,35},{4,36},{20,37},{6,38},{22,39},{8,40}... | collective-permute-start | bytes 516104 | tf_op jit(solution)/shard_map/ppermute | solution.py:66
  142.9 3.9 %collective-permute-start.38 = (bf16[48,1792]{1,0:T(8,128)(2,1)S(1)}, bf16[48,1792]{1,0:T(8,128)(2,1)S(1)}, u32[]{:S(2)}, u32[]{:S(2)}) collective-permute-start(bf16[48,1792]{1,0:T(8,128)(2,1)S(1)} %get-tuple-element.108), channel_id=1, source_target_pairs={{14,224},{30,225},{4,226},{20,227},{2,228},{18,229},{8,230},{24,23... | collective-permute-start | bytes 516104 | tf_op jit(solution)/shard_map/ppermute | solution.py:66
  146.9 3.5 %collective-permute-start.39 = (bf16[48,1792]{1,0:T(8,128)(2,1)S(1)}, bf16[48,1792]{1,0:T(8,128)(2,1)S(1)}, u32[]{:S(2)}, u32[]{:S(2)}) collective-permute-start(bf16[48,1792]{1,0:T(8,128)(2,1)S(1)} %get-tuple-element.109), channel_id=1, source_target_pairs={{0,224},{16,225},{2,226},{18,227},{4,228},{20,229},{6,230},{22,231... | collective-permute-start | bytes 516104 | tf_op jit(solution)/shard_map/ppermute | solution.py:66
  152.9 2.2 %collective-permute-done.38.m2 = bf16[48,1792]{1,0:T(8,128)(2,1)S(1)} collective-permute-done((bf16[48,1792]{1,0:T(8,128)(2,1)S(1)}, bf16[48,1792]{1,0:T(8,128)(2,1)S(1)}, u32[]{:S(2)}, u32[]{:S(2)}) %collective-permute-start.38) | collective-permute-done | bytes 172064 | tf_op jit(solution)/shard_map/ppermute | solution.py:66
  155.1 3.9 %collective-permute-done.39.m3 = bf16[48,1792]{1,0:T(8,128)(2,1)S(1)} collective-permute-done((bf16[48,1792]{1,0:T(8,128)(2,1)S(1)}, bf16[48,1792]{1,0:T(8,128)(2,1)S(1)}, u32[]{:S(2)}, u32[]{:S(2)}) %collective-permute-start.39) | collective-permute-done | bytes 172064 | tf_op jit(solution)/shard_map/ppermute | solution.py:66
  160.2 2.6 %collective-permute-start.40 = (bf16[64,3584]{1,0:T(8,128)(2,1)}, bf16[64,3584]{1,0:T(8,128)(2,1)S(1)}, u32[]{:S(2)}, u32[]{:S(2)}) collective-permute-start(bf16[64,3584]{1,0:T(8,128)(2,1)} %get-tuple-element.111), channel_id=1, source_target_pairs={{0,1},{1,0},{2,3},{3,2},{4,5},{5,4},{6,7},{7,6},{8,9},{9,8},{10,11... | collective-permute-start | bytes 1376264 | tf_op jit(solution)/shard_map/ppermute | solution.py:51
  (90 shorter events, 26.4 us)
Async XLA Ops:
  7.2 14.3 %collective-permute-start.5 = (bf16[48,1792]{1,0:T(8,128)(2,1)S(1)}, bf16[48,1792]{1,0:T(8,128)(2,1)S(1)}, u32[]{:S(2)}, u32[]{:S(2)}) collective-permute-start(bf16[48,1792]{1,0:T(8,128)(2,1)S(1)} %get-tuple-element.59), channel_id=1, source_target_pairs={{0,0},{1,16},{2,2},{3,18},{4,4},{5,20},{6,6},{7,22},{8,8},{9,24},{... | collective-permute-start | bytes 516104 | tf_op jit(solution)/shard_map/ppermute | solution.py:252
  11.4 14.1 %collective-permute-start.7 = (bf16[48,1792]{1,0:T(8,128)(2,1)S(1)}, bf16[48,1792]{1,0:T(8,128)(2,1)S(1)}, u32[]{:S(2)}, u32[]{:S(2)}) collective-permute-start(bf16[48,1792]{1,0:T(8,128)(2,1)S(1)} %get-tuple-element.63), channel_id=1, source_target_pairs={{0,4},{1,20},{2,14},{3,30},{4,8},{5,24},{6,2},{7,18},{8,12},{9,28}... | collective-permute-start | bytes 516104 | tf_op jit(solution)/shard_map/ppermute | solution.py:252
  15.2 13.2 %collective-permute-start.8 = (bf16[48,1792]{1,0:T(8,128)(2,1)S(1)}, bf16[48,1792]{1,0:T(8,128)(2,1)S(1)}, u32[]{:S(2)}, u32[]{:S(2)}) collective-permute-start(bf16[48,1792]{1,0:T(8,128)(2,1)S(1)} %get-tuple-element.64), channel_id=1, source_target_pairs={{0,14},{1,30},{2,4},{3,20},{4,2},{5,18},{6,8},{7,24},{8,6},{9,22},... | collective-permute-start | bytes 516104 | tf_op jit(solution)/shard_map/ppermute | solution.py:252
  20.9 10.9 %collective-permute-start.6 = (bf16[48,1792]{1,0:T(8,128)(2,1)S(1)}, bf16[48,1792]{1,0:T(8,128)(2,1)S(1)}, u32[]{:S(2)}, u32[]{:S(2)}) collective-permute-start(bf16[48,1792]{1,0:T(8,128)(2,1)S(1)} %get-tuple-element.62), channel_id=1, source_target_pairs={{0,10},{1,26},{2,8},{3,24},{4,14},{5,30},{6,12},{7,28},{8,2},{9,18... | collective-permute-start | bytes 516104 | tf_op jit(solution)/shard_map/ppermute | solution.py:252
  31.9 24.8 %collective-permute-start.9 = (bf16[96,3584]{1,0:T(8,128)(2,1)S(1)}, bf16[96,3584]{1,0:T(8,128)(2,1)S(1)}, u32[]{:S(2)}, u32[]{:S(2)}) collective-permute-start(bf16[96,3584]{1,0:T(8,128)(2,1)S(1)} %join.2.refs_0_), channel_id=1, source_target_pairs={{0,2},{1,3},{2,0},{3,1},{4,6},{5,7},{6,4},{7,5},{8,10},{9,11},{10,... | collective-permute-start | bytes 2064392 | tf_op jit(solution)/shard_map/ppermute | solution.py:56
  34.0 12.5 %collective-permute-start.13 = (bf16[96,1792]{1,0:T(8,128)(2,1)S(1)}, bf16[96,1792]{1,0:T(8,128)(2,1)S(1)}, u32[]{:S(2)}, u32[]{:S(2)}) collective-permute-start(bf16[96,1792]{1,0:T(8,128)(2,1)S(1)} %get-tuple-element.76), channel_id=1, source_target_pairs={{0,0},{1,16},{2,2},{3,18},{4,4},{5,20},{6,6},{7,22},{8,8},{9,24},{... | collective-permute-start | bytes 1032200 | tf_op jit(solution)/shard_map/ppermute | solution.py:252
  38.2 22.4 %collective-permute-start.10 = (bf16[96,1792]{1,0:T(8,128)(2,1)S(1)}, bf16[96,1792]{1,0:T(8,128)(2,1)S(1)}, u32[]{:S(2)}, u32[]{:S(2)}) collective-permute-start(bf16[96,1792]{1,0:T(8,128)(2,1)S(1)} %get-tuple-element.73), channel_id=1, source_target_pairs={{0,10},{1,26},{2,8},{3,24},{4,14},{5,30},{6,12},{7,28},{8,2},{9,18... | collective-permute-start | bytes 1032200 | tf_op jit(solution)/shard_map/ppermute | solution.py:252
  41.9 20.0 %collective-permute-start.11 = (bf16[96,1792]{1,0:T(8,128)(2,1)S(1)}, bf16[96,1792]{1,0:T(8,128)(2,1)S(1)}, u32[]{:S(2)}, u32[]{:S(2)}) collective-permute-start(bf16[96,1792]{1,0:T(8,128)(2,1)S(1)} %get-tuple-element.74), channel_id=1, source_target_pairs={{0,4},{1,20},{2,14},{3,30},{4,8},{5,24},{6,2},{7,18},{8,12},{9,28}... | collective-permute-start | bytes 1032200 | tf_op jit(solution)/shard_map/ppermute | solution.py:252
  45.9 20.2 %collective-permute-start.12 = (bf16[96,1792]{1,0:T(8,128)(2,1)S(1)}, bf16[96,1792]{1,0:T(8,128)(2,1)S(1)}, u32[]{:S(2)}, u32[]{:S(2)}) collective-permute-start(bf16[96,1792]{1,0:T(8,128)(2,1)S(1)} %get-tuple-element.75), channel_id=1, source_target_pairs={{0,14},{1,30},{2,4},{3,20},{4,2},{5,18},{6,8},{7,24},{8,6},{9,22},... | collective-permute-start | bytes 1032200 | tf_op jit(solution)/shard_map/ppermute | solution.py:252
  46.5 20.2 %collective-permute-start.16 = (bf16[96,3584]{1,0:T(8,128)(2,1)S(1)}, bf16[96,3584]{1,0:T(8,128)(2,1)S(1)}, u32[]{:S(2)}, u32[]{:S(2)}) collective-permute-start(bf16[96,3584]{1,0:T(8,128)(2,1)S(1)} %join.2.refs_0_), channel_id=1, source_target_pairs={{0,1},{1,0},{2,3},{3,2},{4,5},{5,4},{6,7},{7,6},{8,9},{9,8},{10,11... | collective-permute-start | bytes 2064392 | tf_op jit(solution)/shard_map/ppermute | solution.py:51
  56.7 10.0 %collective-permute-start.17 = (bf16[96,3584]{1,0:T(8,128)(2,1)S(1)}, bf16[96,3584]{1,0:T(8,128)(2,1)S(1)}, u32[]{:S(2)}, u32[]{:S(2)}) collective-permute-start(bf16[96,3584]{1,0:T(8,128)(2,1)S(1)} %collective-permute-done.9.refs_2_), channel_id=1, source_target_pairs={{0,1},{1,0},{2,3},{3,2},{4,5},{5,4},{6,7},{7,6},{8,9},{9,8},{10,11... | collective-permute-start | bytes 2064392 | tf_op jit(solution)/shard_map/ppermute | solution.py:51
  66.1 30.8 %collective-permute-start.20 = (bf16[192,3584]{1,0:T(8,128)(2,1)S(1)}, bf16[192,3584]{1,0:T(8,128)(2,1)S(1)}, u32[]{:S(2)}, u32[]{:S(2)}) collective-permute-start(bf16[192,3584]{1,0:T(8,128)(2,1)S(1)} %join.3.refs_0_), channel_id=1, source_target_pairs={{0,2},{1,3},{2,0},{3,1},{4,6},{5,7},{6,4},{7,5},{8,10},{9,11},{10,... | collective-permute-start | bytes 4128776 | tf_op jit(solution)/shard_map/ppermute | solution.py:56
  69.4 14.0 %collective-permute-start.15 = (bf16[64,3584]{1,0:T(8,128)(2,1)S(1)}, bf16[64,3584]{1,0:T(8,128)(2,1)S(1)}, u32[]{:S(2)}, u32[]{:S(2)}) collective-permute-start(bf16[64,3584]{1,0:T(8,128)(2,1)S(1)} %bitcast.23), channel_id=1, source_target_pairs={{0,32},{1,33},{2,34},{3,35},{4,36},{5,37},{6,38},{7,39},{8,40},{9,... | collective-permute-start | bytes 1376264 | tf_op jit(solution)/shard_map/ppermute | solution.py:66
  70.7 12.7 %collective-permute-start.22 = (bf16[64,3584]{1,0:T(8,128)(2,1)S(1)}, bf16[64,3584]{1,0:T(8,128)(2,1)S(1)}, u32[]{:S(2)}, u32[]{:S(2)}) collective-permute-start(bf16[64,3584]{1,0:T(8,128)(2,1)S(1)} %bitcast.28), channel_id=1, source_target_pairs={{0,224},{1,225},{2,226},{3,227},{4,228},{5,229},{6,230},{7,231},{8... | collective-permute-start | bytes 1376264 | tf_op jit(solution)/shard_map/ppermute | solution.py:66
  73.1 10.3 %collective-permute-start.14 = (f32[8,128]{1,0:T(8,128)S(1)}, f32[8,128]{1,0:T(8,128)S(1)}, u32[]{:S(2)}, u32[]{:S(2)}) collective-permute-start(f32[8,128]{1,0:T(8,128)S(1)} %get-tuple-element.77), channel_id=1, source_target_pairs={{0,32},{1,33},{2,34},{3,35},{4,36},{5,37},{6,38},{7,39},{8,40},{9,... | collective-permute-start | bytes 12296 | tf_op jit(solution)/shard_map/ppermute | solution.py:66
  73.1 10.3 %collective-permute-start.21 = (f32[8,128]{1,0:T(8,128)S(1)}, f32[8,128]{1,0:T(8,128)S(1)}, u32[]{:S(2)}, u32[]{:S(2)}) collective-permute-start(f32[8,128]{1,0:T(8,128)S(1)} %get-tuple-element.84), channel_id=1, source_target_pairs={{0,224},{1,225},{2,226},{3,227},{4,228},{5,229},{6,230},{7,231},{8... | collective-permute-start | bytes 12296 | tf_op jit(solution)/shard_map/ppermute | solution.py:66
  97.1 4.9 %collective-permute-start.19 = (bf16[192,3584]{1,0:T(8,128)(2,1)S(1)}, bf16[192,3584]{1,0:T(8,128)(2,1)S(1)}, u32[]{:S(2)}, u32[]{:S(2)}) collective-permute-start(bf16[192,3584]{1,0:T(8,128)(2,1)S(1)} %join.3.refs_0_), channel_id=1, source_target_pairs={{0,1},{1,0},{2,3},{3,2},{4,5},{5,4},{6,7},{7,6},{8,9},{9,8},{10,11... | collective-permute-start | bytes 4128776 | tf_op jit(solution)/shard_map/ppermute | solution.py:51
  97.4 13.6 %collective-permute-start.26 = (bf16[96,3584]{1,0:T(8,128)(2,1)S(1)}, bf16[96,3584]{1,0:T(8,128)(2,1)S(1)}, u32[]{:S(2)}, u32[]{:S(2)}) collective-permute-start(bf16[96,3584]{1,0:T(8,128)(2,1)S(1)} %get-tuple-element.92), channel_id=1, source_target_pairs={{0,1},{1,0},{2,3},{3,2},{4,5},{5,4},{6,7},{7,6},{8,9},{9,8},{10,11... | collective-permute-start | bytes 2064392 | tf_op jit(solution)/shard_map/ppermute | solution.py:51
  97.6 17.9 %collective-permute-start.27 = (bf16[96,3584]{1,0:T(8,128)(2,1)S(1)}, bf16[96,3584]{1,0:T(8,128)(2,1)S(1)}, u32[]{:S(2)}, u32[]{:S(2)}) collective-permute-start(bf16[96,3584]{1,0:T(8,128)(2,1)S(1)} %chip_sum.3), channel_id=1, source_target_pairs={{0,2},{1,3},{2,0},{3,1},{4,6},{5,7},{6,4},{7,5},{8,10},{9,11},{10,... | collective-permute-start | bytes 2064392 | tf_op jit(solution)/shard_map/ppermute | solution.py:56
  107.6 30.5 %collective-permute-start.34 = (bf16[96,3584]{1,0:T(8,128)(2,1)S(1)}, bf16[96,3584]{1,0:T(8,128)(2,1)S(1)}, u32[]{:S(2)}, u32[]{:S(2)}) collective-permute-start(bf16[96,3584]{1,0:T(8,128)(2,1)S(1)} %get-tuple-element.104), channel_id=1, source_target_pairs={{0,1},{1,0},{2,3},{3,2},{4,5},{5,4},{6,7},{7,6},{8,9},{9,8},{10,11... | collective-permute-start | bytes 2064392 | tf_op jit(solution)/shard_map/ppermute | solution.py:51
  108.8 17.8 %collective-permute-start.29 = (bf16[48,3584]{1,0:T(8,128)(2,1)S(1)}, bf16[48,3584]{1,0:T(8,128)(2,1)S(1)}, u32[]{:S(2)}, u32[]{:S(2)}) collective-permute-start(bf16[48,3584]{1,0:T(8,128)(2,1)S(1)} %chip_sum.4), channel_id=1, source_target_pairs={{0,2},{1,3},{2,0},{3,1},{4,6},{5,7},{6,4},{7,5},{8,10},{9,11},{10,... | collective-permute-start | bytes 1032200 | tf_op jit(solution)/shard_map/ppermute | solution.py:56
  115.8 13.0 %collective-permute-start.28 = (bf16[48,1792]{1,0:T(8,128)(2,1)S(1)}, bf16[48,1792]{1,0:T(8,128)(2,1)S(1)}, u32[]{:S(2)}, u32[]{:S(2)}) collective-permute-start(bf16[48,1792]{1,0:T(8,128)(2,1)S(1)} %get-tuple-element.94), channel_id=1, source_target_pairs={{10,32},{26,33},{8,34},{24,35},{14,36},{30,37},{12,38},{28,39},{2,... | collective-permute-start | bytes 516104 | tf_op jit(solution)/shard_map/ppermute | solution.py:66
  126.6 13.2 %collective-permute-start.37 = (bf16[48,3584]{1,0:T(8,128)(2,1)S(1)}, bf16[48,3584]{1,0:T(8,128)(2,1)S(1)}, u32[]{:S(2)}, u32[]{:S(2)}) collective-permute-start(bf16[48,3584]{1,0:T(8,128)(2,1)S(1)} %chip_sum.5), channel_id=1, source_target_pairs={{0,2},{1,3},{2,0},{3,1},{4,6},{5,7},{6,4},{7,5},{8,10},{9,11},{10,... | collective-permute-start | bytes 1032200 | tf_op jit(solution)/shard_map/ppermute | solution.py:56
  128.8 14.2 %collective-permute-start.30 = (bf16[48,1792]{1,0:T(8,128)(2,1)S(1)}, bf16[48,1792]{1,0:T(8,128)(2,1)S(1)}, u32[]{:S(2)}, u32[]{:S(2)}) collective-permute-start(bf16[48,1792]{1,0:T(8,128)(2,1)S(1)} %get-tuple-element.98), channel_id=1, source_target_pairs={{4,32},{20,33},{14,34},{30,35},{8,36},{24,37},{2,38},{18,39},{12,4... | collective-permute-start | bytes 516104 | tf_op jit(solution)/shard_map/ppermute | solution.py:66
  128.8 18.1 %collective-permute-start.31 = (bf16[48,1792]{1,0:T(8,128)(2,1)S(1)}, bf16[48,1792]{1,0:T(8,128)(2,1)S(1)}, u32[]{:S(2)}, u32[]{:S(2)}) collective-permute-start(bf16[48,1792]{1,0:T(8,128)(2,1)S(1)} %get-tuple-element.99), channel_id=1, source_target_pairs={{14,32},{30,33},{4,34},{20,35},{2,36},{18,37},{8,38},{24,39},{6,40... | collective-permute-start | bytes 516104 | tf_op jit(solution)/shard_map/ppermute | solution.py:66
  138.2 13.4 %collective-permute-start.35 = (bf16[48,1792]{1,0:T(8,128)(2,1)S(1)}, bf16[48,1792]{1,0:T(8,128)(2,1)S(1)}, u32[]{:S(2)}, u32[]{:S(2)}) collective-permute-start(bf16[48,1792]{1,0:T(8,128)(2,1)S(1)} %get-tuple-element.105), channel_id=1, source_target_pairs={{10,224},{26,225},{8,226},{24,227},{14,228},{30,229},{12,230},{28,... | collective-permute-start | bytes 516104 | tf_op jit(solution)/shard_map/ppermute | solution.py:66
  138.3 14.7 %collective-permute-start.36 = (bf16[48,1792]{1,0:T(8,128)(2,1)S(1)}, bf16[48,1792]{1,0:T(8,128)(2,1)S(1)}, u32[]{:S(2)}, u32[]{:S(2)}) collective-permute-start(bf16[48,1792]{1,0:T(8,128)(2,1)S(1)} %get-tuple-element.106), channel_id=1, source_target_pairs={{4,224},{20,225},{14,226},{30,227},{8,228},{24,229},{2,230},{18,23... | collective-permute-start | bytes 516104 | tf_op jit(solution)/shard_map/ppermute | solution.py:66
  139.8 10.6 %collective-permute-start.32 = (bf16[48,1792]{1,0:T(8,128)(2,1)S(1)}, bf16[48,1792]{1,0:T(8,128)(2,1)S(1)}, u32[]{:S(2)}, u32[]{:S(2)}) collective-permute-start(bf16[48,1792]{1,0:T(8,128)(2,1)S(1)} %get-tuple-element.100), channel_id=1, source_target_pairs={{0,32},{16,33},{2,34},{18,35},{4,36},{20,37},{6,38},{22,39},{8,40}... | collective-permute-start | bytes 516104 | tf_op jit(solution)/shard_map/ppermute | solution.py:66
  142.9 12.2 %collective-permute-start.38 = (bf16[48,1792]{1,0:T(8,128)(2,1)S(1)}, bf16[48,1792]{1,0:T(8,128)(2,1)S(1)}, u32[]{:S(2)}, u32[]{:S(2)}) collective-permute-start(bf16[48,1792]{1,0:T(8,128)(2,1)S(1)} %get-tuple-element.108), channel_id=1, source_target_pairs={{14,224},{30,225},{4,226},{20,227},{2,228},{18,229},{8,230},{24,23... | collective-permute-start | bytes 516104 | tf_op jit(solution)/shard_map/ppermute | solution.py:66
  146.9 12.1 %collective-permute-start.39 = (bf16[48,1792]{1,0:T(8,128)(2,1)S(1)}, bf16[48,1792]{1,0:T(8,128)(2,1)S(1)}, u32[]{:S(2)}, u32[]{:S(2)}) collective-permute-start(bf16[48,1792]{1,0:T(8,128)(2,1)S(1)} %get-tuple-element.109), channel_id=1, source_target_pairs={{0,224},{16,225},{2,226},{18,227},{4,228},{20,229},{6,230},{22,231... | collective-permute-start | bytes 516104 | tf_op jit(solution)/shard_map/ppermute | solution.py:66
  150.9 11.9 %collective-permute-start.33 = (bf16[64,3584]{1,0:T(8,128)(2,1)S(1)}, bf16[64,3584]{1,0:T(8,128)(2,1)S(1)}, u32[]{:S(2)}, u32[]{:S(2)}) collective-permute-start(bf16[64,3584]{1,0:T(8,128)(2,1)S(1)} %get-tuple-element.102), channel_id=1, source_target_pairs={{0,1},{1,0},{2,3},{3,2},{4,5},{5,4},{6,7},{7,6},{8,9},{9,8},{10,11... | collective-permute-start | bytes 1376264 | tf_op jit(solution)/shard_map/ppermute | solution.py:51
  160.2 4.2 %collective-permute-start.40 = (bf16[64,3584]{1,0:T(8,128)(2,1)}, bf16[64,3584]{1,0:T(8,128)(2,1)S(1)}, u32[]{:S(2)}, u32[]{:S(2)}) collective-permute-start(bf16[64,3584]{1,0:T(8,128)(2,1)} %get-tuple-element.111), channel_id=1, source_target_pairs={{0,1},{1,0},{2,3},{3,2},{4,5},{5,4},{6,7},{7,6},{8,9},{9,8},{10,11... | collective-permute-start | bytes 1376264 | tf_op jit(solution)/shard_map/ppermute | solution.py:51
  (21 other events, 148.6 us)

commit v6 on v5

--- a/solution.py
+++ b/solution.py
@@ -104,12 +104,10 @@
     return jnp.where((line >> 2) == core, row, -1)
 
 
-def dispatch_kernel(me_ref, own_ids, other_ids, gates_ref, *refs):
+def dispatch_kernel(me_ref, own_ids, other_ids, *refs):
     tokens, meta_ref, outs = refs[: -STEPS - 1], refs[-STEPS - 1], refs[-STEPS:]
     row = token_rows(me_ref, own_ids, other_ids)
-    gates = jnp.concatenate([gates_ref[...], gates_ref[...]], axis=1)
-    which = lax.broadcasted_iota(jnp.int32, (8, 2 * TOK), 0)
-    meta_ref[...] = jnp.where(which == 0, row.astype(F32), jnp.where(which == 1, gates, 0.0))
+    meta_ref[...] = jnp.broadcast_to(row.astype(F32), meta_ref.shape)
     pick = (lax.broadcasted_iota(jnp.int32, (ROWS, 2 * TOK), 0) == row).astype(BF)
     width = 256
     for k in range(len(tokens) // 2):
@@ -124,6 +122,12 @@
                 rows = slice(s * 2 * CAP, (s + 1) * 2 * CAP)
                 block = jnp.concatenate([parts[0][rows], parts[1][rows]], axis=0)
                 outs[s][k * MSG : (k + 1) * MSG, j * width : (j + 1) * width] = block.astype(BF)
+
+
+def meta_kernel(rows, gates_ref, o):
+    gates = jnp.concatenate([gates_ref[...], gates_ref[...]], axis=1)
+    which = lax.broadcasted_iota(jnp.int32, o.shape, 0)
+    o[...] = jnp.where(which == 0, rows[...], gates)
 
 
 def join_kernel(*refs):
@@ -237,10 +241,15 @@
     return lax.optimization_barrier((value, earlier))[0]
 
 
-def dispatch(me, own_ids, other_ids, gates, *tokens):
+def with_gates(rows, gates):
+    (meta,) = call(meta_kernel, [shape(8, 2 * TOK, kind=F32)], 2, "meta")(rows, gates)
+    return meta
+
+
+def dispatch(me, own_ids, other_ids, *tokens):
     outs = [shape(8, 2 * TOK, kind=F32)] + [shape(MSG * (len(tokens) // 2), HALF)] * STEPS
-    meta, *messages = call(dispatch_kernel, outs, 3 + len(tokens), "dispatch", smem=1)(
-        me, own_ids, other_ids, gates, *tokens
+    meta, *messages = call(dispatch_kernel, outs, 2 + len(tokens), "dispatch", smem=1)(
+        me, own_ids, other_ids, *tokens
     )
     return meta, messages
 
@@ -298,10 +307,10 @@
     other_a, x_a_other = other_core(ids_a), other_core(x_a)
     others_b = other_core(ids_b), other_core(x_b), other_core(g_b)
     me_a = after(me, *others_b)
-    meta_a, sent_a = dispatch(me_a, ids_a, other_a, gates_a, x_a, x_a_other)
+    meta_a, sent_a = dispatch(me_a, ids_a, other_a, x_a, x_a_other)
     got_a = send(sent_a, range(STEPS))
     late = after(ids_b, got_a[3])
-    meta_b, sent_b = dispatch(me, late, others_b[0], gates_b, x_b, others_b[1], g_b, others_b[2])
+    meta_b, sent_b = dispatch(me, late, others_b[0], x_b, others_b[1], g_b, others_b[2])
     got_b = send(after(sent_b, *got_a[1:]), range(STEPS))
 
     own_a = join(after(got_a, meta_b))
@@ -312,8 +321,8 @@
     x_a, g_b, meta_a, meta_b = after((x_a, g_b, meta_a, meta_b), across_a, own_b)
     base_a = to_section(x_a, 1, same)
     base_b = to_section(g_b, -1, same)
-    meta_a = to_section(meta_a, 1, same)
-    meta_b = to_section(meta_b, -1, same)
+    meta_a = to_section(with_gates(meta_a, gates_a), 1, same)
+    meta_b = to_section(with_gates(meta_b, gates_b), -1, same)
 
     outs = [shape(ROWS, D)] * 4
     work = 6 * 384 * D * HID

time: 167 us -> 166 us (level)
  no operation moved by 1% of the time
where the time goes in v6:
time: 166 us; the launch traced here: 165 us
  waiting for transfers between devices  74.7 us (45%)
  starting transfers between devices  71.4 us (43%)
  Pallas kernels  13.4 us (8%)
  local copies, waits for them, and re-layouts  4.4 us (3%)
    ppermute x5, waiting for transfers between devices, other_chip(): return lax.ppermute(block, 'expert', pairs)  38.1 us
    ppermute x12, starting transfers between devices, to_section(): return lax.ppermute(block, ('pipe', 'expert'), route)  29.5 us
    ppermute x8, starting transfers between devices, send(): return [lax.ppermute(m, 'expert', near(s)) for m, s in zip(messages, steps)]  26.8 us
    ppermute x8, waiting for transfers between devices, send(): return [lax.ppermute(m, 'expert', near(s)) for m, s in zip(messages, steps)]  16.3 us
    ppermute x12, waiting for transfers between devices, to_section(): return lax.ppermute(block, ('pipe', 'expert'), route)  14.7 us
    ppermute x5, starting transfers between devices, other_chip(): return lax.ppermute(block, 'expert', pairs)  8.14 us
    ppermute x16, starting transfers between devices, other_core(): return lax.ppermute(block, 'expert', pairs)  6.99 us
    ppermute x16, waiting for transfers between devices, other_core(): return lax.ppermute(block, 'expert', pairs)  5.68 us
  transfers between devices with their start and end apart: 41, of which 19 were waited for; matrix products, arithmetic and copies ran while one was open for 0% of the time, Pallas kernels for 7%

profile of v6, /device:TPU:9, one launch (start us, length us, event | category | flops | bytes accessed | tf_op | source)
XLA Modules:
  0.0 164.9 jit_solution(7790468657242223064)
XLA Ops:
  2.4 1.9 %collective-permute-done.other_ids = s32[1,64]{1,0:T(1,128)S(1)} collective-permute-done((s32[1,64]{1,0:T(1,128)}, s32[1,64]{1,0:T(1,128)S(1)}, u32[]{:S(2)}, u32[]{:S(2)}) %collective-permute-start) | collective-permute-done | bytes 288 | tf_op jit(solution)/shard_map/ppermute | solution.py:51
  6.6 4.2 %collective-permute-start.5 = (bf16[48,1792]{1,0:T(8,128)(2,1)S(1)}, bf16[48,1792]{1,0:T(8,128)(2,1)S(1)}, u32[]{:S(2)}, u32[]{:S(2)}) collective-permute-start(bf16[48,1792]{1,0:T(8,128)(2,1)S(1)} %get-tuple-element.59), channel_id=1, source_target_pairs={{0,0},{1,16},{2,2},{3,18},{4,4},{5,20},{6,6},{7,22},{8,8},{9,24},{... | collective-permute-start | bytes 516104 | tf_op jit(solution)/shard_map/ppermute | solution.py:261
  10.8 3.8 %collective-permute-start.7 = (bf16[48,1792]{1,0:T(8,128)(2,1)S(1)}, bf16[48,1792]{1,0:T(8,128)(2,1)S(1)}, u32[]{:S(2)}, u32[]{:S(2)}) collective-permute-start(bf16[48,1792]{1,0:T(8,128)(2,1)S(1)} %get-tuple-element.63), channel_id=1, source_target_pairs={{0,4},{1,20},{2,14},{3,30},{4,8},{5,24},{6,2},{7,18},{8,12},{9,28}... | collective-permute-start | bytes 516104 | tf_op jit(solution)/shard_map/ppermute | solution.py:261
  14.5 5.7 %collective-permute-start.8 = (bf16[48,1792]{1,0:T(8,128)(2,1)S(1)}, bf16[48,1792]{1,0:T(8,128)(2,1)S(1)}, u32[]{:S(2)}, u32[]{:S(2)}) collective-permute-start(bf16[48,1792]{1,0:T(8,128)(2,1)S(1)} %get-tuple-element.64), channel_id=1, source_target_pairs={{0,14},{1,30},{2,4},{3,20},{4,2},{5,18},{6,8},{7,24},{8,6},{9,22},... | collective-permute-start | bytes 516104 | tf_op jit(solution)/shard_map/ppermute | solution.py:261
  24.3 3.5 %collective-permute-done.8.refs_2_ = bf16[48,1792]{1,0:T(8,128)(2,1)S(1)} collective-permute-done((bf16[48,1792]{1,0:T(8,128)(2,1)S(1)}, bf16[48,1792]{1,0:T(8,128)(2,1)S(1)}, u32[]{:S(2)}, u32[]{:S(2)}) %collective-permute-start.8) | collective-permute-done | bytes 172064 | tf_op jit(solution)/shard_map/ppermute | solution.py:261
  27.8 3.4 %collective-permute-done.6.refs_0_ = bf16[48,1792]{1,0:T(8,128)(2,1)S(1)} collective-permute-done((bf16[48,1792]{1,0:T(8,128)(2,1)S(1)}, bf16[48,1792]{1,0:T(8,128)(2,1)S(1)}, u32[]{:S(2)}, u32[]{:S(2)}) %collective-permute-start.6) | collective-permute-done | bytes 172064 | tf_op jit(solution)/shard_map/ppermute | solution.py:261
  31.3 2.1 %collective-permute-start.9 = (bf16[96,3584]{1,0:T(8,128)(2,1)S(1)}, bf16[96,3584]{1,0:T(8,128)(2,1)S(1)}, u32[]{:S(2)}, u32[]{:S(2)}) collective-permute-start(bf16[96,3584]{1,0:T(8,128)(2,1)S(1)} %join.2.refs_0_), channel_id=1, source_target_pairs={{0,2},{1,3},{2,0},{3,1},{4,6},{5,7},{6,4},{7,5},{8,10},{9,11},{10,... | collective-permute-start | bytes 2064392 | tf_op jit(solution)/shard_map/ppermute | solution.py:56
  33.3 4.2 %collective-permute-start.13 = (bf16[96,1792]{1,0:T(8,128)(2,1)S(1)}, bf16[96,1792]{1,0:T(8,128)(2,1)S(1)}, u32[]{:S(2)}, u32[]{:S(2)}) collective-permute-start(bf16[96,1792]{1,0:T(8,128)(2,1)S(1)} %get-tuple-element.76), channel_id=1, source_target_pairs={{0,0},{1,16},{2,2},{3,18},{4,4},{5,20},{6,6},{7,22},{8,8},{9,24},{... | collective-permute-start | bytes 1032200 | tf_op jit(solution)/shard_map/ppermute | solution.py:261
  37.5 3.7 %collective-permute-start.10 = (bf16[96,1792]{1,0:T(8,128)(2,1)S(1)}, bf16[96,1792]{1,0:T(8,128)(2,1)S(1)}, u32[]{:S(2)}, u32[]{:S(2)}) collective-permute-start(bf16[96,1792]{1,0:T(8,128)(2,1)S(1)} %get-tuple-element.73), channel_id=1, source_target_pairs={{0,10},{1,26},{2,8},{3,24},{4,14},{5,30},{6,12},{7,28},{8,2},{9,18... | collective-permute-start | bytes 1032200 | tf_op jit(solution)/shard_map/ppermute | solution.py:261
  41.2 4.0 %collective-permute-start.11 = (bf16[96,1792]{1,0:T(8,128)(2,1)S(1)}, bf16[96,1792]{1,0:T(8,128)(2,1)S(1)}, u32[]{:S(2)}, u32[]{:S(2)}) collective-permute-start(bf16[96,1792]{1,0:T(8,128)(2,1)S(1)} %get-tuple-element.74), channel_id=1, source_target_pairs={{0,4},{1,20},{2,14},{3,30},{4,8},{5,24},{6,2},{7,18},{8,12},{9,28}... | collective-permute-start | bytes 1032200 | tf_op jit(solution)/shard_map/ppermute | solution.py:261
  45.9 10.2 %collective-permute-done.9.refs_2_ = bf16[96,3584]{1,0:T(8,128)(2,1)S(1)} collective-permute-done((bf16[96,3584]{1,0:T(8,128)(2,1)S(1)}, bf16[96,3584]{1,0:T(8,128)(2,1)S(1)}, u32[]{:S(2)}, u32[]{:S(2)}) %collective-permute-start.9) | collective-permute-done | bytes 688160 | tf_op jit(solution)/shard_map/ppermute | solution.py:56
  56.0 3.9 %collective-permute-done.10.refs_0_ = bf16[96,1792]{1,0:T(8,128)(2,1)S(1)} collective-permute-done((bf16[96,1792]{1,0:T(8,128)(2,1)S(1)}, bf16[96,1792]{1,0:T(8,128)(2,1)S(1)}, u32[]{:S(2)}, u32[]{:S(2)}) %collective-permute-start.10) | collective-permute-done | bytes 344096 | tf_op jit(solution)/shard_map/ppermute | solution.py:261
  61.2 4.2 %collective-permute-done.12.refs_2_ = bf16[96,1792]{1,0:T(8,128)(2,1)S(1)} collective-permute-done((bf16[96,1792]{1,0:T(8,128)(2,1)S(1)}, bf16[96,1792]{1,0:T(8,128)(2,1)S(1)}, u32[]{:S(2)}, u32[]{:S(2)}) %collective-permute-start.12) | collective-permute-done | bytes 344096 | tf_op jit(solution)/shard_map/ppermute | solution.py:261
  66.1 2.4 %expert_fwd.1 = (bf16[96,3584]{1,0:T(8,128)(2,1)S(1)}, bf16[96,3584]{1,0:T(8,128)(2,1)S(1)}, bf16[96,3584]{1,0:T(8,128)(2,1)S(1)}, bf16[96,3584]{1,0:T(8,128)(2,1)S(1)}) custom-call(bf16[96,3584]{1,0:T(8,128)(2,1)S(1)} %join.2.refs_0_, bf16[96,3584]{1,0:T(8,128)(2,1)S(1)} %collective-permute-done.16.refs_1_, ...), custom_call_target="tpu_custom_call" | custom-call | flops 2113929216 | tf_op jit(solution)/shard_map/expert_fwd/pallas_call | solution.py:329
  70.0 2.3 %collective-permute-start.22 = (bf16[64,3584]{1,0:T(8,128)(2,1)S(1)}, bf16[64,3584]{1,0:T(8,128)(2,1)S(1)}, u32[]{:S(2)}, u32[]{:S(2)}) collective-permute-start(bf16[64,3584]{1,0:T(8,128)(2,1)S(1)} %bitcast.28), channel_id=1, source_target_pairs={{0,224},{1,225},{2,226},{3,227},{4,228},{5,229},{6,230},{7,231},{8... | collective-permute-start | bytes 1376264 | tf_op jit(solution)/shard_map/ppermute | solution.py:66
  72.6 3.6 %collective-permute-start.21 = (f32[8,128]{1,0:T(8,128)S(1)}, f32[8,128]{1,0:T(8,128)S(1)}, u32[]{:S(2)}, u32[]{:S(2)}) collective-permute-start(f32[8,128]{1,0:T(8,128)S(1)} %meta.3), channel_id=1, source_target_pairs={{0,224},{1,225},{2,226},{3,227},{4,228},{5,229},{6,230},{7,231},{8... | collective-permute-start | bytes 12296 | tf_op jit(solution)/shard_map/ppermute | solution.py:66
  76.3 6.4 %collective-permute-done.14.meta_ref = f32[8,128]{1,0:T(8,128)S(1)} collective-permute-done((f32[8,128]{1,0:T(8,128)S(1)}, f32[8,128]{1,0:T(8,128)S(1)}, u32[]{:S(2)}, u32[]{:S(2)}) %collective-permute-start.14) | collective-permute-done | bytes 4128 | tf_op jit(solution)/shard_map/ppermute | solution.py:66
  82.7 13.5 %collective-permute-done.20.refs_2_ = bf16[192,3584]{1,0:T(8,128)(2,1)S(1)} collective-permute-done((bf16[192,3584]{1,0:T(8,128)(2,1)S(1)}, bf16[192,3584]{1,0:T(8,128)(2,1)S(1)}, u32[]{:S(2)}, u32[]{:S(2)}) %collective-permute-start.20) | collective-permute-done | bytes 1376288 | tf_op jit(solution)/shard_map/ppermute | solution.py:56
  96.9 2.2 %collective-permute-start.27 = (bf16[96,3584]{1,0:T(8,128)(2,1)S(1)}, bf16[96,3584]{1,0:T(8,128)(2,1)S(1)}, u32[]{:S(2)}, u32[]{:S(2)}) collective-permute-start(bf16[96,3584]{1,0:T(8,128)(2,1)S(1)} %chip_sum.3), channel_id=1, source_target_pairs={{0,2},{1,3},{2,0},{3,1},{4,6},{5,7},{6,4},{7,5},{8,10},{9,11},{10,... | collective-permute-start | bytes 2064392 | tf_op jit(solution)/shard_map/ppermute | solution.py:56
  99.3 2.0 %collective-permute-done.19.refs_1_ = bf16[192,3584]{1,0:T(8,128)(2,1)S(1)} collective-permute-done((bf16[192,3584]{1,0:T(8,128)(2,1)S(1)}, bf16[192,3584]{1,0:T(8,128)(2,1)S(1)}, u32[]{:S(2)}, u32[]{:S(2)}) %collective-permute-start.19) | collective-permute-done | bytes 1376288 | tf_op jit(solution)/shard_map/ppermute | solution.py:51
  101.3 5.0 %expert_bwd.1 = (bf16[96,3584]{1,0:T(8,128)(2,1)S(1)}, bf16[96,3584]{1,0:T(8,128)(2,1)S(1)}, bf16[48,3584]{1,0:T(8,128)(2,1)S(1)}, bf16[48,3584]{1,0:T(8,128)(2,...) custom-call(bf16[192,3584]{1,0:T(8,128)(2,1)S(1)} %join.3.refs_0_, ...), custom_call_target="tpu_custom_call" | custom-call | flops 4227858432 | tf_op jit(solution)/shard_map/expert_bwd/pallas_call | solution.py:335
  108.1 2.1 %collective-permute-start.29 = (bf16[48,3584]{1,0:T(8,128)(2,1)S(1)}, bf16[48,3584]{1,0:T(8,128)(2,1)S(1)}, u32[]{:S(2)}, u32[]{:S(2)}) collective-permute-start(bf16[48,3584]{1,0:T(8,128)(2,1)S(1)} %chip_sum.4), channel_id=1, source_target_pairs={{0,2},{1,3},{2,0},{3,1},{4,6},{5,7},{6,4},{7,5},{8,10},{9,11},{10,... | collective-permute-start | bytes 1032200 | tf_op jit(solution)/shard_map/ppermute | solution.py:56
  110.3 4.5 %collective-permute-done.27.c = bf16[96,3584]{1,0:T(8,128)(2,1)S(1)} collective-permute-done((bf16[96,3584]{1,0:T(8,128)(2,1)S(1)}, bf16[96,3584]{1,0:T(8,128)(2,1)S(1)}, u32[]{:S(2)}, u32[]{:S(2)}) %collective-permute-start.27) | collective-permute-done | bytes 688160 | tf_op jit(solution)/shard_map/ppermute | solution.py:56
  115.9 10.0 %collective-permute-done.29.c = bf16[48,3584]{1,0:T(8,128)(2,1)S(1)} collective-permute-done((bf16[48,3584]{1,0:T(8,128)(2,1)S(1)}, bf16[48,3584]{1,0:T(8,128)(2,1)S(1)}, u32[]{:S(2)}, u32[]{:S(2)}) %collective-permute-start.29) | collective-permute-done | bytes 344096 | tf_op jit(solution)/shard_map/ppermute | solution.py:56
  128.2 9.2 %collective-permute-start.31 = (bf16[48,1792]{1,0:T(8,128)(2,1)S(1)}, bf16[48,1792]{1,0:T(8,128)(2,1)S(1)}, u32[]{:S(2)}, u32[]{:S(2)}) collective-permute-start(bf16[48,1792]{1,0:T(8,128)(2,1)S(1)} %get-tuple-element.99), channel_id=1, source_target_pairs={{14,32},{30,33},{4,34},{20,35},{2,36},{18,37},{8,38},{24,39},{6,40... | collective-permute-start | bytes 516104 | tf_op jit(solution)/shard_map/ppermute | solution.py:66
  137.6 1.5 collective-permute-start.36
  139.1 3.0 %collective-permute-start.32 = (bf16[48,1792]{1,0:T(8,128)(2,1)S(1)}, bf16[48,1792]{1,0:T(8,128)(2,1)S(1)}, u32[]{:S(2)}, u32[]{:S(2)}) collective-permute-start(bf16[48,1792]{1,0:T(8,128)(2,1)S(1)} %get-tuple-element.100), channel_id=1, source_target_pairs={{0,32},{16,33},{2,34},{18,35},{4,36},{20,37},{6,38},{22,39},{8,40}... | collective-permute-start | bytes 516104 | tf_op jit(solution)/shard_map/ppermute | solution.py:66
  142.2 4.0 %collective-permute-start.38 = (bf16[48,1792]{1,0:T(8,128)(2,1)S(1)}, bf16[48,1792]{1,0:T(8,128)(2,1)S(1)}, u32[]{:S(2)}, u32[]{:S(2)}) collective-permute-start(bf16[48,1792]{1,0:T(8,128)(2,1)S(1)} %get-tuple-element.108), channel_id=1, source_target_pairs={{14,224},{30,225},{4,226},{20,227},{2,228},{18,229},{8,230},{24,23... | collective-permute-start | bytes 516104 | tf_op jit(solution)/shard_map/ppermute | solution.py:66
  146.3 3.5 %collective-permute-start.39 = (bf16[48,1792]{1,0:T(8,128)(2,1)S(1)}, bf16[48,1792]{1,0:T(8,128)(2,1)S(1)}, u32[]{:S(2)}, u32[]{:S(2)}) collective-permute-start(bf16[48,1792]{1,0:T(8,128)(2,1)S(1)} %get-tuple-element.109), channel_id=1, source_target_pairs={{0,224},{16,225},{2,226},{18,227},{4,228},{20,229},{6,230},{22,231... | collective-permute-start | bytes 516104 | tf_op jit(solution)/shard_map/ppermute | solution.py:66
  152.3 2.2 %collective-permute-done.38.m2 = bf16[48,1792]{1,0:T(8,128)(2,1)S(1)} collective-permute-done((bf16[48,1792]{1,0:T(8,128)(2,1)S(1)}, bf16[48,1792]{1,0:T(8,128)(2,1)S(1)}, u32[]{:S(2)}, u32[]{:S(2)}) %collective-permute-start.38) | collective-permute-done | bytes 172064 | tf_op jit(solution)/shard_map/ppermute | solution.py:66
  154.5 3.9 %collective-permute-done.39.m3 = bf16[48,1792]{1,0:T(8,128)(2,1)S(1)} collective-permute-done((bf16[48,1792]{1,0:T(8,128)(2,1)S(1)}, bf16[48,1792]{1,0:T(8,128)(2,1)S(1)}, u32[]{:S(2)}, u32[]{:S(2)}) %collective-permute-start.39) | collective-permute-done | bytes 172064 | tf_op jit(solution)/shard_map/ppermute | solution.py:66
  159.6 2.6 %collective-permute-start.40 = (bf16[64,3584]{1,0:T(8,128)(2,1)}, bf16[64,3584]{1,0:T(8,128)(2,1)S(1)}, u32[]{:S(2)}, u32[]{:S(2)}) collective-permute-start(bf16[64,3584]{1,0:T(8,128)(2,1)} %get-tuple-element.111), channel_id=1, source_target_pairs={{0,1},{1,0},{2,3},{3,2},{4,5},{5,4},{6,7},{7,6},{8,9},{9,8},{10,11... | collective-permute-start | bytes 1376264 | tf_op jit(solution)/shard_map/ppermute | solution.py:51
  (92 shorter events, 25.6 us)
Async XLA Ops:
  6.6 14.3 %collective-permute-start.5 = (bf16[48,1792]{1,0:T(8,128)(2,1)S(1)}, bf16[48,1792]{1,0:T(8,128)(2,1)S(1)}, u32[]{:S(2)}, u32[]{:S(2)}) collective-permute-start(bf16[48,1792]{1,0:T(8,128)(2,1)S(1)} %get-tuple-element.59), channel_id=1, source_target_pairs={{0,0},{1,16},{2,2},{3,18},{4,4},{5,20},{6,6},{7,22},{8,8},{9,24},{... | collective-permute-start | bytes 516104 | tf_op jit(solution)/shard_map/ppermute | solution.py:261
  10.8 13.5 %collective-permute-start.7 = (bf16[48,1792]{1,0:T(8,128)(2,1)S(1)}, bf16[48,1792]{1,0:T(8,128)(2,1)S(1)}, u32[]{:S(2)}, u32[]{:S(2)}) collective-permute-start(bf16[48,1792]{1,0:T(8,128)(2,1)S(1)} %get-tuple-element.63), channel_id=1, source_target_pairs={{0,4},{1,20},{2,14},{3,30},{4,8},{5,24},{6,2},{7,18},{8,12},{9,28}... | collective-permute-start | bytes 516104 | tf_op jit(solution)/shard_map/ppermute | solution.py:261
  14.5 13.2 %collective-permute-start.8 = (bf16[48,1792]{1,0:T(8,128)(2,1)S(1)}, bf16[48,1792]{1,0:T(8,128)(2,1)S(1)}, u32[]{:S(2)}, u32[]{:S(2)}) collective-permute-start(bf16[48,1792]{1,0:T(8,128)(2,1)S(1)} %get-tuple-element.64), channel_id=1, source_target_pairs={{0,14},{1,30},{2,4},{3,20},{4,2},{5,18},{6,8},{7,24},{8,6},{9,22},... | collective-permute-start | bytes 516104 | tf_op jit(solution)/shard_map/ppermute | solution.py:261
  20.3 10.9 %collective-permute-start.6 = (bf16[48,1792]{1,0:T(8,128)(2,1)S(1)}, bf16[48,1792]{1,0:T(8,128)(2,1)S(1)}, u32[]{:S(2)}, u32[]{:S(2)}) collective-permute-start(bf16[48,1792]{1,0:T(8,128)(2,1)S(1)} %get-tuple-element.62), channel_id=1, source_target_pairs={{0,10},{1,26},{2,8},{3,24},{4,14},{5,30},{6,12},{7,28},{8,2},{9,18... | collective-permute-start | bytes 516104 | tf_op jit(solution)/shard_map/ppermute | solution.py:261
  31.3 24.8 %collective-permute-start.9 = (bf16[96,3584]{1,0:T(8,128)(2,1)S(1)}, bf16[96,3584]{1,0:T(8,128)(2,1)S(1)}, u32[]{:S(2)}, u32[]{:S(2)}) collective-permute-start(bf16[96,3584]{1,0:T(8,128)(2,1)S(1)} %join.2.refs_0_), channel_id=1, source_target_pairs={{0,2},{1,3},{2,0},{3,1},{4,6},{5,7},{6,4},{7,5},{8,10},{9,11},{10,... | collective-permute-start | bytes 2064392 | tf_op jit(solution)/shard_map/ppermute | solution.py:56
  33.3 12.5 %collective-permute-start.13 = (bf16[96,1792]{1,0:T(8,128)(2,1)S(1)}, bf16[96,1792]{1,0:T(8,128)(2,1)S(1)}, u32[]{:S(2)}, u32[]{:S(2)}) collective-permute-start(bf16[96,1792]{1,0:T(8,128)(2,1)S(1)} %get-tuple-element.76), channel_id=1, source_target_pairs={{0,0},{1,16},{2,2},{3,18},{4,4},{5,20},{6,6},{7,22},{8,8},{9,24},{... | collective-permute-start | bytes 1032200 | tf_op jit(solution)/shard_map/ppermute | solution.py:261
  37.5 22.4 %collective-permute-start.10 = (bf16[96,1792]{1,0:T(8,128)(2,1)S(1)}, bf16[96,1792]{1,0:T(8,128)(2,1)S(1)}, u32[]{:S(2)}, u32[]{:S(2)}) collective-permute-start(bf16[96,1792]{1,0:T(8,128)(2,1)S(1)} %get-tuple-element.73), channel_id=1, source_target_pairs={{0,10},{1,26},{2,8},{3,24},{4,14},{5,30},{6,12},{7,28},{8,2},{9,18... | collective-permute-start | bytes 1032200 | tf_op jit(solution)/shard_map/ppermute | solution.py:261
  41.2 20.0 %collective-permute-start.11 = (bf16[96,1792]{1,0:T(8,128)(2,1)S(1)}, bf16[96,1792]{1,0:T(8,128)(2,1)S(1)}, u32[]{:S(2)}, u32[]{:S(2)}) collective-permute-start(bf16[96,1792]{1,0:T(8,128)(2,1)S(1)} %get-tuple-element.74), channel_id=1, source_target_pairs={{0,4},{1,20},{2,14},{3,30},{4,8},{5,24},{6,2},{7,18},{8,12},{9,28}... | collective-permute-start | bytes 1032200 | tf_op jit(solution)/shard_map/ppermute | solution.py:261
  45.2 20.2 %collective-permute-start.12 = (bf16[96,1792]{1,0:T(8,128)(2,1)S(1)}, bf16[96,1792]{1,0:T(8,128)(2,1)S(1)}, u32[]{:S(2)}, u32[]{:S(2)}) collective-permute-start(bf16[96,1792]{1,0:T(8,128)(2,1)S(1)} %get-tuple-element.75), channel_id=1, source_target_pairs={{0,14},{1,30},{2,4},{3,20},{4,2},{5,18},{6,8},{7,24},{8,6},{9,22},... | collective-permute-start | bytes 1032200 | tf_op jit(solution)/shard_map/ppermute | solution.py:261
  45.9 20.1 %collective-permute-start.16 = (bf16[96,3584]{1,0:T(8,128)(2,1)S(1)}, bf16[96,3584]{1,0:T(8,128)(2,1)S(1)}, u32[]{:S(2)}, u32[]{:S(2)}) collective-permute-start(bf16[96,3584]{1,0:T(8,128)(2,1)S(1)} %join.2.refs_0_), channel_id=1, source_target_pairs={{0,1},{1,0},{2,3},{3,2},{4,5},{5,4},{6,7},{7,6},{8,9},{9,8},{10,11... | collective-permute-start | bytes 2064392 | tf_op jit(solution)/shard_map/ppermute | solution.py:51
  56.0 10.0 %collective-permute-start.17 = (bf16[96,3584]{1,0:T(8,128)(2,1)S(1)}, bf16[96,3584]{1,0:T(8,128)(2,1)S(1)}, u32[]{:S(2)}, u32[]{:S(2)}) collective-permute-start(bf16[96,3584]{1,0:T(8,128)(2,1)S(1)} %collective-permute-done.9.refs_2_), channel_id=1, source_target_pairs={{0,1},{1,0},{2,3},{3,2},{4,5},{5,4},{6,7},{7,6},{8,9},{9,8},{10,11... | collective-permute-start | bytes 2064392 | tf_op jit(solution)/shard_map/ppermute | solution.py:51
  65.5 30.7 %collective-permute-start.20 = (bf16[192,3584]{1,0:T(8,128)(2,1)S(1)}, bf16[192,3584]{1,0:T(8,128)(2,1)S(1)}, u32[]{:S(2)}, u32[]{:S(2)}) collective-permute-start(bf16[192,3584]{1,0:T(8,128)(2,1)S(1)} %join.3.refs_0_), channel_id=1, source_target_pairs={{0,2},{1,3},{2,0},{3,1},{4,6},{5,7},{6,4},{7,5},{8,10},{9,11},{10,... | collective-permute-start | bytes 4128776 | tf_op jit(solution)/shard_map/ppermute | solution.py:56
  68.7 14.0 %collective-permute-start.15 = (bf16[64,3584]{1,0:T(8,128)(2,1)S(1)}, bf16[64,3584]{1,0:T(8,128)(2,1)S(1)}, u32[]{:S(2)}, u32[]{:S(2)}) collective-permute-start(bf16[64,3584]{1,0:T(8,128)(2,1)S(1)} %bitcast.23), channel_id=1, source_target_pairs={{0,32},{1,33},{2,34},{3,35},{4,36},{5,37},{6,38},{7,39},{8,40},{9,... | collective-permute-start | bytes 1376264 | tf_op jit(solution)/shard_map/ppermute | solution.py:66
  70.0 12.7 %collective-permute-start.22 = (bf16[64,3584]{1,0:T(8,128)(2,1)S(1)}, bf16[64,3584]{1,0:T(8,128)(2,1)S(1)}, u32[]{:S(2)}, u32[]{:S(2)}) collective-permute-start(bf16[64,3584]{1,0:T(8,128)(2,1)S(1)} %bitcast.28), channel_id=1, source_target_pairs={{0,224},{1,225},{2,226},{3,227},{4,228},{5,229},{6,230},{7,231},{8... | collective-permute-start | bytes 1376264 | tf_op jit(solution)/shard_map/ppermute | solution.py:66
  72.5 10.2 %collective-permute-start.14 = (f32[8,128]{1,0:T(8,128)S(1)}, f32[8,128]{1,0:T(8,128)S(1)}, u32[]{:S(2)}, u32[]{:S(2)}) collective-permute-start(f32[8,128]{1,0:T(8,128)S(1)} %meta.2), channel_id=1, source_target_pairs={{0,32},{1,33},{2,34},{3,35},{4,36},{5,37},{6,38},{7,39},{8,40},{9,... | collective-permute-start | bytes 12296 | tf_op jit(solution)/shard_map/ppermute | solution.py:66
  72.6 10.1 %collective-permute-start.21 = (f32[8,128]{1,0:T(8,128)S(1)}, f32[8,128]{1,0:T(8,128)S(1)}, u32[]{:S(2)}, u32[]{:S(2)}) collective-permute-start(f32[8,128]{1,0:T(8,128)S(1)} %meta.3), channel_id=1, source_target_pairs={{0,224},{1,225},{2,226},{3,227},{4,228},{5,229},{6,230},{7,231},{8... | collective-permute-start | bytes 12296 | tf_op jit(solution)/shard_map/ppermute | solution.py:66
  96.4 4.9 %collective-permute-start.19 = (bf16[192,3584]{1,0:T(8,128)(2,1)S(1)}, bf16[192,3584]{1,0:T(8,128)(2,1)S(1)}, u32[]{:S(2)}, u32[]{:S(2)}) collective-permute-start(bf16[192,3584]{1,0:T(8,128)(2,1)S(1)} %join.3.refs_0_), channel_id=1, source_target_pairs={{0,1},{1,0},{2,3},{3,2},{4,5},{5,4},{6,7},{7,6},{8,9},{9,8},{10,11... | collective-permute-start | bytes 4128776 | tf_op jit(solution)/shard_map/ppermute | solution.py:51
  96.7 13.6 %collective-permute-start.26 = (bf16[96,3584]{1,0:T(8,128)(2,1)S(1)}, bf16[96,3584]{1,0:T(8,128)(2,1)S(1)}, u32[]{:S(2)}, u32[]{:S(2)}) collective-permute-start(bf16[96,3584]{1,0:T(8,128)(2,1)S(1)} %get-tuple-element.92), channel_id=1, source_target_pairs={{0,1},{1,0},{2,3},{3,2},{4,5},{5,4},{6,7},{7,6},{8,9},{9,8},{10,11... | collective-permute-start | bytes 2064392 | tf_op jit(solution)/shard_map/ppermute | solution.py:51
  96.9 17.9 %collective-permute-start.27 = (bf16[96,3584]{1,0:T(8,128)(2,1)S(1)}, bf16[96,3584]{1,0:T(8,128)(2,1)S(1)}, u32[]{:S(2)}, u32[]{:S(2)}) collective-permute-start(bf16[96,3584]{1,0:T(8,128)(2,1)S(1)} %chip_sum.3), channel_id=1, source_target_pairs={{0,2},{1,3},{2,0},{3,1},{4,6},{5,7},{6,4},{7,5},{8,10},{9,11},{10,... | collective-permute-start | bytes 2064392 | tf_op jit(solution)/shard_map/ppermute | solution.py:56
  106.9 30.5 %collective-permute-start.34 = (bf16[96,3584]{1,0:T(8,128)(2,1)S(1)}, bf16[96,3584]{1,0:T(8,128)(2,1)S(1)}, u32[]{:S(2)}, u32[]{:S(2)}) collective-permute-start(bf16[96,3584]{1,0:T(8,128)(2,1)S(1)} %get-tuple-element.104), channel_id=1, source_target_pairs={{0,1},{1,0},{2,3},{3,2},{4,5},{5,4},{6,7},{7,6},{8,9},{9,8},{10,11... | collective-permute-start | bytes 2064392 | tf_op jit(solution)/shard_map/ppermute | solution.py:51
  108.1 17.8 %collective-permute-start.29 = (bf16[48,3584]{1,0:T(8,128)(2,1)S(1)}, bf16[48,3584]{1,0:T(8,128)(2,1)S(1)}, u32[]{:S(2)}, u32[]{:S(2)}) collective-permute-start(bf16[48,3584]{1,0:T(8,128)(2,1)S(1)} %chip_sum.4), channel_id=1, source_target_pairs={{0,2},{1,3},{2,0},{3,1},{4,6},{5,7},{6,4},{7,5},{8,10},{9,11},{10,... | collective-permute-start | bytes 1032200 | tf_op jit(solution)/shard_map/ppermute | solution.py:56
  115.0 12.9 %collective-permute-start.28 = (bf16[48,1792]{1,0:T(8,128)(2,1)S(1)}, bf16[48,1792]{1,0:T(8,128)(2,1)S(1)}, u32[]{:S(2)}, u32[]{:S(2)}) collective-permute-start(bf16[48,1792]{1,0:T(8,128)(2,1)S(1)} %get-tuple-element.94), channel_id=1, source_target_pairs={{10,32},{26,33},{8,34},{24,35},{14,36},{30,37},{12,38},{28,39},{2,... | collective-permute-start | bytes 516104 | tf_op jit(solution)/shard_map/ppermute | solution.py:66
  125.9 13.3 %collective-permute-start.37 = (bf16[48,3584]{1,0:T(8,128)(2,1)S(1)}, bf16[48,3584]{1,0:T(8,128)(2,1)S(1)}, u32[]{:S(2)}, u32[]{:S(2)}) collective-permute-start(bf16[48,3584]{1,0:T(8,128)(2,1)S(1)} %chip_sum.5), channel_id=1, source_target_pairs={{0,2},{1,3},{2,0},{3,1},{4,6},{5,7},{6,4},{7,5},{8,10},{9,11},{10,... | collective-permute-start | bytes 1032200 | tf_op jit(solution)/shard_map/ppermute | solution.py:56
  128.0 14.2 %collective-permute-start.30 = (bf16[48,1792]{1,0:T(8,128)(2,1)S(1)}, bf16[48,1792]{1,0:T(8,128)(2,1)S(1)}, u32[]{:S(2)}, u32[]{:S(2)}) collective-permute-start(bf16[48,1792]{1,0:T(8,128)(2,1)S(1)} %get-tuple-element.98), channel_id=1, source_target_pairs={{4,32},{20,33},{14,34},{30,35},{8,36},{24,37},{2,38},{18,39},{12,4... | collective-permute-start | bytes 516104 | tf_op jit(solution)/shard_map/ppermute | solution.py:66
  128.2 18.1 %collective-permute-start.31 = (bf16[48,1792]{1,0:T(8,128)(2,1)S(1)}, bf16[48,1792]{1,0:T(8,128)(2,1)S(1)}, u32[]{:S(2)}, u32[]{:S(2)}) collective-permute-start(bf16[48,1792]{1,0:T(8,128)(2,1)S(1)} %get-tuple-element.99), channel_id=1, source_target_pairs={{14,32},{30,33},{4,34},{20,35},{2,36},{18,37},{8,38},{24,39},{6,40... | collective-permute-start | bytes 516104 | tf_op jit(solution)/shard_map/ppermute | solution.py:66
  137.5 13.5 %collective-permute-start.35 = (bf16[48,1792]{1,0:T(8,128)(2,1)S(1)}, bf16[48,1792]{1,0:T(8,128)(2,1)S(1)}, u32[]{:S(2)}, u32[]{:S(2)}) collective-permute-start(bf16[48,1792]{1,0:T(8,128)(2,1)S(1)} %get-tuple-element.105), channel_id=1, source_target_pairs={{10,224},{26,225},{8,226},{24,227},{14,228},{30,229},{12,230},{28,... | collective-permute-start | bytes 516104 | tf_op jit(solution)/shard_map/ppermute | solution.py:66
  137.6 14.7 %collective-permute-start.36 = (bf16[48,1792]{1,0:T(8,128)(2,1)S(1)}, bf16[48,1792]{1,0:T(8,128)(2,1)S(1)}, u32[]{:S(2)}, u32[]{:S(2)}) collective-permute-start(bf16[48,1792]{1,0:T(8,128)(2,1)S(1)} %get-tuple-element.106), channel_id=1, source_target_pairs={{4,224},{20,225},{14,226},{30,227},{8,228},{24,229},{2,230},{18,23... | collective-permute-start | bytes 516104 | tf_op jit(solution)/shard_map/ppermute | solution.py:66
  139.1 10.6 %collective-permute-start.32 = (bf16[48,1792]{1,0:T(8,128)(2,1)S(1)}, bf16[48,1792]{1,0:T(8,128)(2,1)S(1)}, u32[]{:S(2)}, u32[]{:S(2)}) collective-permute-start(bf16[48,1792]{1,0:T(8,128)(2,1)S(1)} %get-tuple-element.100), channel_id=1, source_target_pairs={{0,32},{16,33},{2,34},{18,35},{4,36},{20,37},{6,38},{22,39},{8,40}... | collective-permute-start | bytes 516104 | tf_op jit(solution)/shard_map/ppermute | solution.py:66
  142.2 12.2 %collective-permute-start.38 = (bf16[48,1792]{1,0:T(8,128)(2,1)S(1)}, bf16[48,1792]{1,0:T(8,128)(2,1)S(1)}, u32[]{:S(2)}, u32[]{:S(2)}) collective-permute-start(bf16[48,1792]{1,0:T(8,128)(2,1)S(1)} %get-tuple-element.108), channel_id=1, source_target_pairs={{14,224},{30,225},{4,226},{20,227},{2,228},{18,229},{8,230},{24,23... | collective-permute-start | bytes 516104 | tf_op jit(solution)/shard_map/ppermute | solution.py:66
  146.3 12.1 %collective-permute-start.39 = (bf16[48,1792]{1,0:T(8,128)(2,1)S(1)}, bf16[48,1792]{1,0:T(8,128)(2,1)S(1)}, u32[]{:S(2)}, u32[]{:S(2)}) collective-permute-start(bf16[48,1792]{1,0:T(8,128)(2,1)S(1)} %get-tuple-element.109), channel_id=1, source_target_pairs={{0,224},{16,225},{2,226},{18,227},{4,228},{20,229},{6,230},{22,231... | collective-permute-start | bytes 516104 | tf_op jit(solution)/shard_map/ppermute | solution.py:66
  150.2 12.0 %collective-permute-start.33 = (bf16[64,3584]{1,0:T(8,128)(2,1)S(1)}, bf16[64,3584]{1,0:T(8,128)(2,1)S(1)}, u32[]{:S(2)}, u32[]{:S(2)}) collective-permute-start(bf16[64,3584]{1,0:T(8,128)(2,1)S(1)} %get-tuple-element.102), channel_id=1, source_target_pairs={{0,1},{1,0},{2,3},{3,2},{4,5},{5,4},{6,7},{7,6},{8,9},{9,8},{10,11... | collective-permute-start | bytes 1376264 | tf_op jit(solution)/shard_map/ppermute | solution.py:51
  159.6 4.2 %collective-permute-start.40 = (bf16[64,3584]{1,0:T(8,128)(2,1)}, bf16[64,3584]{1,0:T(8,128)(2,1)S(1)}, u32[]{:S(2)}, u32[]{:S(2)}) collective-permute-start(bf16[64,3584]{1,0:T(8,128)(2,1)} %get-tuple-element.111), channel_id=1, source_target_pairs={{0,1},{1,0},{2,3},{3,2},{4,5},{5,4},{6,7},{7,6},{8,9},{9,8},{10,11... | collective-permute-start | bytes 1376264 | tf_op jit(solution)/shard_map/ppermute | solution.py:51
  (21 other events, 160.9 us)
